TPU v7x, 512 devices: a whole 4x8x8 slice. The times are simulated.
512 devices in a mesh: lat: 16 (over z_hi, x), lon: 32 (over y, z_lo, core).
Axes of the slice: x: 4, y: 8, z: 8 (z_hi: 4, z_lo: 2; z = z_hi * 2 + z_lo), core: 2. Of those that a mesh axis runs over, the one named last changes fastest.
Arguments:
- tokens: bfloat16 [2, 96, 768, 192], P(None, 'lat', 'lon'), may hold values from -30 to 30
- cotangent: bfloat16 [2, 96, 768, 192], P(None, 'lat', 'lon'), may hold values from -6 to 6
- norm_gain_vector: float32 [192], replicated, may hold values from 0.1 to 1.9
- norm_bias_vector: float32 [192], replicated, may hold values from -3 to 3
- qkv_weight: bfloat16 [192, 576], replicated, may hold values from -0.4375 to 0.4375
- qkv_bias: float32 [576], replicated, may hold values from -3 to 3
- proj_weight: bfloat16 [192, 192], replicated, may hold values from -0.4375 to 0.4375
- proj_bias: float32 [192], replicated, may hold values from -3 to 3
- earth_bias: float32 [1, 16, 6, 3312], P(None, 'lat'), may hold values from -2.5 to 300, as said below
- lat_valid: int32 [96], replicated, may hold values from 0 to 1, as said below
Outputs:
- block_out: float32 [2, 96, 768, 192], P(None, 'lat', 'lon')
- token_grad: float32 [2, 96, 768, 192], P(None, 'lat', 'lon')
- norm_gain_grad: float32 [192], replicated
- norm_shift_grad: float32 [192], replicated
- qkv_weight_grad: float32 [192, 576], replicated
- qkv_bias_grad: float32 [576], replicated
- proj_weight_grad: float32 [192, 192], replicated
- proj_bias_grad: float32 [192], replicated
- earth_bias_grad: float32 [1, 16, 6, 3312], P(None, 'lat')
Inputs may be any that keep to these rules, and one draw needn't show every extreme that they name: `earth_bias`: bias tables of window types. `lat_valid`: 1 on every latitude row except the last 1 to 5 rows of the grid, which are 0.
All inputs are finite; a program needn't handle non-finite values.
Results may differ from a plain program's by a relative error of at most 0.0094.
Values may be sent and summed in bfloat16 or wider, within the bound.
No kernel may reach another device: no remote copies, remote signals or barrier semaphores. Data moves between devices by JAX's collectives and lax.ppermute only.
A program may use at most 128 MiB of HBM per device.

v0:
```python
import math

import jax
import jax.numpy as jnp
from jax import lax
from jax.sharding import PartitionSpec as P

HEADS = 6
WZ = 2
WLAT = 6
WLON = 12


mask_fill = -10000.0
epsilon = 1e-05
bias_factor = 8.0


def shifted(array, axis, by):
    count = lax.axis_size(axis)
    return lax.ppermute(array, axis, [(i, (i + by) % count) for i in range(count)])


def toeplitz():
    diffs = 2 * WLON - 1
    place = jnp.arange(WLON * WLON, dtype=jnp.int32)
    offset = place // WLON - place % WLON + WLON - 1
    return (jnp.arange(diffs, dtype=jnp.int32)[:, None] == offset[None, :]).astype(jnp.float32)


def to_windows(tile):
    levels, rows, cols, width = tile.shape
    grid = tile.reshape(levels // WZ, WZ, rows // WLAT, WLAT, cols // WLON, WLON, width)
    grid = grid.transpose(0, 2, 4, 1, 3, 5, 6)
    return grid.reshape(levels // WZ * (rows // WLAT), cols // WLON, WZ * WLAT * WLON, width)


def from_windows(blocks, levels, rows, cols):
    width = blocks.shape[-1]
    grid = blocks.reshape(levels // WZ, rows // WLAT, cols // WLON, WZ, WLAT, WLON, width)
    return grid.transpose(0, 3, 1, 4, 2, 5, 6).reshape(levels, rows, cols, width)


def into_shifted(stacked):
    kinds, levels, rows, cols, width = stacked.shape
    half_lat = WLAT // 2
    half_lon = WLON // 2
    stacked = jnp.roll(stacked, -(WZ // 2), axis=1)
    upper = stacked[:, :, :half_lat].reshape(kinds, levels, half_lat, cols * width)
    below = shifted(upper, "lat", -1).reshape(kinds, levels, half_lat, cols, width)
    stacked = jnp.concatenate([stacked[:, :, half_lat:], below], axis=2)
    left = stacked[:, :, :, :half_lon].reshape(kinds, levels, rows, half_lon * width)
    right = shifted(left, "lon", -1).reshape(kinds, levels, rows, half_lon, width)
    return jnp.concatenate([stacked[:, :, :, half_lon:], right], axis=3)


def to_owners(stacked):
    kinds, levels, rows, cols, width = stacked.shape
    half_lat = WLAT // 2
    half_lon = WLON // 2
    tail = stacked[:, :, :, cols - half_lon :].reshape(kinds, levels, rows, half_lon * width)
    front = shifted(tail, "lon", 1).reshape(kinds, levels, rows, half_lon, width)
    stacked = jnp.concatenate([front, stacked[:, :, :, : cols - half_lon]], axis=3)
    bottom = stacked[:, :, rows - half_lat :].reshape(kinds, levels, half_lat, cols * width)
    top = shifted(bottom, "lat", 1).reshape(kinds, levels, half_lat, cols, width)
    stacked = jnp.concatenate([top, stacked[:, :, : rows - half_lat]], axis=2)
    return jnp.roll(stacked, WZ // 2, axis=1)


def window_bias(table_bands, lat_valid, first_band, levels):
    zones, bands, heads, pairs = table_bands.shape
    total_rows = lat_valid.shape[0]
    band_count = total_rows // WLAT
    count = WZ * WLAT * WLON
    table = table_bands.reshape(zones, bands, heads, WZ * WZ * WLAT * WLAT, 2 * WLON - 1)
    spread = jnp.einsum("abhpd,dq->abhpq", table, toeplitz(), precision=lax.Precision.HIGHEST)
    spread = spread.reshape(zones, bands, heads, WZ, WZ, WLAT, WLAT, WLON, WLON)
    spread = spread.transpose(0, 1, 2, 3, 5, 7, 4, 6, 8).reshape(zones, bands, heads, count, count)
    position = jnp.arange(count, dtype=jnp.int32)
    level_in = position // (WLAT * WLON)
    row_in = position // WLON % WLAT
    level = jnp.arange(zones, dtype=jnp.int32)[:, None] * WZ + level_in[None, :]
    level_region = (level >= levels - WZ).astype(jnp.int32) + (level >= levels - WZ // 2).astype(
        jnp.int32
    )
    band_at = (first_band + jnp.arange(bands, dtype=jnp.int32)) % band_count
    row = band_at[:, None] * WLAT + row_in[None, :]
    row_region = (row >= total_rows - WLAT).astype(jnp.int32) + (
        row >= total_rows - WLAT // 2
    ).astype(jnp.int32)
    rolled = jnp.roll(lat_valid, -(WLAT // 2))
    doubled = jnp.concatenate([rolled, rolled])
    tile_valid = lax.dynamic_slice_in_dim(doubled, band_at[0] * WLAT, bands * WLAT)
    key_ok = jnp.broadcast_to(
        tile_valid.reshape(bands, 1, WLAT, 1), (bands, WZ, WLAT, WLON)
    ).reshape(bands, count)
    same_level = level_region[:, None, :, None] == level_region[:, None, None, :]
    same_row = row_region[None, :, :, None] == row_region[None, :, None, :]
    allowed = same_level & same_row & (key_ok[None, :, None, :] == 1)
    masked = jnp.where(allowed, jnp.float32(0.0), jnp.float32(mask_fill))
    return (spread + masked[:, :, None]).reshape(zones * bands, heads, count, count)


def bias_table_grad(bias_part, zones, bands):
    heads = bias_part.shape[1]
    grid = bias_part.reshape(zones, bands, heads, WZ, WLAT, WLON, WZ, WLAT, WLON)
    grid = grid.transpose(0, 1, 2, 3, 6, 4, 7, 5, 8).reshape(
        zones, bands, heads, WZ * WZ * WLAT * WLAT, WLON * WLON
    )
    table = jnp.einsum("abhpq,dq->abhpd", grid, toeplitz(), precision=lax.Precision.HIGHEST)
    return table.reshape(zones, bands, heads, -1) * bias_factor


def forward(xw, add, params):
    norm_gain_vector, norm_bias_vector, qkv_weight, qkv_bias, proj_weight, proj_bias = params
    f32 = jnp.float32
    groups, across, count, width = xw.shape
    head_dim = width // HEADS
    scale = 1.0 / math.sqrt(head_dim)
    xf = xw.astype(f32)
    mean_value = jnp.mean(xf, axis=-1, keepdims=True)
    centered_input = xf - mean_value
    inverse_deviation = lax.rsqrt(
        jnp.mean(centered_input * centered_input, axis=-1, keepdims=True) + epsilon
    )
    standardized_input = centered_input * inverse_deviation
    normalized_input = (standardized_input * norm_gain_vector + norm_bias_vector).astype(
        jnp.bfloat16
    )
    qkv = (
        jnp.einsum("aonc,cd->aond", normalized_input, qkv_weight, preferred_element_type=f32)
        + qkv_bias
    )
    split = qkv.astype(jnp.bfloat16).reshape(groups, across, count, 3, HEADS, head_dim)
    query_rows = split[:, :, :, 0]
    key_rows = split[:, :, :, 1]
    value_rows = split[:, :, :, 2]
    scores = (
        jnp.einsum("aonhd,aomhd->aohnm", query_rows, key_rows, preferred_element_type=f32) * scale
        + add[:, None]
    )
    probabilities_wide = jax.nn.softmax(scores, axis=-1)
    attention_probabilities = probabilities_wide.astype(jnp.bfloat16)
    attention_rows = jnp.einsum(
        "aohnm,aomhd->aonhd", attention_probabilities, value_rows, preferred_element_type=f32
    )
    attention_rows = attention_rows.reshape(groups, across, count, width).astype(jnp.bfloat16)
    output_rows = (
        xf
        + jnp.einsum("aonc,ce->aone", attention_rows, proj_weight, preferred_element_type=f32)
        + proj_bias
    )
    return (
        output_rows,
        (
            standardized_input,
            inverse_deviation,
            normalized_input,
            query_rows,
            key_rows,
            value_rows,
            probabilities_wide,
            attention_probabilities,
            attention_rows,
        ),
    )


def backward(saved_residuals, dyw, params, counted):
    norm_gain_vector, norm_bias_vector, qkv_weight, qkv_bias, proj_weight, proj_bias = params
    (
        standardized_input,
        inverse_deviation,
        normalized_input,
        query_rows,
        key_rows,
        value_rows,
        probabilities_wide,
        attention_probabilities,
        attention_rows,
    ) = saved_residuals
    f32 = jnp.float32
    groups, across, count, width = dyw.shape
    head_dim = width // HEADS
    scale = 1.0 / math.sqrt(head_dim)
    keep = counted[:, :, None, None]
    kept_dy = jnp.where(keep, dyw, jnp.zeros_like(dyw))
    proj_bias_grad = jnp.sum(kept_dy, axis=(0, 1, 2), dtype=f32)
    proj_weight_grad = jnp.einsum(
        "aonc,aone->ce", attention_rows, kept_dy, preferred_element_type=f32
    )
    d_attn = jnp.einsum("aone,ce->aonc", dyw, proj_weight, preferred_element_type=f32).astype(
        jnp.bfloat16
    )
    d_attn = d_attn.reshape(groups, across, count, HEADS, head_dim)
    d_values = jnp.einsum(
        "aohnm,aonhd->aomhd", attention_probabilities, d_attn, preferred_element_type=f32
    )
    d_probs = jnp.einsum("aonhd,aomhd->aohnm", d_attn, value_rows, preferred_element_type=f32)
    d_scores = probabilities_wide * (
        d_probs - jnp.sum(probabilities_wide * d_probs, axis=-1, keepdims=True)
    )
    bias_part = jnp.sum(
        jnp.where(counted[:, :, None, None, None], d_scores, jnp.float32(0.0)), axis=1
    )
    d_scores_b = d_scores.astype(jnp.bfloat16)
    d_query = (
        jnp.einsum("aohnm,aomhd->aonhd", d_scores_b, key_rows, preferred_element_type=f32) * scale
    )
    d_keys = (
        jnp.einsum("aohnm,aonhd->aomhd", d_scores_b, query_rows, preferred_element_type=f32) * scale
    )
    d_qkv = (
        jnp.stack([d_query, d_keys, d_values], axis=3)
        .reshape(groups, across, count, 3 * width)
        .astype(jnp.bfloat16)
    )
    kept_qkv = jnp.where(keep, d_qkv, jnp.zeros_like(d_qkv))
    qkv_bias_grad = jnp.sum(kept_qkv, axis=(0, 1, 2), dtype=f32)
    qkv_weight_grad = jnp.einsum(
        "aonc,aond->cd", normalized_input, kept_qkv, preferred_element_type=f32
    )
    normalized_gradient = jnp.einsum("aond,cd->aonc", d_qkv, qkv_weight, preferred_element_type=f32)
    retained_normalized = jnp.where(keep, normalized_gradient, jnp.float32(0.0))
    gain_gradient = jnp.sum(retained_normalized * standardized_input, axis=(0, 1, 2))
    shift_grad = jnp.sum(retained_normalized, axis=(0, 1, 2))
    standardized_gradient = normalized_gradient * norm_gain_vector
    input_gradient = inverse_deviation * (
        standardized_gradient
        - jnp.mean(standardized_gradient, axis=-1, keepdims=True)
        - standardized_input
        * jnp.mean(standardized_gradient * standardized_input, axis=-1, keepdims=True)
    )
    grad = dyw.astype(f32) + input_gradient
    return (
        grad,
        bias_part,
        (
            gain_gradient,
            shift_grad,
            qkv_weight_grad,
            qkv_bias_grad,
            proj_weight_grad,
            proj_bias_grad,
        ),
    )


def local(
    tokens,
    cotangent,
    norm_gain_vector,
    norm_bias_vector,
    qkv_weight,
    qkv_bias,
    proj_weight,
    proj_bias,
    earth_bias,
    lat_valid,
):
    levels, rows, cols, width = tokens.shape
    lat_count = lax.axis_size("lat")
    lon_count = lax.axis_size("lon")
    lat_at = lax.axis_index("lat")
    zones = levels // WZ
    bands = rows // WLAT
    params = (norm_gain_vector, norm_bias_vector, qkv_weight, qkv_bias, proj_weight, proj_bias)
    add = window_bias(earth_bias, lat_valid, lat_at * bands, levels)
    counted = jnp.ones((zones * bands, cols // WLON), bool)
    moved = into_shifted(jnp.stack([tokens, cotangent]))
    out_w, saved_residuals = forward(to_windows(moved[0]), add, params)
    grad_w, bias_part, grads = backward(saved_residuals, to_windows(moved[1]), params, counted)
    results = jnp.stack(
        [from_windows(out_w, levels, rows, cols), from_windows(grad_w, levels, rows, cols)]
    )
    back = to_owners(results)
    block_out = back[0]
    token_grad = back[1]
    table_part = bias_table_grad(bias_part, zones, bands)
    gain_gradient, shift_grad, qkv_weight_grad, qkv_bias_grad, proj_weight_grad, proj_bias_grad = (
        grads
    )
    earth_bias_grad = lax.psum(table_part, "lon")
    summed = lax.psum(
        (
            gain_gradient,
            shift_grad,
            qkv_weight_grad,
            qkv_bias_grad,
            proj_weight_grad,
            proj_bias_grad,
        ),
        ("lat", "lon"),
    )
    norm_by = 1.0 / math.sqrt(levels * rows * cols * lat_count * lon_count)
    return (
        block_out,
        token_grad,
        summed[0] * norm_by,
        summed[1] * norm_by,
        summed[2] * norm_by,
        summed[3] * norm_by,
        summed[4] * norm_by,
        summed[5] * norm_by,
        earth_bias_grad,
    )


def solution(mesh):
    placed = (
        P(None, "lat", "lon", None),
        P(None, "lat", "lon", None),
        P(),
        P(),
        P(),
        P(),
        P(),
        P(),
        P(None, "lat", None, None),
        P(),
    )
    return jax.shard_map(
        local,
        mesh=mesh,
        in_specs=placed,
        out_specs=(
            P(None, "lat", "lon", None),
            P(None, "lat", "lon", None),
            P(),
            P(),
            P(),
            P(),
            P(),
            P(),
            P(None, "lat", None, None),
        ),
        check_vma=False,
    )
```

profile of v0, /device:TPU:1, one launch (start us, length us, event | category | flops | bytes accessed | tf_op | source)
XLA Modules:
  0.0 667.7 jit_solution(16145273018762778755)
XLA Ops:
  7.2 1.0 copy_bitcast_fusion
  8.6 13.7 %collective-permute-start = (bf16[2,2,3,4608]{3,1,2,0:T(2,128)(2,1)S(1)}, bf16[2,2,3,4608]{3,1,2,0:T(2,128)(2,1)S(1)}, u32[]{:S(2)}, u32[]{:S(2)}) collective-permute-start(bf16[2,2,3,4608]{3,1,2,0:T(2,128)(2,1)S(1)} %reshape.649), channel_id=1, source_target_pairs={{0,480},{32,0},{64,32},{96,64},{128,96},{160,128},{192,160},{224,1... | collective-permute-start | bytes 331784 | tf_op jit(solution)/shard_map/ppermute | solution.py:21
  23.0 3.0 convolution_bitcast_fusion
  26.0 3.9 copy.132
  29.9 4.9 reshape.658
  35.5 1.4 copy.133
  37.2 3.0 collective-permute-start.1
  40.3 2.6 collective-permute-done.1
  46.0 1.9 fusion.43
  48.4 0.8 copy-done.1
  49.7 2.1 fusion.8
  52.4 0.8 copy-done.2
  54.0 0.6 multiply_reduce_fusion.1
  54.6 1.3 convolution_bitcast_fusion.1
  57.6 1.9 collective-permute-start.2
  59.6 98.2 %all-reduce = (f32[192]{0:T(256)S(1)}, f32[192]{0:T(256)S(1)}, f32[576]{0:T(1024)S(1)}, f32[192]{0:T(256)S(1)}) all-reduce(f32[192]{0:T(256)S(1)} %get-tuple-element.36, f32[192]{0:T(256)S(1)} %get-tuple-element.39, f32[576]{0:T(1024)S(1)} %reduce_sum.110, ...), channel_id=1, replica_groups=mesh['lat'=16,'lon'=32] {'lat','lon'}, use_global_device_ids=true, to_apply=%region_8.9 | all-reduce | flops 1152 | bytes 9216 | tf_op jit(solution)/shard_map/psum | solution.py:284
  157.8 0.6 broadcast_multiply_fusion.8
  158.9 0.6 broadcast_multiply_fusion.3
  160.6 5.0 reshape.667
  165.5 7.7 %copy.159 = f32[1,1,6,2,2,6,6,12,12]{8,7,6,5,4,3,2,1,0:T(8,128)} copy(f32[1,1,6,2,2,6,6,12,12]{8,6,4,7,5,3,2,1,0:T(8,128)} %bitcast.148) | data formatting | bytes 995328 | tf_op jit(solution)/shard_map/transpose | solution.py:107
  173.2 4.9 reshape.668
  178.9 0.9 mul.177
  179.9 0.9 convolution_bitcast_fusion.3
  180.8 196.3 %all-reduce.5.cloned.1.call-done = f32[1,1,6,3312]{3,2,1,0:T(8,128)} async-done(((f32[1,1,6,3312]{3,2,1,0:T(8,128)}), f32[1,1,6,3312]{3,2,1,0:T(8,128)}) %all-reduce.5.cloned.1.call-update) | async-done | bytes 79504 | tf_op jit(solution)/shard_map/psum | solution.py:283
  377.1 1.6 copy.163
  379.7 2.1 collective-permute-start.3
  381.8 272.5 %all-reduce.7.cloned.1.call-done = (f32[192,576]{1,0:T(8,128)}, f32[192,192]{1,0:T(8,128)}) async-done(((f32[192,576]{1,0:T(8,128)}, f32[192,192]{1,0:T(8,128)}), (f32[192,576]{1,0:T(8,128)}, f32[192,192]{1,0:T(8,128)})) %all-reduce.7.cloned.1.call-update) | async-done | bytes 589840 | tf_op jit(solution)/shard_map/psum | solution.py:284
  654.4 1.9 broadcast_multiply_fusion
  656.2 1.6 broadcast_multiply_fusion.1
  658.6 0.6 fusion.10
  659.4 0.7 copy.161
  660.2 0.7 copy.162
  (103 shorter events, 13.2 us)
Async XLA Ops:
  7.2 38.2 %copy-start = (bf16[192,576]{1,0:T(8,128)(2,1)S(1)}, bf16[192,576]{1,0:T(8,128)(2,1)}, u32[]{:S(2)}) copy-start(bf16[192,576]{1,0:T(8,128)(2,1)} %param.14) | copy-start | bytes 663556
  7.2 15.1 %copy-start.5 = (f32[1,1,6,3312]{3,1,2,0:T(1,128)S(1)}, f32[1,1,6,3312]{3,1,2,0:T(1,128)}, u32[]{:S(2)}) copy-start(f32[1,1,6,3312]{3,1,2,0:T(1,128)} %param.18) | copy-start | bytes 238468
  7.2 369.9 %all-reduce.5.cloned.1.call-start = ((), (), s32[]{:S(2)}) async-start(), calls=%async_computation | async-start | bytes 212992 | tf_op jit(solution)/shard_map/psum | solution.py:283
  8.6 28.2 %collective-permute-start = (bf16[2,2,3,4608]{3,1,2,0:T(2,128)(2,1)S(1)}, bf16[2,2,3,4608]{3,1,2,0:T(2,128)(2,1)S(1)}, u32[]{:S(2)}, u32[]{:S(2)}) collective-permute-start(bf16[2,2,3,4608]{3,1,2,0:T(2,128)(2,1)S(1)} %reshape.649), channel_id=1, source_target_pairs={{0,480},{32,0},{64,32},{96,64},{128,96},{160,128},{192,160},{224,1... | collective-permute-start | bytes 331784 | tf_op jit(solution)/shard_map/ppermute | solution.py:21
  29.9 5.0 copy-start.7
  37.2 5.8 collective-permute-start.1
  43.2 1.9 copy-start.3
  43.3 2.1 copy-start.6
  43.3 2.1 copy-start.8
  43.4 2.1 copy-start.11
  48.0 1.2 copy-start.1
  51.7 1.5 copy-start.2
  53.7 0.9 copy-start.9
  54.6 2.0 copy-start.4
  54.6 2.0 copy-start.10
  57.6 321.1 %collective-permute-start.2 = (f32[2,2,6,1152]{3,1,2,0:T(2,128)S(1)}, f32[2,2,6,1152]{3,1,2,0:T(2,128)S(1)}, u32[]{:S(2)}, u32[]{:S(2)}) collective-permute-start(f32[2,2,6,1152]{3,1,2,0:T(2,128)S(1)} %reshape.663), channel_id=1, source_target_pairs={{0,1},{1,2},{2,3},{3,4},{4,5},{5,6},{6,7},{7,8},{8,9},{9,10},{10,1... | collective-permute-start | bytes 331784 | tf_op jit(solution)/shard_map/ppermute | solution.py:21
  179.8 474.5 %all-reduce.7.cloned.1.call-start = ((), (), s32[]{:S(2)}) async-start(), calls=%async_computation.1 | async-start | bytes 1376256 | tf_op jit(solution)/shard_map/psum | solution.py:284
  379.7 278.1 %collective-permute-start.3 = (f32[2,2,3,4608]{3,1,2,0:T(2,128)S(1)}, f32[2,2,3,4608]{3,1,2,0:T(2,128)S(1)}, u32[]{:S(2)}, u32[]{:S(2)}) collective-permute-start(f32[2,2,3,4608]{3,1,2,0:T(2,128)S(1)} %reshape.665), channel_id=1, source_target_pairs={{0,32},{32,64},{64,96},{96,128},{128,160},{160,192},{192,224},{224... | collective-permute-start | bytes 663560 | tf_op jit(solution)/shard_map/ppermute | solution.py:21
Sparse Core Ops, SparseCore 0:
  179.9 197.0 all-reduce.4
  383.6 270.6 all-reduce.6
where the time goes:
time: 668 us
  waiting for transfers between devices  471 us (71%)
  blocking collectives  98.2 us (15%)
  local copies, waits for them, and re-layouts  40.2 us (6%)
  starting transfers between devices  20.8 us (3%)
  between operations  14.7 us (2%)
  other arithmetic  11.4 us (2%)
  matrix products  10.9 us (2%)
    psum x1, waiting for transfers between devices, local(): lax.psum((gain_gradient, shift_grad, qkv_weight_grad, qkv_bias_grad, proj...  273 us
    psum x1, waiting for transfers between devices, local(): earth_bias_grad = lax.psum(table_part, 'lon')  196 us
    psum x1, blocking collectives, local(): lax.psum((gain_gradient, shift_grad, qkv_weight_grad, qkv_bias_grad, proj...  98.2 us
    ppermute x4, starting transfers between devices, shifted(): lax.ppermute(array, axis, [(i, (i + by) % count) for i in range(count)])  20.7 us
  transfers between devices with their start and end apart: 6, of which 3 were waited for; matrix products, arithmetic and copies ran while one was open for 7% of the time, Pallas kernels for 0%

commit v1 on v0

--- a/solution.py
+++ b/solution.py
@@ -244,6 +244,45 @@
             proj_bias_grad,
         ),
     )
+
+
+def spread_to_all(piece, axis):
+    count = lax.axis_size(axis)
+    return lax.all_to_all(jnp.broadcast_to(piece[None], (count,) + piece.shape), axis, 0, 0)
+
+
+def reduce_all(qkv_weight_grad, proj_weight_grad, vectors, table):
+    f32 = jnp.float32
+    lon_count = lax.axis_size("lon")
+    width, wide = qkv_weight_grad.shape
+    across = wide + width
+    vector = jnp.concatenate(vectors)
+    vector_rows = vector.shape[0] // 128
+    entries = across - 128
+    matrix = jnp.concatenate([qkv_weight_grad, proj_weight_grad], axis=1)
+    matrix = matrix.reshape(lon_count, width // lon_count, across)
+    flat = table.reshape(-1)
+    flat = jnp.pad(flat, (0, lon_count * entries - flat.shape[0])).reshape(lon_count, 1, entries)
+    vector = jnp.pad(vector.reshape(vector_rows, 1, 128), ((0, lon_count - vector_rows), (0, 0), (0, 0)))
+    last = jnp.concatenate([flat, vector], axis=2)
+    parts = jnp.concatenate([matrix, last, jnp.zeros_like(last)], axis=1).astype(jnp.bfloat16)
+    by_lon = jnp.sum(lax.all_to_all(parts, "lon", 0, 0).astype(f32), axis=0)
+    by_lat = jnp.sum(spread_to_all(by_lon.astype(jnp.bfloat16), "lat").astype(f32), axis=0)
+    row = lax.broadcasted_iota(jnp.int32, by_lat.shape, 0)
+    column = lax.broadcasted_iota(jnp.int32, by_lat.shape, 1)
+    is_table = (row == width // lon_count) & (column < entries)
+    done = jnp.where(is_table, by_lon, by_lat).astype(jnp.bfloat16)
+    full = spread_to_all(done, "lon").astype(f32)
+    rows = width // lon_count
+    matrix = full[:, :rows].reshape(width, across)
+    flat = full[:, rows, :entries].reshape(-1)[: table.size].reshape(table.shape)
+    vector = full[:vector_rows, rows, entries:].reshape(-1)
+    pieces = []
+    start = 0
+    for v in vectors:
+        pieces.append(vector[start : start + v.shape[0]])
+        start += v.shape[0]
+    return (matrix[:, :wide], matrix[:, wide:], tuple(pieces)), flat
 
 
 def local(
@@ -280,19 +319,22 @@
     gain_gradient, shift_grad, qkv_weight_grad, qkv_bias_grad, proj_weight_grad, proj_bias_grad = (
         grads
     )
-    earth_bias_grad = lax.psum(table_part, "lon")
-    summed = lax.psum(
-        (
-            gain_gradient,
-            shift_grad,
-            qkv_weight_grad,
-            qkv_bias_grad,
-            proj_weight_grad,
-            proj_bias_grad,
-        ),
-        ("lat", "lon"),
-    )
     norm_by = 1.0 / math.sqrt(levels * rows * cols * lat_count * lon_count)
+    summed, earth_bias_grad = reduce_all(
+        qkv_weight_grad,
+        proj_weight_grad,
+        (gain_gradient, shift_grad, qkv_bias_grad, proj_bias_grad),
+        table_part,
+    )
+    qkv_weight_grad, proj_weight_grad, (gain_gradient, shift_grad, qkv_bias_grad, proj_bias_grad) = summed
+    summed = (
+        gain_gradient,
+        shift_grad,
+        qkv_weight_grad,
+        qkv_bias_grad,
+        proj_weight_grad,
+        proj_bias_grad,
+    )
     return (
         block_out,
         token_grad,

time: 668 us -> 142 us (0.21)
  waiting for transfers between devices: 471 us -> 38.5 us
  blocking collectives: 98.2 us -> 0 us
  starting transfers between devices: 20.8 us -> 42.6 us
  between operations: 14.7 us -> 1.43 us
    psum x2 -> x0, waiting for transfers between devices: 469 us -> none  [the longest x1 273 us: local(): lax.psum((gain_gradient, shift_grad, qkv_weight_grad, qkv_bias_grad, proj...]
    psum x1 -> x0, blocking collectives: 98.2 us -> none  [local(): lax.psum((gain_gradient, shift_grad, qkv_weight_grad, qkv_bias_grad, proj...]
    ppermute x4, waiting for transfers between devices: 2.63 us -> 24.1 us  [shifted(): lax.ppermute(array, axis, [(i, (i + by) % count) for i in range(count)])]
    all_to_all x0 -> x3, starting transfers between devices: none -> 19 us  [the longest x2 10.1 us: spread_to_all(): lax.all_to_all(jnp.broadcast_to(piece[None], (count,) + piece.shape), axi...]
    all_to_all x0 -> x3, waiting for transfers between devices: none -> 14.4 us  [the longest x1 13.5 us: reduce_all(): by_lon = jnp.sum(lax.all_to_all(parts, 'lon', 0, 0).astype(f32), axis=0)]
  transfers between devices with their start and end apart: 6 -> 7, of which waited for: 3 -> 5; matrix products, arithmetic and copies ran while one was open for 7% -> 14% of each run, Pallas kernels for 0% -> 0%
where the time goes in v1:
time: 142 us; the launch traced here: 141 us
  starting transfers between devices  42.6 us (30%)
  local copies, waits for them, and re-layouts  41.2 us (29%)
  waiting for transfers between devices  38.5 us (27%)
  matrix products  9.66 us (7%)
  other arithmetic  8.12 us (6%)
  between operations  1.43 us (1%)
    ppermute x4, waiting for transfers between devices, shifted(): lax.ppermute(array, axis, [(i, (i + by) % count) for i in range(count)])  24.1 us
    ppermute x4, starting transfers between devices, shifted(): lax.ppermute(array, axis, [(i, (i + by) % count) for i in range(count)])  23.7 us
    all_to_all x1, waiting for transfers between devices, reduce_all(): by_lon = jnp.sum(lax.all_to_all(parts, 'lon', 0, 0).astype(f32), axis=0)  13.5 us
    all_to_all x2, starting transfers between devices, spread_to_all(): lax.all_to_all(jnp.broadcast_to(piece[None], (count,) + piece.shape), axi...  10.1 us
    all_to_all x1, starting transfers between devices, reduce_all(): by_lon = jnp.sum(lax.all_to_all(parts, 'lon', 0, 0).astype(f32), axis=0)  8.89 us
    transpose x1, local copies, waits for them, and re-layouts, bias_table_grad(): grid.transpose(0, 1, 2, 3, 6, 4, 7, 5, 8)  7.67 us
    another operation x3, local copies, waits for them, and re-layouts  5.47 us
    reshape x1, local copies, waits for them, and re-layouts, bias_table_grad(): bias_part.reshape(zones, bands, heads, WZ, WLAT, WLON, WZ, WLAT, WLON)  4.98 us
  transfers between devices with their start and end apart: 7, of which 5 were waited for; matrix products, arithmetic and copies ran while one was open for 14% of the time, Pallas kernels for 0%

profile of v1, /device:TPU:1, one launch (start us, length us, event | category | flops | bytes accessed | tf_op | source)
XLA Modules:
  0.0 141.4 jit_solution(11724561789076329548)
XLA Ops:
  0.7 1.0 copy_bitcast_fusion
  2.1 13.7 %collective-permute-start = (bf16[2,2,3,4608]{3,1,2,0:T(2,128)(2,1)S(1)}, bf16[2,2,3,4608]{3,1,2,0:T(2,128)(2,1)S(1)}, u32[]{:S(2)}, u32[]{:S(2)}) collective-permute-start(bf16[2,2,3,4608]{3,1,2,0:T(2,128)(2,1)S(1)} %reshape.694), channel_id=1, source_target_pairs={{0,480},{32,0},{64,32},{96,64},{128,96},{160,128},{192,160},{224,1... | collective-permute-start | bytes 331784 | tf_op jit(solution)/shard_map/ppermute | solution.py:21
  16.9 3.0 %convolution_bitcast_fusion = f32[1,1,6,2,6,12,2,6,12]{8,7,4,6,3,2,5,1,0:T(8,128)S(1)} fusion(f32[6,2,2,6,6,23,1]{5,4,3,2,1,0,6:T(8,128)S(1)} %reshape.724, pred[12,12,23,1,1,1,1]{2,1,0,3,4,5,6:T(8,128)(4,1)S(1)} %reshape.723), kind=kOutput, calls=%fused_computation.1 | convolution fusion | flops 34338816 | bytes 580464 | tf_op jit(solution)/shard_map/abhpd,dq->abhpq/dot_general | solution.py:76
  19.9 3.9 %copy.178 = f32[1,1,6,2,6,12,2,6,12]{8,7,6,5,4,3,2,1,0:T(8,128)} copy(f32[1,1,6,2,6,12,2,6,12]{8,7,4,6,3,2,5,1,0:T(8,128)S(1)} %convolution_bitcast_fusion) | data formatting | bytes 995328 | tf_op jit(solution)/shard_map/transpose | solution.py:78
  23.8 4.9 %reshape.703 = f32[6,144,144]{2,1,0:T(8,128)S(1)} reshape(f32[1,1,6,2,6,12,2,6,12]{8,7,6,5,4,3,2,1,0:T(8,128)} %copy.178) | data formatting | bytes 995328 | tf_op jit(solution)/shard_map/reshape | solution.py:78
  28.9 1.4 copy.179
  30.7 3.0 %collective-permute-start.1 = (bf16[2,2,6,1152]{3,1,2,0:T(2,128)(2,1)S(1)}, bf16[2,2,6,1152]{3,1,2,0:T(2,128)(2,1)S(1)}, u32[]{:S(2)}, u32[]{:S(2)}) collective-permute-start(bf16[2,2,6,1152]{3,1,2,0:T(2,128)(2,1)S(1)} %reshape.696), channel_id=1, source_target_pairs={{0,31},{1,0},{2,1},{3,2},{4,3},{5,4},{6,5},{7,6},{8,7},{9,8},{10,9... | collective-permute-start | bytes 165896 | tf_op jit(solution)/shard_map/ppermute | solution.py:21
  33.8 2.6 %collective-permute-done.1 = bf16[2,2,6,1152]{3,1,2,0:T(2,128)(2,1)S(1)} collective-permute-done((bf16[2,2,6,1152]{3,1,2,0:T(2,128)(2,1)S(1)}, bf16[2,2,6,1152]{3,1,2,0:T(2,128)(2,1)S(1)}, u32[]{:S(2)}, u32[]{:S(2)}) %collective-permute-start.1) | collective-permute-done | bytes 55328 | tf_op jit(solution)/shard_map/ppermute | solution.py:21
  38.4 0.8 copy.189
  40.3 2.2 %fusion.55 = (f32[2,6,144]{2,1,0:T(8,128)S(1)}, f32[2,6,144,144]{2,3,1,0:T(8,128)S(1)}) fusion(f32[6,144,144]{1,2,0:T(8,128)} %copy.179, bf16[1,2,144,3,6,32]{2,5,4,3,1,0:T(8,128)(2,1)S(1)} %bitcast.175), kind=kOutput, calls=%fused_computation.137 | convolution fusion | flops 16920720 | bytes 1893120 | tf_op jit(solution)/shard_map/sub | solution.py:142
  42.7 0.6 copy-done.7
  48.5 5.0 %reshape.713 = f32[1,1,6,2,6,12,2,6,12]{8,7,6,5,4,3,2,1,0:T(8,128)} reshape(f32[6,144,144]{2,1,0:T(8,128)S(1)} %copy.204) | data formatting | bytes 995328 | tf_op jit(solution)/shard_map/reshape | solution.py:106
  53.5 7.7 %copy.205 = f32[1,1,6,2,2,6,6,12,12]{8,7,6,5,4,3,2,1,0:T(8,128)} copy(f32[1,1,6,2,2,6,6,12,12]{8,6,4,7,5,3,2,1,0:T(8,128)} %bitcast.157) | data formatting | bytes 995328 | tf_op jit(solution)/shard_map/transpose | solution.py:107
  61.1 4.9 %reshape.714 = f32[6,144,144]{2,1,0:T(8,128)S(1)} reshape(f32[1,1,6,2,2,6,6,12,12]{8,7,6,5,4,3,2,1,0:T(8,128)} %copy.205) | data formatting | bytes 995328 | tf_op jit(solution)/shard_map/reshape.98
  67.3 1.0 fusion.23
  68.2 8.9 %all-to-all-start = ((bf16[32,8,768]{2,1,0:T(8,128)(2,1)}), bf16[32,8,768]{2,1,0:T(8,128)(2,1)S(1)}, u32[]{:S(2)}, u32[]{:S(2)}) async-start(bf16[32,8,768]{2,1,0:T(8,128)(2,1)} %fusion.23), calls=%async_computation | async-start | bytes 786432 | tf_op jit(solution)/shard_map/all_to_all | solution.py:269
  77.4 13.5 %all-to-all-done = bf16[32,8,768]{2,1,0:T(8,128)(2,1)S(1)} async-done(((bf16[32,8,768]{2,1,0:T(8,128)(2,1)}), bf16[32,8,768]{2,1,0:T(8,128)(2,1)S(1)}, u32[]{:S(2)}, u32[]{:S(2)}) %all-to-all-start) | async-done | bytes 393248 | tf_op jit(solution)/shard_map/all_to_all | solution.py:269
  91.0 0.7 broadcast_in_dim.37
  91.7 3.5 %all-to-all-start.1 = ((bf16[16,8,768]{2,1,0:T(8,128)(2,1)}), bf16[16,8,768]{2,1,0:T(8,128)(2,1)S(1)}, u32[]{:S(2)}, u32[]{:S(2)}) async-start(bf16[16,8,768]{2,1,0:T(8,128)(2,1)} %broadcast_in_dim.37), calls=%async_computation.1 | async-start | bytes 393216 | tf_op jit(solution)/shard_map/all_to_all | solution.py:251
  96.7 4.7 %collective-permute-start.2 = (f32[2,2,6,1152]{3,1,2,0:T(2,128)S(1)}, f32[2,2,6,1152]{3,1,2,0:T(2,128)S(1)}, u32[]{:S(2)}, u32[]{:S(2)}) collective-permute-start(f32[2,2,6,1152]{3,1,2,0:T(2,128)S(1)} %reshape.708), channel_id=1, source_target_pairs={{0,1},{1,2},{2,3},{3,4},{4,5},{5,6},{6,7},{7,8},{8,9},{9,10},{10,1... | collective-permute-start | bytes 331784 | tf_op jit(solution)/shard_map/ppermute | solution.py:21
  101.4 2.5 %collective-permute-done.2 = f32[2,2,6,1152]{3,1,2,0:T(2,128)S(1)} collective-permute-done((f32[2,2,6,1152]{3,1,2,0:T(2,128)S(1)}, f32[2,2,6,1152]{3,1,2,0:T(2,128)S(1)}, u32[]{:S(2)}, u32[]{:S(2)}) %collective-permute-start.2) | collective-permute-done | bytes 110624 | tf_op jit(solution)/shard_map/ppermute | solution.py:21
  104.4 0.9 all-to-all-done.1
  105.4 0.8 broadcast_in_dim.38
  106.1 6.5 %all-to-all-start.2 = ((bf16[32,8,768]{2,1,0:T(8,128)(2,1)}), bf16[32,8,768]{2,1,0:T(8,128)(2,1)S(1)}, u32[]{:S(2)}, u32[]{:S(2)}) async-start(bf16[32,8,768]{2,1,0:T(8,128)(2,1)} %broadcast_in_dim.38), calls=%async_computation.2 | async-start | bytes 786432 | tf_op jit(solution)/shard_map/all_to_all | solution.py:251
  113.2 2.3 %collective-permute-start.3 = (f32[2,2,3,4608]{3,1,2,0:T(2,128)S(1)}, f32[2,2,3,4608]{3,1,2,0:T(2,128)S(1)}, u32[]{:S(2)}, u32[]{:S(2)}) collective-permute-start(f32[2,2,3,4608]{3,1,2,0:T(2,128)S(1)} %reshape.710), channel_id=1, source_target_pairs={{0,32},{32,64},{64,96},{96,128},{128,160},{160,192},{192,224},{224... | collective-permute-start | bytes 663560 | tf_op jit(solution)/shard_map/ppermute | solution.py:21
  115.4 19.0 %collective-permute-done.3 = f32[2,2,3,4608]{3,1,2,0:T(2,128)S(1)} collective-permute-done((f32[2,2,3,4608]{3,1,2,0:T(2,128)S(1)}, f32[2,2,3,4608]{3,1,2,0:T(2,128)S(1)}, u32[]{:S(2)}, u32[]{:S(2)}) %collective-permute-start.3) | collective-permute-done | bytes 221216 | tf_op jit(solution)/shard_map/ppermute | solution.py:21
  136.0 0.7 copy.210
  136.8 0.7 copy.209
  137.6 0.8 slice_multiply_fusion.1
  138.4 0.8 slice_multiply_fusion
  139.3 0.6 slice_multiply_fusion.3
  140.7 0.8 reshape.718
  (123 shorter events, 16.6 us)
Async XLA Ops:
  0.6 39.0 %copy-start = (bf16[192,576]{1,0:T(8,128)(2,1)S(1)}, bf16[192,576]{1,0:T(8,128)(2,1)}, u32[]{:S(2)}) copy-start(bf16[192,576]{1,0:T(8,128)(2,1)} %param.14) | copy-start | bytes 663556
  0.7 15.2 %copy-start.10 = (s32[96]{0:T(128)S(1)}, s32[96]{0:T(128)}, u32[]{:S(2)}) copy-start(s32[96]{0:T(128)} %param.19) | copy-start | bytes 1156
  0.7 15.7 %copy-start.8 = (f32[1,1,6,3312]{3,1,2,0:T(1,128)S(1)}, f32[1,1,6,3312]{3,1,2,0:T(1,128)}, u32[]{:S(2)}) copy-start(f32[1,1,6,3312]{3,1,2,0:T(1,128)} %param.18) | copy-start | bytes 238468
  2.1 28.3 %collective-permute-start = (bf16[2,2,3,4608]{3,1,2,0:T(2,128)(2,1)S(1)}, bf16[2,2,3,4608]{3,1,2,0:T(2,128)(2,1)S(1)}, u32[]{:S(2)}, u32[]{:S(2)}) collective-permute-start(bf16[2,2,3,4608]{3,1,2,0:T(2,128)(2,1)S(1)} %reshape.694), channel_id=1, source_target_pairs={{0,480},{32,0},{64,32},{96,64},{128,96},{160,128},{192,160},{224,1... | collective-permute-start | bytes 331784 | tf_op jit(solution)/shard_map/ppermute | solution.py:21
  30.7 5.8 %collective-permute-start.1 = (bf16[2,2,6,1152]{3,1,2,0:T(2,128)(2,1)S(1)}, bf16[2,2,6,1152]{3,1,2,0:T(2,128)(2,1)S(1)}, u32[]{:S(2)}, u32[]{:S(2)}) collective-permute-start(bf16[2,2,6,1152]{3,1,2,0:T(2,128)(2,1)S(1)} %reshape.696), channel_id=1, source_target_pairs={{0,31},{1,0},{2,1},{3,2},{4,3},{5,4},{6,5},{7,6},{8,7},{9,8},{10,9... | collective-permute-start | bytes 165896 | tf_op jit(solution)/shard_map/ppermute | solution.py:21
  36.6 1.6 %copy-start.5 = (bf16[192,192]{1,0:T(8,128)(2,1)S(1)}, bf16[192,192]{1,0:T(8,128)(2,1)}, u32[]{:S(2)}) copy-start(bf16[192,192]{1,0:T(8,128)(2,1)} %param.16) | copy-start | bytes 221188
  36.9 2.8 %copy-start.9 = (f32[192]{0:T(256)S(1)}, f32[192]{0:T(256)}, u32[]{:S(2)}) copy-start(f32[192]{0:T(256)} %param.12) | copy-start | bytes 2308
  36.9 2.8 %copy-start.11 = (f32[192]{0:T(256)S(1)}, f32[192]{0:T(256)}, u32[]{:S(2)}) copy-start(f32[192]{0:T(256)} %param.13) | copy-start | bytes 2308
  36.9 2.8 %copy-start.13 = (f32[576]{0:T(1024)S(1)}, f32[576]{0:T(1024)}, u32[]{:S(2)}) copy-start(f32[576]{0:T(1024)} %param.15) | copy-start | bytes 6916
  40.2 3.5 %copy-start.1 = (bf16[2,144,576]{1,2,0:T(8,128)(2,1)}, bf16[2,144,576]{1,2,0:T(8,128)(2,1)S(1)}, u32[]{:S(2)}) copy-start(bf16[2,144,576]{1,2,0:T(8,128)(2,1)S(1)} %copy.174) | copy-start | bytes 995332
  42.4 0.9 copy-start.7
  42.7 4.7 %copy-start.3 = (bf16[2,6,32,144]{3,2,1,0:T(8,128)(2,1)}, bf16[2,6,32,144]{3,2,1,0:T(8,128)(2,1)S(1)}, u32[]{:S(2)}) copy-start(bf16[2,6,32,144]{3,2,1,0:T(8,128)(2,1)S(1)} %convolution_convert_fusion) | copy-start | bytes 331780
  44.2 1.1 copy-start.2
  67.2 27.9 %copy-start.4 = (bf16[2,6,32,144]{3,2,1,0:T(8,128)(2,1)S(1)}, bf16[2,6,32,144]{3,2,1,0:T(8,128)(2,1)}, u32[]{:S(2)}) copy-start(bf16[2,6,32,144]{3,2,1,0:T(8,128)(2,1)} %copy-done.3) | copy-start | bytes 331780
  67.3 27.9 %copy-start.6 = (bf16[192,192]{1,0:T(8,128)(2,1)S(1)}, bf16[192,192]{1,0:T(8,128)(2,1)}, u32[]{:S(2)}) copy-start(bf16[192,192]{1,0:T(8,128)(2,1)} %param.16) | copy-start | bytes 221188
  67.3 27.9 %copy-start.12 = (f32[192]{0:T(256)S(1)}, f32[192]{0:T(256)}, u32[]{:S(2)}) copy-start(f32[192]{0:T(256)} %param.17) | copy-start | bytes 2308
  68.2 22.7 %all-to-all-start = ((bf16[32,8,768]{2,1,0:T(8,128)(2,1)}), bf16[32,8,768]{2,1,0:T(8,128)(2,1)S(1)}, u32[]{:S(2)}, u32[]{:S(2)}) async-start(bf16[32,8,768]{2,1,0:T(8,128)(2,1)} %fusion.23), calls=%async_computation | async-start | bytes 786432 | tf_op jit(solution)/shard_map/all_to_all | solution.py:269
  91.7 13.6 %all-to-all-start.1 = ((bf16[16,8,768]{2,1,0:T(8,128)(2,1)}), bf16[16,8,768]{2,1,0:T(8,128)(2,1)S(1)}, u32[]{:S(2)}, u32[]{:S(2)}) async-start(bf16[16,8,768]{2,1,0:T(8,128)(2,1)} %broadcast_in_dim.37), calls=%async_computation.1 | async-start | bytes 393216 | tf_op jit(solution)/shard_map/all_to_all | solution.py:251
  96.7 7.2 %collective-permute-start.2 = (f32[2,2,6,1152]{3,1,2,0:T(2,128)S(1)}, f32[2,2,6,1152]{3,1,2,0:T(2,128)S(1)}, u32[]{:S(2)}, u32[]{:S(2)}) collective-permute-start(f32[2,2,6,1152]{3,1,2,0:T(2,128)S(1)} %reshape.708), channel_id=1, source_target_pairs={{0,1},{1,2},{2,3},{3,4},{4,5},{5,6},{6,7},{7,8},{8,9},{9,10},{10,1... | collective-permute-start | bytes 331784 | tf_op jit(solution)/shard_map/ppermute | solution.py:21
  106.1 31.4 %all-to-all-start.2 = ((bf16[32,8,768]{2,1,0:T(8,128)(2,1)}), bf16[32,8,768]{2,1,0:T(8,128)(2,1)S(1)}, u32[]{:S(2)}, u32[]{:S(2)}) async-start(bf16[32,8,768]{2,1,0:T(8,128)(2,1)} %broadcast_in_dim.38), calls=%async_computation.2 | async-start | bytes 786432 | tf_op jit(solution)/shard_map/all_to_all | solution.py:251
  113.2 21.3 %collective-permute-start.3 = (f32[2,2,3,4608]{3,1,2,0:T(2,128)S(1)}, f32[2,2,3,4608]{3,1,2,0:T(2,128)S(1)}, u32[]{:S(2)}, u32[]{:S(2)}) collective-permute-start(f32[2,2,3,4608]{3,1,2,0:T(2,128)S(1)} %reshape.710), channel_id=1, source_target_pairs={{0,32},{32,64},{64,96},{96,128},{128,160},{160,192},{192,224},{224... | collective-permute-start | bytes 663560 | tf_op jit(solution)/shard_map/ppermute | solution.py:21

commit v2 on v0

v2 whole, which is shorter than its diff:
```python
import math

import jax
import jax.numpy as jnp
import numpy as np
from jax import lax
from jax.experimental import pallas as pl
from jax.experimental.pallas import tpu as pltpu
from jax.sharding import PartitionSpec as P

HEADS = 6
WZ = 2
WLAT = 6
WLON = 12

HALF_LAT = WLAT // 2
HALF_LON = WLON // 2
GROUP = WZ * WLAT
COUNT = GROUP * WLON
DIFFS = 2 * WLON - 1
SKEW = DIFFS * GROUP
LANES = 128
SPREAD = 3 * LANES

mask_fill = -10000.0
epsilon = 1e-05
bias_factor = 8.0

f32 = jnp.float32
bf16 = jnp.bfloat16


def matmul(a, b, dims=((1,), (0,)), precision=None):
    return lax.dot_general(a, b, (dims, ((), ())), preferred_element_type=f32, precision=precision)


def order_of_skew():
    place = np.zeros((SKEW, SPREAD), np.float32)
    for z in range(WZ):
        for r in range(WLAT):
            for d in range(DIFFS):
                place[(z * WLAT + r) * DIFFS + d, (DIFFS - 1 - d) * GROUP + z * WLAT + r] = 1.0
    return place


def bias_kernel(table_ref, place_ref, masked_ref, add_ref):
    skewed = matmul(table_ref[...], place_ref[...], precision=lax.Precision.HIGHEST)
    for i in range(WLON):
        shift = (GROUP * (i - WLON + 1)) % SPREAD
        rolled = skewed if shift == 0 else pltpu.roll(skewed, shift, 1)
        rows = slice(i * GROUP, (i + 1) * GROUP)
        masked = masked_ref[rows, :]
        for h in range(HEADS):
            add_ref[h * COUNT + i * GROUP : h * COUNT + (i + 1) * GROUP, :] = (
                rolled[h * GROUP : (h + 1) * GROUP, :COUNT] + masked
            )


def head_lanes(width, h):
    lane = lax.broadcasted_iota(jnp.int32, (1, width), 1)
    return (lane // 32 == h).astype(f32)


def attention_kernel(
    x_ref,
    dy_ref,
    gain_ref,
    shift_ref,
    qkv_weight_ref,
    qkv_bias_ref,
    proj_weight_ref,
    proj_bias_ref,
    add_ref,
    out_ref,
    grad_ref,
    parts_ref,
    d_bias_ref,
):
    tokens, width = x_ref.shape
    windows = tokens // COUNT
    head_dim = width // HEADS
    scale = 1.0 / math.sqrt(head_dim)
    xf = x_ref[...].astype(f32)
    mean_value = jnp.mean(xf, axis=-1, keepdims=True)
    centered = xf - mean_value
    inverse = lax.rsqrt(jnp.mean(centered * centered, axis=-1, keepdims=True) + epsilon)
    xhat = centered * inverse
    gain = gain_ref[...]
    normed = (xhat * gain + shift_ref[...]).astype(bf16)
    weights = [qkv_weight_ref[:, k * width : (k + 1) * width] for k in range(3)]
    q, k, v = [
        (matmul(normed, weights[i]) + qkv_bias_ref[:, i * width : (i + 1) * width]).astype(bf16)
        for i in range(3)
    ]
    dy = dy_ref[...]
    proj_weight = proj_weight_ref[...]
    d_attn = matmul(dy, proj_weight, ((1,), (1,))).astype(bf16)
    tiles = [(0, 4), (4, 2)]
    whole = []
    for w in range(windows):
        rows = slice(w * COUNT, (w + 1) * COUNT)
        per_tile = []
        for first, heads in tiles:
            lanes = slice(first * head_dim, (first + heads) * head_dim)
            masks = [head_lanes(heads * head_dim, h) for h in range(heads)]
            masks_b = [m.astype(bf16) for m in masks]
            qt, kt, vt, at = q[rows, lanes], k[rows, lanes], v[rows, lanes], d_attn[rows, lanes]
            q_stack = jnp.concatenate([qt * m for m in masks_b], axis=0)
            a_stack = jnp.concatenate([at * m for m in masks_b], axis=0)

            def by_head(stacked):
                total = stacked[:COUNT] * masks[0]
                for h in range(1, heads):
                    total = total + stacked[h * COUNT : (h + 1) * COUNT] * masks[h]
                return total

            at_rows = slice(first * COUNT, (first + heads) * COUNT)
            scores = matmul(q_stack, kt, ((1,), (1,))) * scale + add_ref[at_rows, :]
            top = jnp.max(scores, axis=-1, keepdims=True)
            e = jnp.exp(scores - top)
            probs_f = e * (1.0 / jnp.sum(e, axis=-1, keepdims=True))
            probs = probs_f.astype(bf16)
            attn = by_head(matmul(probs, vt)).astype(bf16)
            d_probs = matmul(a_stack, vt, ((1,), (1,)))
            d_scores = probs_f * (d_probs - jnp.sum(probs_f * d_probs, axis=-1, keepdims=True))
            if w == 0:
                d_bias_ref[at_rows, :] = d_scores
            else:
                d_bias_ref[at_rows, :] += d_scores
            d_scores_b = d_scores.astype(bf16)
            d_v = matmul(probs, a_stack, ((0,), (0,))).astype(bf16)
            d_q = (by_head(matmul(d_scores_b, kt)) * scale).astype(bf16)
            d_k = (matmul(d_scores_b, q_stack, ((0,), (0,))) * scale).astype(bf16)
            per_tile.append((attn, d_q, d_k, d_v))
        whole.append([jnp.concatenate([t[i] for t in per_tile], axis=1) for i in range(4)])
    attn, d_q, d_k, d_v = [jnp.concatenate([t[i] for t in whole], axis=0) for i in range(4)]
    out_ref[...] = xf + matmul(attn, proj_weight) + proj_bias_ref[...]
    d_parts = (d_q, d_k, d_v)
    d_normed = sum(matmul(d_parts[i], weights[i], ((1,), (1,))) for i in range(3))
    d_xhat = d_normed * gain
    grad_ref[...] = dy.astype(f32) + inverse * (
        d_xhat
        - jnp.mean(d_xhat, axis=-1, keepdims=True)
        - xhat * jnp.mean(d_xhat * xhat, axis=-1, keepdims=True)
    )
    d_qkv = jnp.concatenate(d_parts, axis=1)
    qkv_weight_grad = matmul(normed, d_qkv, ((0,), (0,)))
    proj_weight_grad = matmul(attn, dy, ((0,), (0,)))
    matrix = jnp.concatenate([qkv_weight_grad, proj_weight_grad], axis=1)
    vector = jnp.concatenate(
        [
            jnp.sum(d_normed * xhat, axis=0, keepdims=True),
            jnp.sum(d_normed, axis=0, keepdims=True),
            jnp.sum(d_qkv.astype(f32), axis=0, keepdims=True),
            jnp.sum(dy.astype(f32), axis=0, keepdims=True),
        ],
        axis=1,
    )
    skewed = jnp.zeros((HEADS * GROUP, SPREAD), f32)
    for i in range(WLON):
        part = jnp.concatenate(
            [
                d_bias_ref[h * COUNT + i * GROUP : h * COUNT + (i + 1) * GROUP, :]
                for h in range(HEADS)
            ],
            axis=0,
        )
        part = jnp.concatenate([part, jnp.zeros((HEADS * GROUP, SPREAD - COUNT), f32)], axis=1)
        shift = GROUP * (WLON - 1 - i)
        skewed = skewed + (part if shift == 0 else pltpu.roll(part, shift, 1))
    pack(parts_ref, matrix, vector, skewed)


def table_slots(pieces, pairs):
    slots = []
    for p in range(pairs):
        if p < pieces:
            slots.append((p, 0, p, 4 * LANES))
        else:
            slots.append((p - pieces, 2 * LANES, p - pieces + (pairs - pieces), 2 * LANES))
    return slots


def pack(parts_ref, matrix, vector, skewed):
    pieces = parts_ref.shape[0]
    rows = matrix.shape[0] // pieces
    for d in range(pieces):
        parts_ref[d, 0:rows, :] = matrix[d * rows : (d + 1) * rows, :]
        parts_ref[d, rows:8, :] = jnp.zeros((8 - rows, matrix.shape[1]), f32)
    for p, (d, at, d2, at2) in enumerate(table_slots(pieces, skewed.shape[0] // 2)):
        pair = slice(2 * p, 2 * p + 2)
        parts_ref[d, rows : rows + 2, at : at + 2 * LANES] = skewed[pair, : 2 * LANES]
        parts_ref[d2, rows : rows + 2, at2 : at2 + LANES] = skewed[pair, 2 * LANES :]
    for d in range(vector.shape[1] // LANES):
        parts_ref[d, rows : rows + 1, 5 * LANES :] = vector[:, d * LANES : (d + 1) * LANES]


def unpack_kernel(norm_by, full_ref, place_ref, qkv_ref, proj_ref, table_ref, gain_ref, shift_ref, qkv_bias_ref, proj_bias_ref, wide_ref, skewed_ref):
    pieces = full_ref.shape[0]
    width, wide = qkv_ref.shape
    rows = width // pieces
    wide_ref[...] = full_ref[...].astype(f32)
    for d in range(pieces):
        piece = wide_ref[d, 0:rows, :] * norm_by
        qkv_ref[d * rows : (d + 1) * rows, :] = piece[:, :wide]
        proj_ref[d * rows : (d + 1) * rows, :] = piece[:, wide:]
    for p, (d, at, d2, at2) in enumerate(table_slots(pieces, skewed_ref.shape[0] // 2)):
        skewed_ref[2 * p : 2 * p + 2, : 2 * LANES] = wide_ref[d, rows : rows + 2, at : at + 2 * LANES]
        skewed_ref[2 * p : 2 * p + 2, 2 * LANES :] = wide_ref[d2, rows : rows + 2, at2 : at2 + LANES]
    table_ref[...] = matmul(
        skewed_ref[...] * bias_factor, place_ref[...], ((1,), (1,)), lax.Precision.HIGHEST
    )
    count = (3 * width + wide) // LANES
    vector = jnp.concatenate(
        [wide_ref[d, rows : rows + 1, 5 * LANES :] for d in range(count)], axis=1
    )
    vector = vector * norm_by
    gain_ref[...] = vector[:, :width]
    shift_ref[...] = vector[:, width : 2 * width]
    qkv_bias_ref[...] = vector[:, 2 * width : 2 * width + wide]
    proj_bias_ref[...] = vector[:, 2 * width + wide :]


VMEM_LIMIT = 48 * 1024 * 1024


def call(kernel, out_shape, name, scratch=()):
    return pl.pallas_call(
        kernel,
        out_shape=out_shape,
        scratch_shapes=scratch,
        compiler_params=pltpu.CompilerParams(vmem_limit_bytes=VMEM_LIMIT),
        name=name,
    )


def struct(shape, dtype=f32):
    return jax.ShapeDtypeStruct(shape, dtype)


def spread_to_all(piece, axis):
    count = lax.axis_size(axis)
    return lax.all_to_all(jnp.broadcast_to(piece[None], (count,) + piece.shape), axis, 0, 0)


def reduce_all(parts, rows):
    by_lon = jnp.sum(lax.all_to_all(parts.astype(bf16), "lon", 0, 0).astype(f32), axis=0)
    by_lat = jnp.sum(spread_to_all(by_lon.astype(bf16), "lat").astype(f32), axis=0)
    row = lax.broadcasted_iota(jnp.int32, by_lat.shape, 0)
    column = lax.broadcasted_iota(jnp.int32, by_lat.shape, 1)
    is_table = (row >= rows) & (column < 5 * LANES)
    done = jnp.where(is_table, by_lon, by_lat).astype(bf16)
    return spread_to_all(done, "lon")


def mask_of_windows(lat_valid, band, levels):
    total_rows = lat_valid.shape[0]
    position = jnp.arange(COUNT, dtype=jnp.int32)
    level = position % GROUP // WLAT
    row_in = position % WLAT
    level_region = (level >= levels - WZ).astype(jnp.int32) + (level >= levels - WZ // 2).astype(jnp.int32)
    row = band * WLAT + row_in
    row_region = (row >= total_rows - WLAT).astype(jnp.int32) + (row >= total_rows - HALF_LAT).astype(jnp.int32)
    rolled = jnp.roll(lat_valid, -HALF_LAT)
    valid = lax.dynamic_slice_in_dim(rolled, band * WLAT, WLAT)
    key_ok = jnp.tile(valid, WZ * WLON)
    allowed = (
        (level_region[:, None] == level_region[None, :])
        & (row_region[:, None] == row_region[None, :])
        & (key_ok[None, :] == 1)
    )
    return jnp.where(allowed, f32(0.0), f32(mask_fill))


def to_neighbour(value, axes, steps):
    counts = [lax.axis_size(a) for a in axes]
    if len(axes) == 1:
        n = counts[0]
        return lax.ppermute(value, axes[0], [(i, (i + steps[0]) % n) for i in range(n)])
    na, nb = counts
    pairs = [
        (a * nb + b, (a + steps[0]) % na * nb + (b + steps[1]) % nb)
        for a in range(na)
        for b in range(nb)
    ]
    return lax.ppermute(value, axes, pairs)


def local(
    tokens,
    cotangent,
    norm_gain_vector,
    norm_bias_vector,
    qkv_weight,
    qkv_bias,
    proj_weight,
    proj_bias,
    earth_bias,
    lat_valid,
):
    levels, rows, cols, width = tokens.shape
    wide = qkv_weight.shape[1]
    lat_count = lax.axis_size("lat")
    lon_count = lax.axis_size("lon")
    total = levels * rows * cols
    lat_halo = jnp.stack([a[:, :HALF_LAT, HALF_LON:] for a in (tokens, cotangent)])
    lon_halo = jnp.stack([a[:, HALF_LAT:, :HALF_LON] for a in (tokens, cotangent)])
    corner = jnp.stack([a[:, :HALF_LAT, :HALF_LON] for a in (tokens, cotangent)])
    lat_halo = to_neighbour(lat_halo, ("lat",), (-1,))
    corner = to_neighbour(corner, ("lat", "lon"), (-1, -1))
    lon_halo = to_neighbour(lon_halo, ("lon",), (-1,))

    place = jnp.asarray(order_of_skew())
    table = earth_bias.reshape(HEADS, WZ, WZ, WLAT, WLAT * DIFFS).transpose(0, 1, 3, 2, 4)
    masked = mask_of_windows(lat_valid, lax.axis_index("lat"), levels)
    add = call(bias_kernel, struct((HEADS * COUNT, COUNT)), "bias")(
        table.reshape(HEADS * GROUP, SKEW), place, masked
    )

    def windows_of(kind, array):
        own = jnp.concatenate([array[:, HALF_LAT:, HALF_LON:], lat_halo[kind]], axis=1)
        side = jnp.concatenate([lon_halo[kind], corner[kind]], axis=1)
        moved = jnp.roll(jnp.concatenate([own, side], axis=2), -(WZ // 2), axis=0)
        return moved.transpose(2, 0, 1, 3).reshape(total, width)

    out, grad, parts = call(
        attention_kernel,
        (struct((total, width)), struct((total, width)), struct((lon_count, 8, wide + width))),
        "attention",
        [pltpu.VMEM((HEADS * COUNT, COUNT), f32)],
    )(
        windows_of(0, tokens),
        windows_of(1, cotangent),
        norm_gain_vector[None],
        norm_bias_vector[None],
        qkv_weight,
        qkv_bias[None],
        proj_weight,
        proj_bias[None],
        add,
    )
    full = reduce_all(parts, width // lon_count)

    both = jnp.stack([out, grad]).reshape(2, cols, levels, rows, width)
    both = jnp.roll(both, WZ // 2, axis=2).transpose(0, 2, 3, 1, 4)
    half = both.astype(bf16)
    inner = rows - HALF_LAT
    edge = cols - HALF_LON
    lat_back = to_neighbour(half[:, :, inner:, :edge], ("lat",), (1,))
    corner_back = to_neighbour(half[:, :, inner:, edge:], ("lat", "lon"), (1, 1))
    lon_back = to_neighbour(half[:, :, :inner, edge:], ("lon",), (1,))
    top = jnp.concatenate([corner_back, lat_back], axis=3).astype(f32)
    bottom = jnp.concatenate([lon_back.astype(f32), both[:, :, :inner, :edge]], axis=3)
    back = jnp.concatenate([top, bottom], axis=2)

    norm_by = 1.0 / math.sqrt(total * lat_count * lon_count)

    def unpack(*refs):
        unpack_kernel(norm_by, *refs)

    qkv_weight_grad, proj_weight_grad, table, gain, shift, qkv_bias_grad, proj_bias_grad = call(
        unpack,
        (
            struct((width, wide)),
            struct((width, width)),
            struct((HEADS * GROUP, SKEW)),
            struct((1, width)),
            struct((1, width)),
            struct((1, wide)),
            struct((1, width)),
        ),
        "unpack",
        [pltpu.VMEM((lon_count, 8, wide + width), f32), pltpu.VMEM((HEADS * GROUP, SPREAD), f32)],
    )(full, place)
    table = table.reshape(HEADS, WZ, WLAT, WZ, WLAT * DIFFS).transpose(0, 1, 3, 2, 4)
    return (
        back[0],
        back[1],
        gain[0],
        shift[0],
        qkv_weight_grad,
        qkv_bias_grad[0],
        proj_weight_grad,
        proj_bias_grad[0],
        table.reshape(earth_bias.shape),
    )


def solution(mesh):
    placed = (
        P(None, "lat", "lon", None),
        P(None, "lat", "lon", None),
        P(),
        P(),
        P(),
        P(),
        P(),
        P(),
        P(None, "lat", None, None),
        P(),
    )
    return jax.shard_map(
        local,
        mesh=mesh,
        in_specs=placed,
        out_specs=(
            P(None, "lat", "lon", None),
            P(None, "lat", "lon", None),
            P(),
            P(),
            P(),
            P(),
            P(),
            P(),
            P(None, "lat", None, None),
        ),
        check_vma=False,
    )
```

time: 668 us -> 107 us (0.16)
  waiting for transfers between devices: 471 us -> 35.7 us
  blocking collectives: 98.2 us -> 0 us
  starting transfers between devices: 20.8 us -> 51.8 us
  local copies, waits for them, and re-layouts: 40.2 us -> 9.37 us
  between operations: 14.7 us -> 1.15 us
  matrix products: 10.9 us -> 0 us
  other arithmetic: 11.4 us -> 2.8 us
    psum x2 -> x0, waiting for transfers between devices: 469 us -> none  [the longest x1 273 us: local(): lax.psum((gain_gradient, shift_grad, qkv_weight_grad, qkv_bias_grad, proj...]
    psum x1 -> x0, blocking collectives: 98.2 us -> none  [local(): lax.psum((gain_gradient, shift_grad, qkv_weight_grad, qkv_bias_grad, proj...]
    all_to_all x0 -> x3, waiting for transfers between devices: none -> 23.1 us  [the longest x1 13.6 us: reduce_all(): lax.all_to_all(parts.astype(bf16), 'lon', 0, 0).astype(f32)]
    all_to_all x0 -> x3, starting transfers between devices: none -> 20.9 us  [the longest x2 14.4 us: spread_to_all(): lax.all_to_all(jnp.broadcast_to(piece[None], (count,) + piece.shape), axi...]
    transpose x5 -> x3, local copies, waits for them, and re-layouts: 12.1 us -> 0.15 us  [the longest x1 0.08 us: local(): earth_bias.reshape(HEADS, WZ, WZ, WLAT, WLAT * DIFFS)]
    ppermute x4 -> x6, starting transfers between devices: 20.7 us -> 30.9 us  [the longest x2 17.4 us: to_neighbour(): return lax.ppermute(value, axes, pairs)]
    ppermute x4 -> x6, waiting for transfers between devices: 2.63 us -> 12.6 us  [the longest x2 11.5 us: to_neighbour(): return lax.ppermute(value, axes, pairs)]
    reshape x12 -> x7, local copies, waits for them, and re-layouts: 11.5 us -> 1.56 us  [the longest x1 0.85 us: local(): table.reshape(earth_bias.shape)]
  transfers between devices with their start and end apart: 6 -> 9, of which waited for: 3 -> 4; matrix products, arithmetic and copies ran while one was open for 7% -> 4% of each run, Pallas kernels for 0% -> 1%
where the time goes in v2:
time: 107 us
  starting transfers between devices  51.8 us (48%)
  waiting for transfers between devices  35.7 us (33%)
  local copies, waits for them, and re-layouts  9.37 us (9%)
  Pallas kernels  6.07 us (6%)
  other arithmetic  2.8 us (3%)
  between operations  1.15 us (1%)
    ppermute x2, starting transfers between devices, to_neighbour(): return lax.ppermute(value, axes, pairs)  17.4 us
    all_to_all x2, starting transfers between devices, spread_to_all(): lax.all_to_all(jnp.broadcast_to(piece[None], (count,) + piece.shape), axi...  14.4 us
    all_to_all x1, waiting for transfers between devices, reduce_all(): lax.all_to_all(parts.astype(bf16), 'lon', 0, 0).astype(f32)  13.6 us
    ppermute x4, starting transfers between devices, to_neighbour(): lax.ppermute(value, axes[0], [(i, (i + steps[0]) % n) for i in range(n)])  13.5 us
    ppermute x2, waiting for transfers between devices, to_neighbour(): return lax.ppermute(value, axes, pairs)  11.5 us
    all_to_all x2, waiting for transfers between devices, spread_to_all(): lax.all_to_all(jnp.broadcast_to(piece[None], (count,) + piece.shape), axi...  9.5 us
    all_to_all x1, starting transfers between devices, reduce_all(): lax.all_to_all(parts.astype(bf16), 'lon', 0, 0).astype(f32)  6.49 us
    unnamed x25, local copies, waits for them, and re-layouts  4.65 us
  transfers between devices with their start and end apart: 9, of which 4 were waited for; matrix products, arithmetic and copies ran while one was open for 4% of the time, Pallas kernels for 1%

profile of v2, /device:TPU:1, one launch (start us, length us, event | category | flops | bytes accessed | tf_op | source)
XLA Modules:
  0.0 106.8 jit_solution(17858809969510911591)
XLA Ops:
  0.7 0.8 slice_bitcast_fusion.12
  1.5 14.4 %collective-permute-start.2 = (bf16[2,2,3,6,192]{4,3,2,1,0:T(8,128)(2,1)S(1)}, bf16[2,2,3,6,192]{4,3,2,1,0:T(8,128)(2,1)S(1)}, u32[]{:S(2)}, u32[]{:S(2)}) collective-permute-start(bf16[2,2,3,6,192]{4,3,2,1,0:T(8,128)(2,1)S(1)} %pad_maximum_fusion.2), channel_id=1, source_target_pairs={{0,511},{1,480},{2,481},{3,482},{4,483},{5,484},{6,485},{7,486},{8... | collective-permute-start | bytes 82952 | tf_op jit(solution)/shard_map/ppermute | solution.py:286
  15.9 4.7 %collective-permute-start.1 = (bf16[2,2,3,6,192]{4,3,2,1,0:T(8,128)(2,1)S(1)}, bf16[2,2,3,6,192]{4,3,2,1,0:T(8,128)(2,1)S(1)}, u32[]{:S(2)}, u32[]{:S(2)}) collective-permute-start(bf16[2,2,3,6,192]{4,3,2,1,0:T(8,128)(2,1)S(1)} %pad_maximum_fusion.1), channel_id=1, source_target_pairs={{0,31},{1,0},{2,1},{3,2},{4,3},{5,4},{6,5},{7,6},{8,7},{9,8},{10,9... | collective-permute-start | bytes 82952 | tf_op jit(solution)/shard_map/ppermute | solution.py:279
  20.7 3.4 %collective-permute-start = (bf16[2,2,3,18,192]{4,3,2,1,0:T(8,128)(2,1)S(1)}, bf16[2,2,3,18,192]{4,3,2,1,0:T(8,128)(2,1)S(1)}, u32[]{:S(2)}, u32[]{:S(2)}) collective-permute-start(bf16[2,2,3,18,192]{4,3,2,1,0:T(8,128)(2,1)S(1)} %pad_maximum_fusion), channel_id=1, source_target_pairs={{0,480},{32,0},{64,32},{96,64},{128,96},{160,128},{192,160},{224,1... | collective-permute-start | bytes 248840 | tf_op jit(solution)/shard_map/ppermute | solution.py:279
  24.1 0.6 copy-done.10
  25.3 0.6 copy-done.9
  26.0 0.2 reduce
  26.2 0.2 reshape.159
  26.7 0.6 copy-done
  27.2 0.8 bias.1.add_ref
  28.1 1.1 collective-permute-done
  29.7 0.8 copy-done.1
  30.6 3.8 %attention.1 = (f32[288,192]{1,0:T(8,128)S(1)}, f32[288,192]{1,0:T(8,128)S(1)}, f32[32,8,768]{2,1,0:T(8,128)S(1)}) custom-call(bf16[288,192]{1,0:T(8,128)(2,1)S(1)} %reshape.157.x_ref, bf16[288,192]{1,0:T(8,128)(2,1)S(1)} %reshape.158.dy_ref, f32[1,192]{1,0:T(1,128)S(1)} %bitcast.47, f32[1,192]{1,0:T(1,128)S(1)} %bitcast.48, bf16[192,576]{1,0:T(8,128)(2,1)S(1)} %copy-done.1, ...), custom_call_target="tpu_custom_call" | custom-call | tf_op jit(solution)/shard_map/attention/pallas_call | solution.py:326
  34.4 0.8 convert_element_type.83
  35.2 6.5 %all-to-all-start = ((bf16[32,8,768]{2,1,0:T(8,128)(2,1)}), bf16[32,8,768]{2,1,0:T(8,128)(2,1)S(1)}, u32[]{:S(2)}, u32[]{:S(2)}) async-start(bf16[32,8,768]{2,1,0:T(8,128)(2,1)} %convert_element_type.83), calls=%async_computation | async-start | bytes 786432 | tf_op jit(solution)/shard_map/all_to_all | solution.py:247
  41.9 13.6 %all-to-all-done = bf16[32,8,768]{2,1,0:T(8,128)(2,1)S(1)} async-done(((bf16[32,8,768]{2,1,0:T(8,128)(2,1)}), bf16[32,8,768]{2,1,0:T(8,128)(2,1)S(1)}, u32[]{:S(2)}, u32[]{:S(2)}) %all-to-all-start) | async-done | bytes 393248 | tf_op jit(solution)/shard_map/all_to_all | solution.py:247
  55.5 0.7 broadcast_in_dim.42
  56.2 7.8 %all-to-all-start.1 = ((bf16[16,8,768]{2,1,0:T(8,128)(2,1)}), bf16[16,8,768]{2,1,0:T(8,128)(2,1)S(1)}, u32[]{:S(2)}, u32[]{:S(2)}) async-start(bf16[16,8,768]{2,1,0:T(8,128)(2,1)} %broadcast_in_dim.42), calls=%async_computation.1 | async-start | bytes 393216 | tf_op jit(solution)/shard_map/all_to_all | solution.py:243
  64.3 9.5 %all-to-all-done.1 = bf16[16,8,768]{2,1,0:T(8,128)(2,1)S(1)} async-done(((bf16[16,8,768]{2,1,0:T(8,128)(2,1)}), bf16[16,8,768]{2,1,0:T(8,128)(2,1)S(1)}, u32[]{:S(2)}, u32[]{:S(2)}) %all-to-all-start.1) | async-done | bytes 196640 | tf_op jit(solution)/shard_map/all_to_all | solution.py:243
  73.9 0.8 broadcast_in_dim.43
  74.7 6.6 %all-to-all-start.2 = ((bf16[32,8,768]{2,1,0:T(8,128)(2,1)}), bf16[32,8,768]{2,1,0:T(8,128)(2,1)S(1)}, u32[]{:S(2)}, u32[]{:S(2)}) async-start(bf16[32,8,768]{2,1,0:T(8,128)(2,1)} %broadcast_in_dim.43), calls=%async_computation.2 | async-start | bytes 786432 | tf_op jit(solution)/shard_map/all_to_all | solution.py:243
  81.3 3.5 %collective-permute-start.5 = (bf16[2,2,3,6,192]{4,2,1,3,0:T(4,128)(2,1)S(1)}, bf16[2,2,3,6,192]{4,2,1,3,0:T(4,128)(2,1)S(1)}, u32[]{:S(2)}, u32[]{:S(2)}) collective-permute-start(bf16[2,2,3,6,192]{4,2,1,3,0:T(4,128)(2,1)S(1)} %get-tuple-element.52), channel_id=1, source_target_pairs={{0,1},{1,2},{2,3},{3,4},{4,5},{5,6},{6,7},{7,8},{8,9},{9,10},{10,1... | collective-permute-start | bytes 82952 | tf_op jit(solution)/shard_map/ppermute | solution.py:279
  84.9 1.9 %collective-permute-start.4 = (bf16[2,2,3,18,192]{4,2,1,3,0:T(4,128)(2,1)S(1)}, bf16[2,2,3,18,192]{4,2,1,3,0:T(4,128)(2,1)S(1)}, u32[]{:S(2)}, u32[]{:S(2)}) collective-permute-start(bf16[2,2,3,18,192]{4,2,1,3,0:T(4,128)(2,1)S(1)} %slice.131), channel_id=1, source_target_pairs={{0,32},{32,64},{64,96},{96,128},{128,160},{160,192},{192,224},{224... | collective-permute-start | bytes 248840 | tf_op jit(solution)/shard_map/ppermute | solution.py:279
  86.8 3.0 %collective-permute-start.3 = (bf16[2,2,3,6,192]{4,2,1,3,0:T(4,128)(2,1)S(1)}, bf16[2,2,3,6,192]{4,2,1,3,0:T(4,128)(2,1)S(1)}, u32[]{:S(2)}, u32[]{:S(2)}) collective-permute-start(bf16[2,2,3,6,192]{4,2,1,3,0:T(4,128)(2,1)S(1)} %get-tuple-element.51), channel_id=1, source_target_pairs={{0,33},{1,34},{2,35},{3,36},{4,37},{5,38},{6,39},{7,40},{8,41},{9,... | collective-permute-start | bytes 82952 | tf_op jit(solution)/shard_map/ppermute | solution.py:286
  90.0 11.5 %collective-permute-done.3 = bf16[2,2,3,6,192]{4,2,1,3,0:T(4,128)(2,1)S(1)} collective-permute-done((bf16[2,2,3,6,192]{4,2,1,3,0:T(4,128)(2,1)S(1)}, bf16[2,2,3,6,192]{4,2,1,3,0:T(4,128)(2,1)S(1)}, u32[]{:S(2)}, u32[]{:S(2)}) %collective-permute-start.3) | collective-permute-done | bytes 27680 | tf_op jit(solution)/shard_map/ppermute | solution.py:286
  101.7 0.2 maximum_maximum_fusion
  101.9 0.9 copy.37
  102.8 0.9 copy.38
  103.7 1.5 %unpack.1 = (f32[192,576]{1,0:T(8,128)}, f32[192,192]{1,0:T(8,128)}, f32[72,276]{1,0:T(8,128)S(1)}, f32[1,192]{1,0:T(1,128)}, f32[1,192]{1,0:T(1,128)}, /*index=5*/f32[1,576]{1,0:T(1,128)S(1)}, f32[1,192]{1,0:T(1,128)}) custom-call(bf16[32,8,768]{2,1,0:T(8,128)(2,1)S(1)} %all-to-all-done.2.refs_0_, f32[276,384]{1,0:T(8,128)S(1)} %copy-done), custom_call_target="tpu_custom_call" | custom-call | tf_op jit(solution)/shard_map/unpack/pallas_call | solution.py:361
  105.2 0.6 reduce.1
  105.8 0.2 reshape.161
  106.0 0.8 reshape.163
  (69 shorter events, 2.6 us)
Async XLA Ops:
  0.6 20.0 %copy-start.7 = (bf16[2,6,24,192]{3,2,1,0:T(8,128)(2,1)S(1)}, bf16[2,6,24,192]{3,2,1,0:T(8,128)(2,1)}, u32[]{:S(2)}) copy-start(bf16[2,6,24,192]{3,2,1,0:T(8,128)(2,1)} %param.11) | copy-start | bytes 331780
  1.5 19.1 %copy-start.6 = (bf16[2,6,24,192]{3,2,1,0:T(8,128)(2,1)S(1)}, bf16[2,6,24,192]{3,2,1,0:T(8,128)(2,1)}, u32[]{:S(2)}) copy-start(bf16[2,6,24,192]{3,2,1,0:T(8,128)(2,1)} %param.12) | copy-start | bytes 331780
  1.5 26.5 %collective-permute-start.2 = (bf16[2,2,3,6,192]{4,3,2,1,0:T(8,128)(2,1)S(1)}, bf16[2,2,3,6,192]{4,3,2,1,0:T(8,128)(2,1)S(1)}, u32[]{:S(2)}, u32[]{:S(2)}) collective-permute-start(bf16[2,2,3,6,192]{4,3,2,1,0:T(8,128)(2,1)S(1)} %pad_maximum_fusion.2), channel_id=1, source_target_pairs={{0,511},{1,480},{2,481},{3,482},{4,483},{5,484},{6,485},{7,486},{8... | collective-permute-start | bytes 82952 | tf_op jit(solution)/shard_map/ppermute | solution.py:286
  15.9 12.1 %collective-permute-start.1 = (bf16[2,2,3,6,192]{4,3,2,1,0:T(8,128)(2,1)S(1)}, bf16[2,2,3,6,192]{4,3,2,1,0:T(8,128)(2,1)S(1)}, u32[]{:S(2)}, u32[]{:S(2)}) collective-permute-start(bf16[2,2,3,6,192]{4,3,2,1,0:T(8,128)(2,1)S(1)} %pad_maximum_fusion.1), channel_id=1, source_target_pairs={{0,31},{1,0},{2,1},{3,2},{4,3},{5,4},{6,5},{7,6},{8,7},{9,8},{10,9... | collective-permute-start | bytes 82952 | tf_op jit(solution)/shard_map/ppermute | solution.py:279
  20.7 8.4 %collective-permute-start = (bf16[2,2,3,18,192]{4,3,2,1,0:T(8,128)(2,1)S(1)}, bf16[2,2,3,18,192]{4,3,2,1,0:T(8,128)(2,1)S(1)}, u32[]{:S(2)}, u32[]{:S(2)}) collective-permute-start(bf16[2,2,3,18,192]{4,3,2,1,0:T(8,128)(2,1)S(1)} %pad_maximum_fusion), channel_id=1, source_target_pairs={{0,480},{32,0},{64,32},{96,64},{128,96},{160,128},{192,160},{224,1... | collective-permute-start | bytes 248840 | tf_op jit(solution)/shard_map/ppermute | solution.py:279
  24.1 0.7 copy-start.10
  25.1 0.9 copy-start.8
  25.1 0.7 copy-start.9
  26.2 1.0 copy-start
  29.6 0.9 copy-start.1
  29.6 1.0 copy-start.2
  29.6 1.0 copy-start.4
  29.6 1.0 copy-start.5
  29.7 0.9 copy-start.3
  35.2 20.3 %all-to-all-start = ((bf16[32,8,768]{2,1,0:T(8,128)(2,1)}), bf16[32,8,768]{2,1,0:T(8,128)(2,1)S(1)}, u32[]{:S(2)}, u32[]{:S(2)}) async-start(bf16[32,8,768]{2,1,0:T(8,128)(2,1)} %convert_element_type.83), calls=%async_computation | async-start | bytes 786432 | tf_op jit(solution)/shard_map/all_to_all | solution.py:247
  56.2 17.6 %all-to-all-start.1 = ((bf16[16,8,768]{2,1,0:T(8,128)(2,1)}), bf16[16,8,768]{2,1,0:T(8,128)(2,1)S(1)}, u32[]{:S(2)}, u32[]{:S(2)}) async-start(bf16[16,8,768]{2,1,0:T(8,128)(2,1)} %broadcast_in_dim.42), calls=%async_computation.1 | async-start | bytes 393216 | tf_op jit(solution)/shard_map/all_to_all | solution.py:243
  74.7 29.1 %all-to-all-start.2 = ((bf16[32,8,768]{2,1,0:T(8,128)(2,1)}), bf16[32,8,768]{2,1,0:T(8,128)(2,1)S(1)}, u32[]{:S(2)}, u32[]{:S(2)}) async-start(bf16[32,8,768]{2,1,0:T(8,128)(2,1)} %broadcast_in_dim.43), calls=%async_computation.2 | async-start | bytes 786432 | tf_op jit(solution)/shard_map/all_to_all | solution.py:243
  81.3 8.7 %collective-permute-start.5 = (bf16[2,2,3,6,192]{4,2,1,3,0:T(4,128)(2,1)S(1)}, bf16[2,2,3,6,192]{4,2,1,3,0:T(4,128)(2,1)S(1)}, u32[]{:S(2)}, u32[]{:S(2)}) collective-permute-start(bf16[2,2,3,6,192]{4,2,1,3,0:T(4,128)(2,1)S(1)} %get-tuple-element.52), channel_id=1, source_target_pairs={{0,1},{1,2},{2,3},{3,4},{4,5},{5,6},{6,7},{7,8},{8,9},{9,10},{10,1... | collective-permute-start | bytes 82952 | tf_op jit(solution)/shard_map/ppermute | solution.py:279
  84.9 16.7 %collective-permute-start.4 = (bf16[2,2,3,18,192]{4,2,1,3,0:T(4,128)(2,1)S(1)}, bf16[2,2,3,18,192]{4,2,1,3,0:T(4,128)(2,1)S(1)}, u32[]{:S(2)}, u32[]{:S(2)}) collective-permute-start(bf16[2,2,3,18,192]{4,2,1,3,0:T(4,128)(2,1)S(1)} %slice.131), channel_id=1, source_target_pairs={{0,32},{32,64},{64,96},{96,128},{128,160},{160,192},{192,224},{224... | collective-permute-start | bytes 248840 | tf_op jit(solution)/shard_map/ppermute | solution.py:279
  86.8 14.8 %collective-permute-start.3 = (bf16[2,2,3,6,192]{4,2,1,3,0:T(4,128)(2,1)S(1)}, bf16[2,2,3,6,192]{4,2,1,3,0:T(4,128)(2,1)S(1)}, u32[]{:S(2)}, u32[]{:S(2)}) collective-permute-start(bf16[2,2,3,6,192]{4,2,1,3,0:T(4,128)(2,1)S(1)} %get-tuple-element.51), channel_id=1, source_target_pairs={{0,33},{1,34},{2,35},{3,36},{4,37},{5,38},{6,39},{7,40},{8,41},{9,... | collective-permute-start | bytes 82952 | tf_op jit(solution)/shard_map/ppermute | solution.py:286

commit v3 on v2

--- a/solution.py
+++ b/solution.py
@@ -2,7 +2,6 @@
 
 import jax
 import jax.numpy as jnp
-import numpy as np
 from jax import lax
 from jax.experimental import pallas as pl
 from jax.experimental.pallas import tpu as pltpu
@@ -18,7 +17,7 @@
 GROUP = WZ * WLAT
 COUNT = GROUP * WLON
 DIFFS = 2 * WLON - 1
-SKEW = DIFFS * GROUP
+SIDE = WLAT * DIFFS
 LANES = 128
 SPREAD = 3 * LANES
 
@@ -34,34 +33,83 @@
     return lax.dot_general(a, b, (dims, ((), ())), preferred_element_type=f32, precision=precision)
 
 
-def order_of_skew():
-    place = np.zeros((SKEW, SPREAD), np.float32)
-    for z in range(WZ):
-        for r in range(WLAT):
-            for d in range(DIFFS):
-                place[(z * WLAT + r) * DIFFS + d, (DIFFS - 1 - d) * GROUP + z * WLAT + r] = 1.0
-    return place
-
-
-def bias_kernel(table_ref, place_ref, masked_ref, add_ref):
-    skewed = matmul(table_ref[...], place_ref[...], precision=lax.Precision.HIGHEST)
+def order_of_skew(z):
+    row = lax.broadcasted_iota(jnp.int32, (SIDE, 1), 0)
+    lat = sum((row >= k * DIFFS).astype(jnp.int32) for k in range(1, WLAT))
+    diff = row - DIFFS * lat
+    target = (DIFFS - 1 - diff) * GROUP + z * WLAT + lat
+    return (lax.broadcasted_iota(jnp.int32, (SIDE, SPREAD), 1) == target).astype(f32)
+
+
+def to_tiles(tiles_ref, value):
+    for t in range(tiles_ref.shape[0]):
+        part = value[:, t * LANES : (t + 1) * LANES]
+        tiles_ref[t, :, : part.shape[1]] = part
+
+
+def strided_rows(tiles_ref, start, count, stride):
+    tiles = [tiles_ref[t, pl.ds(start, count, stride=stride), :] for t in range(tiles_ref.shape[0])]
+    return jnp.concatenate(tiles, axis=1)
+
+
+def bias_kernel(place_ref, valid_ref, table_ref, add_ref, sides_ref, skewed_ref):
+    for zn in range(WZ):
+        for zm in range(WZ):
+            for ln in range(WLAT):
+                at = ((zn * WZ + zm) * WLAT + ln) * SIDE
+                row = (zn * WLAT + ln) * HEADS
+                for h in range(HEADS):
+                    sides_ref[zm, row + h : row + h + 1, :] = table_ref[h, :, at : at + SIDE]
+    skewed = sum(
+        matmul(sides_ref[z], order_of_skew(z), precision=lax.Precision.HIGHEST) for z in range(WZ)
+    )
+    to_tiles(skewed_ref, skewed)
+    skewed = jnp.concatenate(
+        [strided_rows(skewed_ref, h, GROUP, HEADS) for h in range(HEADS)], axis=0
+    )
+    masked = mask_of_windows(place_ref[0], valid_ref)
     for i in range(WLON):
         shift = (GROUP * (i - WLON + 1)) % SPREAD
         rolled = skewed if shift == 0 else pltpu.roll(skewed, shift, 1)
-        rows = slice(i * GROUP, (i + 1) * GROUP)
-        masked = masked_ref[rows, :]
         for h in range(HEADS):
             add_ref[h * COUNT + i * GROUP : h * COUNT + (i + 1) * GROUP, :] = (
                 rolled[h * GROUP : (h + 1) * GROUP, :COUNT] + masked
             )
 
 
+def mask_of_windows(band, valid_ref):
+    total_rows = valid_ref.shape[0]
+
+    def place_of(shape, axis):
+        position = lax.broadcasted_iota(jnp.int32, shape, axis)
+        group = position - GROUP * sum(
+            (position >= GROUP * k).astype(jnp.int32) for k in range(1, shape[axis] // GROUP)
+        )
+        level = (group >= WLAT).astype(jnp.int32)
+        row_in = group - WLAT * level
+        row = band * WLAT + row_in
+        region = (row >= total_rows - WLAT).astype(jnp.int32) + (
+            row >= total_rows - HALF_LAT
+        ).astype(jnp.int32)
+        return level, row_in, region
+
+    level_n, _, region_n = place_of((GROUP, COUNT), 0)
+    level_m, row_m, region_m = place_of((GROUP, COUNT), 1)
+    key_ok = jnp.zeros((GROUP, COUNT), jnp.int32)
+    for r in range(WLAT):
+        at = lax.rem(band * WLAT + r + HALF_LAT, total_rows)
+        key_ok = jnp.where(row_m == r, valid_ref[at], key_ok)
+    allowed = (level_n == level_m) & (region_n == region_m) & (key_ok == 1)
+    return jnp.where(allowed, f32(0.0), f32(mask_fill))
+
+
 def head_lanes(width, h):
     lane = lax.broadcasted_iota(jnp.int32, (1, width), 1)
     return (lane // 32 == h).astype(f32)
 
 
 def attention_kernel(
+    place_ref,
     x_ref,
     dy_ref,
     gain_ref,
@@ -73,8 +121,12 @@
     add_ref,
     out_ref,
     grad_ref,
+    bottom_ref,
+    mine_ref,
+    other_ref,
+    d_bias_ref,
     parts_ref,
-    d_bias_ref,
+    result_ref,
 ):
     tokens, width = x_ref.shape
     windows = tokens // COUNT
@@ -134,15 +186,18 @@
             per_tile.append((attn, d_q, d_k, d_v))
         whole.append([jnp.concatenate([t[i] for t in per_tile], axis=1) for i in range(4)])
     attn, d_q, d_k, d_v = [jnp.concatenate([t[i] for t in whole], axis=0) for i in range(4)]
-    out_ref[...] = xf + matmul(attn, proj_weight) + proj_bias_ref[...]
+    to_tiles(result_ref, xf + matmul(attn, proj_weight) + proj_bias_ref[...])
+    to_grid(result_ref, out_ref, bottom_ref, 0)
     d_parts = (d_q, d_k, d_v)
     d_normed = sum(matmul(d_parts[i], weights[i], ((1,), (1,))) for i in range(3))
     d_xhat = d_normed * gain
-    grad_ref[...] = dy.astype(f32) + inverse * (
+    d_centered = inverse * (
         d_xhat
         - jnp.mean(d_xhat, axis=-1, keepdims=True)
         - xhat * jnp.mean(d_xhat * xhat, axis=-1, keepdims=True)
     )
+    to_tiles(result_ref, dy.astype(f32) + d_centered)
+    to_grid(result_ref, grad_ref, bottom_ref, 1)
     d_qkv = jnp.concatenate(d_parts, axis=1)
     qkv_weight_grad = matmul(normed, d_qkv, ((0,), (0,)))
     proj_weight_grad = matmul(attn, dy, ((0,), (0,)))
@@ -169,6 +224,22 @@
         shift = GROUP * (WLON - 1 - i)
         skewed = skewed + (part if shift == 0 else pltpu.roll(part, shift, 1))
     pack(parts_ref, matrix, vector, skewed)
+    core = place_ref[1]
+    mine_ref[...] = parts_ref[core]
+    other_ref[...] = parts_ref[1 - core].astype(bf16)
+
+
+def to_grid(result_ref, grid_ref, bottom_ref, kind):
+    levels, rows, cols, width = grid_ref.shape
+    for z in range(levels):
+        for r in range(rows):
+            line = strided_rows(result_ref, z * rows + r, cols, levels * rows)[:, :width]
+            to = (z + WZ // 2) % levels
+            if r < rows - HALF_LAT:
+                grid_ref[to, r + HALF_LAT] = line
+            else:
+                bottom_ref[kind, to, r - rows + HALF_LAT] = line.astype(bf16)
+                grid_ref[to, r - rows + HALF_LAT] = jnp.zeros_like(line)
 
 
 def table_slots(pieces, pairs):
@@ -182,37 +253,77 @@
 
 
 def pack(parts_ref, matrix, vector, skewed):
-    pieces = parts_ref.shape[0]
+    cores, half = parts_ref.shape[:2]
+    pieces = cores * half
     rows = matrix.shape[0] // pieces
     for d in range(pieces):
-        parts_ref[d, 0:rows, :] = matrix[d * rows : (d + 1) * rows, :]
-        parts_ref[d, rows:8, :] = jnp.zeros((8 - rows, matrix.shape[1]), f32)
+        parts_ref[d % cores, d // cores, 0:rows, :] = matrix[d * rows : (d + 1) * rows, :]
+        parts_ref[d % cores, d // cores, rows:8, :] = jnp.zeros((8 - rows, matrix.shape[1]), f32)
     for p, (d, at, d2, at2) in enumerate(table_slots(pieces, skewed.shape[0] // 2)):
         pair = slice(2 * p, 2 * p + 2)
-        parts_ref[d, rows : rows + 2, at : at + 2 * LANES] = skewed[pair, : 2 * LANES]
-        parts_ref[d2, rows : rows + 2, at2 : at2 + LANES] = skewed[pair, 2 * LANES :]
+        parts_ref[d % cores, d // cores, rows : rows + 2, at : at + 2 * LANES] = skewed[pair, : 2 * LANES]
+        parts_ref[d2 % cores, d2 // cores, rows : rows + 2, at2 : at2 + LANES] = skewed[pair, 2 * LANES :]
     for d in range(vector.shape[1] // LANES):
-        parts_ref[d, rows : rows + 1, 5 * LANES :] = vector[:, d * LANES : (d + 1) * LANES]
-
-
-def unpack_kernel(norm_by, full_ref, place_ref, qkv_ref, proj_ref, table_ref, gain_ref, shift_ref, qkv_bias_ref, proj_bias_ref, wide_ref, skewed_ref):
-    pieces = full_ref.shape[0]
+        parts_ref[d % cores, d // cores, rows : rows + 1, 5 * LANES :] = vector[
+            :, d * LANES : (d + 1) * LANES
+        ]
+
+
+def unpack_kernel(
+    norm_by,
+    place_ref,
+    mine_ref,
+    other_ref,
+    qkv_ref,
+    proj_ref,
+    table_ref,
+    gain_ref,
+    shift_ref,
+    qkv_bias_ref,
+    proj_bias_ref,
+    wide_ref,
+    skewed_ref,
+):
+    core = place_ref[1]
+    wide_ref[core] = mine_ref[...].astype(f32)
+    wide_ref[1 - core] = other_ref[...].astype(f32)
+    cores, half = wide_ref.shape[:2]
+    pieces = cores * half
     width, wide = qkv_ref.shape
     rows = width // pieces
-    wide_ref[...] = full_ref[...].astype(f32)
     for d in range(pieces):
-        piece = wide_ref[d, 0:rows, :] * norm_by
+        piece = wide_ref[d % cores, d // cores, 0:rows, :] * norm_by
         qkv_ref[d * rows : (d + 1) * rows, :] = piece[:, :wide]
         proj_ref[d * rows : (d + 1) * rows, :] = piece[:, wide:]
-    for p, (d, at, d2, at2) in enumerate(table_slots(pieces, skewed_ref.shape[0] // 2)):
-        skewed_ref[2 * p : 2 * p + 2, : 2 * LANES] = wide_ref[d, rows : rows + 2, at : at + 2 * LANES]
-        skewed_ref[2 * p : 2 * p + 2, 2 * LANES :] = wide_ref[d2, rows : rows + 2, at2 : at2 + LANES]
-    table_ref[...] = matmul(
-        skewed_ref[...] * bias_factor, place_ref[...], ((1,), (1,)), lax.Precision.HIGHEST
-    )
+    for p, (d, at, d2, at2) in enumerate(table_slots(pieces, skewed_ref.shape[1] // 2)):
+        for t in range(2):
+            lanes = slice(at + t * LANES, at + (t + 1) * LANES)
+            skewed_ref[t, 2 * p : 2 * p + 2, :] = wide_ref[
+                d % cores, d // cores, rows : rows + 2, lanes
+            ]
+        skewed_ref[2, 2 * p : 2 * p + 2, :] = wide_ref[
+            d2 % cores, d2 // cores, rows : rows + 2, at2 : at2 + LANES
+        ]
+    skewed = bias_factor * jnp.concatenate(
+        [strided_rows(skewed_ref, a, HEADS, GROUP) for a in range(GROUP)], axis=0
+    )
+    sides = [
+        matmul(skewed, order_of_skew(z), ((1,), (1,)), lax.Precision.HIGHEST) for z in range(WZ)
+    ]
+    table = jnp.concatenate(
+        [
+            sides[zm][(zn * WLAT + ln) * HEADS : (zn * WLAT + ln + 1) * HEADS]
+            for zn in range(WZ)
+            for zm in range(WZ)
+            for ln in range(WLAT)
+        ],
+        axis=1,
+    )
+    for h in range(HEADS):
+        table_ref[h] = table[h : h + 1]
     count = (3 * width + wide) // LANES
     vector = jnp.concatenate(
-        [wide_ref[d, rows : rows + 1, 5 * LANES :] for d in range(count)], axis=1
+        [wide_ref[d % cores, d // cores, rows : rows + 1, 5 * LANES :] for d in range(count)], axis=1
     )
     vector = vector * norm_by
     gain_ref[...] = vector[:, :width]
@@ -224,52 +335,39 @@
 VMEM_LIMIT = 48 * 1024 * 1024
 
 
-def call(kernel, out_shape, name, scratch=()):
+def call(kernel, out_shape, name, scalars, arrays, scratch=()):
+    smem = pl.BlockSpec(memory_space=pltpu.SMEM)
+    vmem = pl.BlockSpec(memory_space=pltpu.VMEM)
     return pl.pallas_call(
         kernel,
         out_shape=out_shape,
+        in_specs=[smem] * len(scalars) + [vmem] * len(arrays),
         scratch_shapes=scratch,
         compiler_params=pltpu.CompilerParams(vmem_limit_bytes=VMEM_LIMIT),
         name=name,
-    )
+    )(*scalars, *arrays)
 
 
 def struct(shape, dtype=f32):
     return jax.ShapeDtypeStruct(shape, dtype)
 
 
-def spread_to_all(piece, axis):
-    count = lax.axis_size(axis)
-    return lax.all_to_all(jnp.broadcast_to(piece[None], (count,) + piece.shape), axis, 0, 0)
-
-
-def reduce_all(parts, rows):
-    by_lon = jnp.sum(lax.all_to_all(parts.astype(bf16), "lon", 0, 0).astype(f32), axis=0)
-    by_lat = jnp.sum(spread_to_all(by_lon.astype(bf16), "lat").astype(f32), axis=0)
-    row = lax.broadcasted_iota(jnp.int32, by_lat.shape, 0)
-    column = lax.broadcasted_iota(jnp.int32, by_lat.shape, 1)
-    is_table = (row >= rows) & (column < 5 * LANES)
-    done = jnp.where(is_table, by_lon, by_lat).astype(bf16)
-    return spread_to_all(done, "lon")
-
-
-def mask_of_windows(lat_valid, band, levels):
-    total_rows = lat_valid.shape[0]
-    position = jnp.arange(COUNT, dtype=jnp.int32)
-    level = position % GROUP // WLAT
-    row_in = position % WLAT
-    level_region = (level >= levels - WZ).astype(jnp.int32) + (level >= levels - WZ // 2).astype(jnp.int32)
-    row = band * WLAT + row_in
-    row_region = (row >= total_rows - WLAT).astype(jnp.int32) + (row >= total_rows - HALF_LAT).astype(jnp.int32)
-    rolled = jnp.roll(lat_valid, -HALF_LAT)
-    valid = lax.dynamic_slice_in_dim(rolled, band * WLAT, WLAT)
-    key_ok = jnp.tile(valid, WZ * WLON)
-    allowed = (
-        (level_region[:, None] == level_region[None, :])
-        & (row_region[:, None] == row_region[None, :])
-        & (key_ok[None, :] == 1)
-    )
-    return jnp.where(allowed, f32(0.0), f32(mask_fill))
+CORES = 2
+
+
+def swap_cores(value):
+    count = lax.axis_size("lon")
+    return lax.ppermute(value, "lon", [(i, i ^ 1) for i in range(count)])
+
+
+def same_core():
+    count = lax.axis_size("lon")
+    return [list(range(c, count, CORES)) for c in range(CORES)]
+
+
+def spread_to_all(piece, axis, count, groups=None):
+    wide = jnp.broadcast_to(piece[None], (count,) + piece.shape)
+    return lax.all_to_all(wide, axis, 0, 0, axis_index_groups=groups)
 
 
 def to_neighbour(value, axes, steps):
@@ -303,6 +401,7 @@
     lat_count = lax.axis_size("lat")
     lon_count = lax.axis_size("lon")
     total = levels * rows * cols
+    place = jnp.stack([lax.axis_index("lat"), lax.axis_index("lon") % CORES]).astype(jnp.int32)
     lat_halo = jnp.stack([a[:, :HALF_LAT, HALF_LON:] for a in (tokens, cotangent)])
     lon_halo = jnp.stack([a[:, HALF_LAT:, :HALF_LON] for a in (tokens, cotangent)])
     corner = jnp.stack([a[:, :HALF_LAT, :HALF_LON] for a in (tokens, cotangent)])
@@ -310,11 +409,13 @@
     corner = to_neighbour(corner, ("lat", "lon"), (-1, -1))
     lon_halo = to_neighbour(lon_halo, ("lon",), (-1,))
 
-    place = jnp.asarray(order_of_skew())
-    table = earth_bias.reshape(HEADS, WZ, WZ, WLAT, WLAT * DIFFS).transpose(0, 1, 3, 2, 4)
-    masked = mask_of_windows(lat_valid, lax.axis_index("lat"), levels)
-    add = call(bias_kernel, struct((HEADS * COUNT, COUNT)), "bias")(
-        table.reshape(HEADS * GROUP, SKEW), place, masked
+    add = call(
+        bias_kernel,
+        struct((HEADS * COUNT, COUNT)),
+        "bias",
+        [place, lat_valid],
+        [earth_bias.reshape(HEADS, 1, -1)],
+        [pltpu.VMEM((WZ, HEADS * GROUP, SIDE), f32), pltpu.VMEM((SPREAD // LANES, HEADS * GROUP, LANES), f32)],
     )
 
     def windows_of(kind, array):
@@ -323,35 +424,63 @@
         moved = jnp.roll(jnp.concatenate([own, side], axis=2), -(WZ // 2), axis=0)
         return moved.transpose(2, 0, 1, 3).reshape(total, width)
 
-    out, grad, parts = call(
+    half = lon_count // CORES
+    across = wide + width
+    out, grad, bottom, mine, other = call(
         attention_kernel,
-        (struct((total, width)), struct((total, width)), struct((lon_count, 8, wide + width))),
+        (
+            struct(tokens.shape),
+            struct(tokens.shape),
+            struct((2, levels, HALF_LAT, cols, width), bf16),
+            struct((half, 8, across)),
+            struct((half, 8, across), bf16),
+        ),
         "attention",
-        [pltpu.VMEM((HEADS * COUNT, COUNT), f32)],
-    )(
-        windows_of(0, tokens),
-        windows_of(1, cotangent),
-        norm_gain_vector[None],
-        norm_bias_vector[None],
-        qkv_weight,
-        qkv_bias[None],
-        proj_weight,
-        proj_bias[None],
-        add,
-    )
-    full = reduce_all(parts, width // lon_count)
-
-    both = jnp.stack([out, grad]).reshape(2, cols, levels, rows, width)
-    both = jnp.roll(both, WZ // 2, axis=2).transpose(0, 2, 3, 1, 4)
-    half = both.astype(bf16)
-    inner = rows - HALF_LAT
+        [place],
+        [
+            windows_of(0, tokens),
+            windows_of(1, cotangent),
+            norm_gain_vector[None],
+            norm_bias_vector[None],
+            qkv_weight,
+            qkv_bias[None],
+            proj_weight,
+            proj_bias[None],
+            add,
+        ],
+        [
+            pltpu.VMEM((HEADS * COUNT, COUNT), f32),
+            pltpu.VMEM((CORES, half, 8, across), f32),
+            pltpu.VMEM((pl.cdiv(width, LANES), total, LANES), f32),
+        ],
+    )
+
+    pair = (mine + swap_cores(other).astype(f32)).astype(bf16)
+    by_lon = jnp.sum(lax.all_to_all(pair, "lon", 0, 0, axis_index_groups=same_core()).astype(f32), axis=0)
+    top = to_neighbour(bottom, ("lat",), (1,))
+    by_lon, top = lax.optimization_barrier((by_lon, top))
+    by_lat = spread_to_all(by_lon.astype(bf16), "lat", lat_count)
     edge = cols - HALF_LON
-    lat_back = to_neighbour(half[:, :, inner:, :edge], ("lat",), (1,))
-    corner_back = to_neighbour(half[:, :, inner:, edge:], ("lat", "lon"), (1, 1))
-    lon_back = to_neighbour(half[:, :, :inner, edge:], ("lon",), (1,))
-    top = jnp.concatenate([corner_back, lat_back], axis=3).astype(f32)
-    bottom = jnp.concatenate([lon_back.astype(f32), both[:, :, :inner, :edge]], axis=3)
-    back = jnp.concatenate([top, bottom], axis=2)
+    right = jnp.concatenate(
+        [top[:, :, :, edge:], jnp.stack([a[:, HALF_LAT:, edge:] for a in (out, grad)]).astype(bf16)],
+        axis=2,
+    )
+    left = to_neighbour(right, ("lon",), (1,))
+    by_lat, left = lax.optimization_barrier((by_lat, left))
+    by_lat = jnp.sum(by_lat.astype(f32), axis=0)
+    row = lax.broadcasted_iota(jnp.int32, by_lat.shape, 0)
+    column = lax.broadcasted_iota(jnp.int32, by_lat.shape, 1)
+    is_table = (row >= width // lon_count) & (column < 5 * LANES)
+    done = jnp.where(is_table, by_lon, by_lat).astype(bf16)
+    mine = spread_to_all(done, "lon", half, same_core())
+    other = swap_cores(mine)
+
+    def owned(kind, array):
+        upper = jnp.concatenate([left[kind, :, :HALF_LAT], top[kind, :, :, :edge]], axis=2)
+        lower = jnp.concatenate(
+            [left[kind, :, HALF_LAT:].astype(f32), array[:, HALF_LAT:, :edge]], axis=2
+        )
+        return jnp.concatenate([upper.astype(f32), lower], axis=1)
 
     norm_by = 1.0 / math.sqrt(total * lat_count * lon_count)
 
@@ -363,19 +492,20 @@
         (
             struct((width, wide)),
             struct((width, width)),
-            struct((HEADS * GROUP, SKEW)),
+            struct((HEADS, 1, earth_bias.shape[-1])),
             struct((1, width)),
             struct((1, width)),
             struct((1, wide)),
             struct((1, width)),
         ),
         "unpack",
-        [pltpu.VMEM((lon_count, 8, wide + width), f32), pltpu.VMEM((HEADS * GROUP, SPREAD), f32)],
-    )(full, place)
-    table = table.reshape(HEADS, WZ, WLAT, WZ, WLAT * DIFFS).transpose(0, 1, 3, 2, 4)
+        [place],
+        [mine, other],
+        [pltpu.VMEM((CORES, half, 8, across), f32), pltpu.VMEM((SPREAD // LANES, HEADS * GROUP, LANES), f32)],
+    )
     return (
-        back[0],
-        back[1],
+        owned(0, out),
+        owned(1, grad),
         gain[0],
         shift[0],
         qkv_weight_grad,

time: 107 us -> 100 us (0.935)
  waiting for transfers between devices: 35.7 us -> 31.2 us
  local copies, waits for them, and re-layouts: 9.37 us -> 5.8 us
  Pallas kernels: 6.07 us -> 8.18 us
  starting transfers between devices: 51.8 us -> 50.1 us
    ppermute x2 -> x1, starting transfers between devices: 17.4 us -> 5.88 us  [to_neighbour(): return lax.ppermute(value, axes, pairs)]
    ppermute x2 -> x1, waiting for transfers between devices: 11.5 us -> 0.01 us  [to_neighbour(): return lax.ppermute(value, axes, pairs)]
    ppermute x0 -> x2, starting transfers between devices: none -> 8.3 us  [swap_cores(): return lax.ppermute(value, 'lon', [(i, i ^ 1) for i in range(count)])]
    ppermute x4, starting transfers between devices: 13.5 us -> 20.5 us  [to_neighbour(): lax.ppermute(value, axes[0], [(i, (i + steps[0]) % n) for i in range(n)])]
    ppermute x4, waiting for transfers between devices: 1.07 us -> 7.96 us  [to_neighbour(): lax.ppermute(value, axes[0], [(i, (i + steps[0]) % n) for i in range(n)])]
    all_to_all x3, starting transfers between devices: 20.9 us -> 15.4 us  [the longest x2 9.2 us: spread_to_all(): return lax.all_to_all(wide, axis, 0, 0, axis_index_groups=groups)]
    unnamed x25 -> x16, local copies, waits for them, and re-layouts: 4.65 us -> 2.16 us
    pallas_call x3, Pallas kernels: 6.07 us -> 8.18 us  [call(): pl.pallas_call(kernel, out_shape=out_shape, in_specs=[smem] * len(scalars...]
  transfers between devices with their start and end apart: 9 -> 10, of which waited for: 4 -> 7; matrix products, arithmetic and copies ran while one was open for 4% -> 3% of each run, Pallas kernels for 1% -> 2%
where the time goes in v3:
time: 100 us; the launch traced here: 99.7 us
  starting transfers between devices  50.1 us (50%)
  waiting for transfers between devices  31.2 us (31%)
  Pallas kernels  8.18 us (8%)
  local copies, waits for them, and re-layouts  5.8 us (6%)
  other arithmetic  3.38 us (3%)
  between operations  1.04 us (1%)
    ppermute x4, starting transfers between devices, to_neighbour(): lax.ppermute(value, axes[0], [(i, (i + steps[0]) % n) for i in range(n)])  20.5 us
    all_to_all x2, waiting for transfers between devices, spread_to_all(): return lax.all_to_all(wide, axis, 0, 0, axis_index_groups=groups)  13.7 us
    all_to_all x2, starting transfers between devices, spread_to_all(): return lax.all_to_all(wide, axis, 0, 0, axis_index_groups=groups)  9.2 us
    ppermute x2, starting transfers between devices, swap_cores(): return lax.ppermute(value, 'lon', [(i, i ^ 1) for i in range(count)])  8.3 us
    pallas_call x3, Pallas kernels, call(): pl.pallas_call(kernel, out_shape=out_shape, in_specs=[smem] * len(scalars...  8.18 us
    all_to_all x1, waiting for transfers between devices, local(): lax.all_to_all(pair, 'lon', 0, 0, axis_index_groups=same_core()).astype(f32)  7.97 us
    ppermute x4, waiting for transfers between devices, to_neighbour(): lax.ppermute(value, axes[0], [(i, (i + steps[0]) % n) for i in range(n)])  7.96 us
    all_to_all x1, starting transfers between devices, local(): lax.all_to_all(pair, 'lon', 0, 0, axis_index_groups=same_core()).astype(f32)  6.24 us
  transfers between devices with their start and end apart: 10, of which 7 were waited for; matrix products, arithmetic and copies ran while one was open for 3% of the time, Pallas kernels for 2%

profile of v3, /device:TPU:1, one launch (start us, length us, event | category | flops | bytes accessed | tf_op | source)
XLA Modules:
  0.0 99.7 jit_solution(14240811267465533629)
XLA Ops:
  0.6 1.1 %fusion.3 = (bf16[2,3,18,192]{3,2,1,0:T(8,128)(2,1)S(1)}, bf16[1,2,3,18,192]{4,3,2,1,0:T(8,128)(2,1)S(1)}, bf16[1,2,3,18,192]{4,3,2,1,0:T(8,128)(2,1)S(1)}, bf16[2,3,18,192]{3,2,1,0:T(8,128)(2,1)S(1)}) fusion(bf16[2,6,24,192]{3,2,1,0:T(8,128)(2,1)} %param.11, bf16[2,6,24,192]{3,2,1,0:T(8,128)(2,1)} %param.10), kind=kLoop, calls=%fused_computation.42 | loop fusion | bytes 331776 | tf_op jit(solution)/shard_map/slice | solution.py:422
  1.8 13.7 %collective-permute-start = (bf16[2,2,3,18,192]{4,3,2,1,0:T(8,128)(2,1)S(1)}, bf16[2,2,3,18,192]{4,3,2,1,0:T(8,128)(2,1)S(1)}, u32[]{:S(2)}, u32[]{:S(2)}) collective-permute-start(bf16[2,2,3,18,192]{4,3,2,1,0:T(8,128)(2,1)S(1)} %pad_maximum_fusion), channel_id=1, source_target_pairs={{0,480},{32,0},{64,32},{96,64},{128,96},{160,128},{192,160},{224,1... | collective-permute-start | bytes 248840 | tf_op jit(solution)/shard_map/ppermute | solution.py:377
  15.5 0.8 slice_bitcast_fusion.14
  16.3 3.0 %collective-permute-start.1 = (bf16[2,2,3,6,192]{4,3,2,1,0:T(8,128)(2,1)S(1)}, bf16[2,2,3,6,192]{4,3,2,1,0:T(8,128)(2,1)S(1)}, u32[]{:S(2)}, u32[]{:S(2)}) collective-permute-start(bf16[2,2,3,6,192]{4,3,2,1,0:T(8,128)(2,1)S(1)} %pad_maximum_fusion.1), channel_id=1, source_target_pairs={{0,31},{1,0},{2,1},{3,2},{4,3},{5,4},{6,5},{7,6},{8,7},{9,8},{10,9... | collective-permute-start | bytes 82952 | tf_op jit(solution)/shard_map/ppermute | solution.py:377
  19.3 5.9 %collective-permute-start.2 = (bf16[2,2,3,6,192]{4,3,2,1,0:T(8,128)(2,1)S(1)}, bf16[2,2,3,6,192]{4,3,2,1,0:T(8,128)(2,1)S(1)}, u32[]{:S(2)}, u32[]{:S(2)}) collective-permute-start(bf16[2,2,3,6,192]{4,3,2,1,0:T(8,128)(2,1)S(1)} %pad_maximum_fusion.2), channel_id=1, source_target_pairs={{0,511},{1,480},{2,481},{3,482},{4,483},{5,484},{6,485},{7,486},{8... | collective-permute-start | bytes 82952 | tf_op jit(solution)/shard_map/ppermute | solution.py:384
  25.3 0.6 copy-done.7
  25.9 0.7 copy-done.6
  26.6 1.5 %bias.1.add_ref = f32[864,144]{1,0:T(8,128)S(1)} custom-call(s32[2]{0:T(128)S(1)} %pad_add_fusion.place_ref.refs_0_, s32[96]{0:T(128)S(1)} %copy-done.6, f32[6,1,3312]{2,1,0:T(1,128)S(1)} %bitcast.58), custom_call_target="tpu_custom_call" | custom-call | tf_op jit(solution)/shard_map/bias/pallas_call | solution.py:341
  28.3 0.1 reshape.37.dy_ref
  28.7 0.8 copy-done
  29.6 4.4 %attention.1 = (f32[2,6,24,192]{3,2,1,0:T(8,128)S(1)}, f32[2,6,24,192]{3,2,1,0:T(8,128)S(1)}, bf16[2,2,3,24,192]{4,3,2,1,0:T(8,128)(2,1)S(1)}, f32[16,8,768]{2,1,0:T(8,128)S(1)}, bf16[16,8,768]{2,1,0:T(8,128)(2,1)S(1)}) custom-call(s32[2]{0:T(128)S(1)} %pad_add_fusion.place_ref.refs_0_, bf16[288,192]{1,0:T(8,128)(2,1)S(1)} %reshape.36.x_ref, ...), custom_call_target="tpu_custom_call" | custom-call | tf_op jit(solution)/shard_map/attention/pallas_call | solution.py:341
  34.0 2.1 %collective-permute-start.3 = (bf16[16,8,768]{2,1,0:T(8,128)(2,1)S(1)}, bf16[16,8,768]{2,1,0:T(8,128)(2,1)S(1)}, u32[]{:S(2)}, u32[]{:S(2)}) collective-permute-start(bf16[16,8,768]{2,1,0:T(8,128)(2,1)S(1)} %get-tuple-element.26), channel_id=1, source_target_pairs={{0,1},{1,0},{2,3},{3,2},{4,5},{5,4},{6,7},{7,6},{8,9},{9,8},{10,11... | collective-permute-start | bytes 589832 | tf_op jit(solution)/shard_map/ppermute | solution.py:360
  36.1 1.3 %collective-permute-done.3 = bf16[16,8,768]{2,1,0:T(8,128)(2,1)S(1)} collective-permute-done((bf16[16,8,768]{2,1,0:T(8,128)(2,1)S(1)}, bf16[16,8,768]{2,1,0:T(8,128)(2,1)S(1)}, u32[]{:S(2)}, u32[]{:S(2)}) %collective-permute-start.3) | collective-permute-done | bytes 196640 | tf_op jit(solution)/shard_map/ppermute | solution.py:360
  37.4 0.7 add_convert_fusion
  38.1 6.2 %all-to-all-start = ((bf16[16,8,768]{2,1,0:T(8,128)(2,1)}), bf16[16,8,768]{2,1,0:T(8,128)(2,1)S(1)}, u32[]{:S(2)}, u32[]{:S(2)}) async-start(bf16[16,8,768]{2,1,0:T(8,128)(2,1)} %add_convert_fusion), calls=%async_computation | async-start | bytes 393216 | tf_op jit(solution)/shard_map/all_to_all | solution.py:459
  44.4 1.9 %collective-permute-start.4 = (bf16[2,2,3,24,192]{4,3,2,1,0:T(8,128)(2,1)S(1)}, bf16[2,2,3,24,192]{4,3,2,1,0:T(8,128)(2,1)S(1)}, u32[]{:S(2)}, u32[]{:S(2)}) collective-permute-start(bf16[2,2,3,24,192]{4,3,2,1,0:T(8,128)(2,1)S(1)} %get-tuple-element.27), channel_id=1, source_target_pairs={{0,32},{32,64},{64,96},{96,128},{128,160},{160,192},{192,224},{224... | collective-permute-start | bytes 331784 | tf_op jit(solution)/shard_map/ppermute | solution.py:377
  46.3 8.0 %all-to-all-done = bf16[16,8,768]{2,1,0:T(8,128)(2,1)S(1)} async-done(((bf16[16,8,768]{2,1,0:T(8,128)(2,1)}), bf16[16,8,768]{2,1,0:T(8,128)(2,1)S(1)}, u32[]{:S(2)}, u32[]{:S(2)}) %all-to-all-start) | async-done | bytes 196640 | tf_op jit(solution)/shard_map/all_to_all | solution.py:459
  54.3 5.7 %collective-permute-done.4 = bf16[2,2,3,24,192]{4,3,2,1,0:T(8,128)(2,1)S(1)} collective-permute-done((bf16[2,2,3,24,192]{4,3,2,1,0:T(8,128)(2,1)S(1)}, bf16[2,2,3,24,192]{4,3,2,1,0:T(8,128)(2,1)S(1)}, u32[]{:S(2)}, u32[]{:S(2)}) %collective-permute-start.4) | collective-permute-done | bytes 110624 | tf_op jit(solution)/shard_map/ppermute | solution.py:377
  60.0 0.7 broadcast_in_dim.28
  60.7 3.5 %all-to-all-start.1 = ((bf16[16,8,768]{2,1,0:T(8,128)(2,1)}), bf16[16,8,768]{2,1,0:T(8,128)(2,1)S(1)}, u32[]{:S(2)}, u32[]{:S(2)}) async-start(bf16[16,8,768]{2,1,0:T(8,128)(2,1)} %broadcast_in_dim.28), calls=%async_computation.1 | async-start | bytes 393216 | tf_op jit(solution)/shard_map/all_to_all | solution.py:370
  64.4 1.9 %collective-permute-start.5 = (bf16[2,2,6,6,192]{4,3,2,1,0:T(8,128)(2,1)S(1)}, bf16[2,2,6,6,192]{4,3,2,1,0:T(8,128)(2,1)S(1)}, u32[]{:S(2)}, u32[]{:S(2)}) collective-permute-start(bf16[2,2,6,6,192]{4,3,2,1,0:T(8,128)(2,1)S(1)} %maximum_maximum_fusion.4), channel_id=1, source_target_pairs={{0,1},{1,2},{2,3},{3,4},{4,5},{5,6},{6,7},{7,8},{8,9},{9,10},{10,1... | collective-permute-start | bytes 165896 | tf_op jit(solution)/shard_map/ppermute | solution.py:377
  66.3 2.2 %collective-permute-done.5 = bf16[2,2,6,6,192]{4,3,2,1,0:T(8,128)(2,1)S(1)} collective-permute-done((bf16[2,2,6,6,192]{4,3,2,1,0:T(8,128)(2,1)S(1)}, bf16[2,2,6,6,192]{4,3,2,1,0:T(8,128)(2,1)S(1)}, u32[]{:S(2)}, u32[]{:S(2)}) %collective-permute-start.5) | collective-permute-done | bytes 55328 | tf_op jit(solution)/shard_map/ppermute | solution.py:377
  68.5 5.4 %all-to-all-done.1 = bf16[16,8,768]{2,1,0:T(8,128)(2,1)S(1)} async-done(((bf16[16,8,768]{2,1,0:T(8,128)(2,1)}), bf16[16,8,768]{2,1,0:T(8,128)(2,1)S(1)}, u32[]{:S(2)}, u32[]{:S(2)}) %all-to-all-start.1) | async-done | bytes 196640 | tf_op jit(solution)/shard_map/all_to_all | solution.py:370
  74.0 0.7 broadcast_in_dim.29
  74.7 5.7 %all-to-all-start.2 = ((bf16[16,8,768]{2,1,0:T(8,128)(2,1)}), bf16[16,8,768]{2,1,0:T(8,128)(2,1)S(1)}, u32[]{:S(2)}, u32[]{:S(2)}) async-start(bf16[16,8,768]{2,1,0:T(8,128)(2,1)} %broadcast_in_dim.29), calls=%async_computation.2 | async-start | bytes 393216 | tf_op jit(solution)/shard_map/all_to_all | solution.py:370
  80.5 0.7 maximum_maximum_fusion.1
  81.2 8.3 %all-to-all-done.2.refs_1_ = bf16[16,8,768]{2,1,0:T(8,128)(2,1)S(1)} async-done(((bf16[16,8,768]{2,1,0:T(8,128)(2,1)}), bf16[16,8,768]{2,1,0:T(8,128)(2,1)S(1)}, u32[]{:S(2)}, u32[]{:S(2)}) %all-to-all-start.2) | async-done | bytes 196640 | tf_op jit(solution)/shard_map/all_to_all | solution.py:370
  89.5 6.2 %collective-permute-start.6 = (bf16[16,8,768]{2,1,0:T(8,128)(2,1)S(1)}, bf16[16,8,768]{2,1,0:T(8,128)(2,1)S(1)}, u32[]{:S(2)}, u32[]{:S(2)}) collective-permute-start(bf16[16,8,768]{2,1,0:T(8,128)(2,1)S(1)} %all-to-all-done.2.refs_1_), channel_id=1, source_target_pairs={{0,1},{1,0},{2,3},{3,2},{4,5},{5,4},{6,7},{7,6},{8,9},{9,8},{10,11... | collective-permute-start | bytes 589832 | tf_op jit(solution)/shard_map/ppermute | solution.py:360
  95.8 0.7 maximum_maximum_fusion
  96.6 0.3 collective-permute-done.6.refs_2_
  96.8 2.3 %unpack.1 = (f32[192,576]{1,0:T(8,128)}, f32[192,192]{1,0:T(8,128)}, f32[6,1,3312]{2,1,0:T(1,128)}, f32[1,192]{1,0:T(1,128)}, f32[1,192]{1,0:T(1,128)}, /*index=5*/f32[1,576]{1,0:T(1,128)S(1)}, f32[1,192]{1,0:T(1,128)}) custom-call(s32[2]{0:T(128)S(1)} %pad_add_fusion.place_ref.refs_0_, bf16[16,8,768]{2,1,0:T(8,128)(2,1)S(1)} %all-to-all-done.2.refs_1_, ...), custom_call_target="tpu_custom_call" | custom-call | tf_op jit(solution)/shard_map/unpack/pallas_call | solution.py:341
  99.1 0.6 reduce
  (48 shorter events, 1.0 us)
Async XLA Ops:
  1.8 26.4 %collective-permute-start = (bf16[2,2,3,18,192]{4,3,2,1,0:T(8,128)(2,1)S(1)}, bf16[2,2,3,18,192]{4,3,2,1,0:T(8,128)(2,1)S(1)}, u32[]{:S(2)}, u32[]{:S(2)}) collective-permute-start(bf16[2,2,3,18,192]{4,3,2,1,0:T(8,128)(2,1)S(1)} %pad_maximum_fusion), channel_id=1, source_target_pairs={{0,480},{32,0},{64,32},{96,64},{128,96},{160,128},{192,160},{224,1... | collective-permute-start | bytes 248840 | tf_op jit(solution)/shard_map/ppermute | solution.py:377
  16.3 9.6 %copy-start.2 = (f32[1,1,6,3312]{3,1,2,0:T(1,128)S(1)}, f32[1,1,6,3312]{3,1,2,0:T(1,128)}, u32[]{:S(2)}) copy-start(f32[1,1,6,3312]{3,1,2,0:T(1,128)} %param.18) | copy-start | bytes 238468
  16.3 11.8 %collective-permute-start.1 = (bf16[2,2,3,6,192]{4,3,2,1,0:T(8,128)(2,1)S(1)}, bf16[2,2,3,6,192]{4,3,2,1,0:T(8,128)(2,1)S(1)}, u32[]{:S(2)}, u32[]{:S(2)}) collective-permute-start(bf16[2,2,3,6,192]{4,3,2,1,0:T(8,128)(2,1)S(1)} %pad_maximum_fusion.1), channel_id=1, source_target_pairs={{0,31},{1,0},{2,1},{3,2},{4,3},{5,4},{6,5},{7,6},{8,7},{9,8},{10,9... | collective-permute-start | bytes 82952 | tf_op jit(solution)/shard_map/ppermute | solution.py:377
  19.3 8.8 %collective-permute-start.2 = (bf16[2,2,3,6,192]{4,3,2,1,0:T(8,128)(2,1)S(1)}, bf16[2,2,3,6,192]{4,3,2,1,0:T(8,128)(2,1)S(1)}, u32[]{:S(2)}, u32[]{:S(2)}) collective-permute-start(bf16[2,2,3,6,192]{4,3,2,1,0:T(8,128)(2,1)S(1)} %pad_maximum_fusion.2), channel_id=1, source_target_pairs={{0,511},{1,480},{2,481},{3,482},{4,483},{5,484},{6,485},{7,486},{8... | collective-permute-start | bytes 82952 | tf_op jit(solution)/shard_map/ppermute | solution.py:384
  25.2 0.7 copy-start.7
  25.9 0.7 copy-start.6
  28.6 0.9 copy-start
  28.6 1.0 %copy-start.1 = (bf16[192,192]{1,0:T(8,128)(2,1)S(1)}, bf16[192,192]{1,0:T(8,128)(2,1)}, u32[]{:S(2)}) copy-start(bf16[192,192]{1,0:T(8,128)(2,1)} %proj_weight_ref.1) | copy-start | bytes 221188
  28.6 1.0 %copy-start.4 = (f32[192]{0:T(256)S(1)}, f32[192]{0:T(256)}, u32[]{:S(2)}) copy-start(f32[192]{0:T(256)} %param.13) | copy-start | bytes 2308
  28.6 1.0 copy-start.5
  28.7 0.9 copy-start.3
  34.0 3.3 %collective-permute-start.3 = (bf16[16,8,768]{2,1,0:T(8,128)(2,1)S(1)}, bf16[16,8,768]{2,1,0:T(8,128)(2,1)S(1)}, u32[]{:S(2)}, u32[]{:S(2)}) collective-permute-start(bf16[16,8,768]{2,1,0:T(8,128)(2,1)S(1)} %get-tuple-element.26), channel_id=1, source_target_pairs={{0,1},{1,0},{2,3},{3,2},{4,5},{5,4},{6,7},{7,6},{8,9},{9,8},{10,11... | collective-permute-start | bytes 589832 | tf_op jit(solution)/shard_map/ppermute | solution.py:360
  38.1 16.2 %all-to-all-start = ((bf16[16,8,768]{2,1,0:T(8,128)(2,1)}), bf16[16,8,768]{2,1,0:T(8,128)(2,1)S(1)}, u32[]{:S(2)}, u32[]{:S(2)}) async-start(bf16[16,8,768]{2,1,0:T(8,128)(2,1)} %add_convert_fusion), calls=%async_computation | async-start | bytes 393216 | tf_op jit(solution)/shard_map/all_to_all | solution.py:459
  44.4 15.7 %collective-permute-start.4 = (bf16[2,2,3,24,192]{4,3,2,1,0:T(8,128)(2,1)S(1)}, bf16[2,2,3,24,192]{4,3,2,1,0:T(8,128)(2,1)S(1)}, u32[]{:S(2)}, u32[]{:S(2)}) collective-permute-start(bf16[2,2,3,24,192]{4,3,2,1,0:T(8,128)(2,1)S(1)} %get-tuple-element.27), channel_id=1, source_target_pairs={{0,32},{32,64},{64,96},{96,128},{128,160},{160,192},{192,224},{224... | collective-permute-start | bytes 331784 | tf_op jit(solution)/shard_map/ppermute | solution.py:377
  60.7 13.2 %all-to-all-start.1 = ((bf16[16,8,768]{2,1,0:T(8,128)(2,1)}), bf16[16,8,768]{2,1,0:T(8,128)(2,1)S(1)}, u32[]{:S(2)}, u32[]{:S(2)}) async-start(bf16[16,8,768]{2,1,0:T(8,128)(2,1)} %broadcast_in_dim.28), calls=%async_computation.1 | async-start | bytes 393216 | tf_op jit(solution)/shard_map/all_to_all | solution.py:370
  64.4 4.2 %collective-permute-start.5 = (bf16[2,2,6,6,192]{4,3,2,1,0:T(8,128)(2,1)S(1)}, bf16[2,2,6,6,192]{4,3,2,1,0:T(8,128)(2,1)S(1)}, u32[]{:S(2)}, u32[]{:S(2)}) collective-permute-start(bf16[2,2,6,6,192]{4,3,2,1,0:T(8,128)(2,1)S(1)} %maximum_maximum_fusion.4), channel_id=1, source_target_pairs={{0,1},{1,2},{2,3},{3,4},{4,5},{5,6},{6,7},{7,8},{8,9},{9,10},{10,1... | collective-permute-start | bytes 165896 | tf_op jit(solution)/shard_map/ppermute | solution.py:377
  74.7 14.8 %all-to-all-start.2 = ((bf16[16,8,768]{2,1,0:T(8,128)(2,1)}), bf16[16,8,768]{2,1,0:T(8,128)(2,1)S(1)}, u32[]{:S(2)}, u32[]{:S(2)}) async-start(bf16[16,8,768]{2,1,0:T(8,128)(2,1)} %broadcast_in_dim.29), calls=%async_computation.2 | async-start | bytes 393216 | tf_op jit(solution)/shard_map/all_to_all | solution.py:370
  89.5 7.3 %collective-permute-start.6 = (bf16[16,8,768]{2,1,0:T(8,128)(2,1)S(1)}, bf16[16,8,768]{2,1,0:T(8,128)(2,1)S(1)}, u32[]{:S(2)}, u32[]{:S(2)}) collective-permute-start(bf16[16,8,768]{2,1,0:T(8,128)(2,1)S(1)} %all-to-all-done.2.refs_1_), channel_id=1, source_target_pairs={{0,1},{1,0},{2,3},{3,2},{4,5},{5,4},{6,7},{7,6},{8,9},{9,8},{10,11... | collective-permute-start | bytes 589832 | tf_op jit(solution)/shard_map/ppermute | solution.py:360

commit v4 on v3

--- a/solution.py
+++ b/solution.py
@@ -52,14 +52,27 @@
     return jnp.concatenate(tiles, axis=1)
 
 
-def bias_kernel(place_ref, valid_ref, table_ref, add_ref, sides_ref, skewed_ref):
+def bias_kernel(
+    place_ref,
+    valid_ref,
+    table_ref,
+    qkv_weight_ref,
+    proj_weight_ref,
+    add_ref,
+    qkv_out_ref,
+    proj_out_ref,
+    sides_ref,
+    skewed_ref,
+):
+    qkv_out_ref[...] = qkv_weight_ref[...]
+    proj_out_ref[...] = proj_weight_ref[...]
     for zn in range(WZ):
         for zm in range(WZ):
             for ln in range(WLAT):
                 at = ((zn * WZ + zm) * WLAT + ln) * SIDE
                 row = (zn * WLAT + ln) * HEADS
                 for h in range(HEADS):
-                    sides_ref[zm, row + h : row + h + 1, :] = table_ref[h, :, at : at + SIDE]
+                    sides_ref[zm, row + h : row + h + 1, :] = table_ref[0, h, :, at : at + SIDE]
     skewed = sum(
         matmul(sides_ref[z], order_of_skew(z), precision=lax.Precision.HIGHEST) for z in range(WZ)
     )
@@ -108,31 +121,50 @@
     return (lane // 32 == h).astype(f32)
 
 
-def attention_kernel(
-    place_ref,
-    x_ref,
-    dy_ref,
-    gain_ref,
-    shift_ref,
-    qkv_weight_ref,
-    qkv_bias_ref,
-    proj_weight_ref,
-    proj_bias_ref,
-    add_ref,
-    out_ref,
-    grad_ref,
-    bottom_ref,
-    mine_ref,
-    other_ref,
-    d_bias_ref,
-    parts_ref,
-    result_ref,
+def gather_window(kind, first, own_ref, lat_ref, right_ref, tiles_ref):
+    levels, rows, cols, width = own_ref.shape
+    inner = rows - HALF_LAT
+    for z in range(levels):
+        src = (z + WZ // 2) % levels
+        for r in range(rows):
+            line = own_ref[src, HALF_LAT + r] if r < inner else lat_ref[kind, src, r - inner]
+            line = line.astype(f32)[first:]
+            if right_ref is None:
+                line = line[:WLON]
+            else:
+                line = jnp.concatenate([line, right_ref[kind, src, r].astype(f32)], axis=0)
+            line = jnp.concatenate([line, jnp.zeros((WLON, -width % LANES), f32)], axis=1)
+            for t in range(tiles_ref.shape[0]):
+                tiles_ref[t, pl.ds(z * rows + r, WLON, stride=GROUP), :] = line[
+                    :, t * LANES : (t + 1) * LANES
+                ]
+    return jnp.concatenate([tiles_ref[t] for t in range(tiles_ref.shape[0])], axis=1)[:, :width]
+
+
+def scatter_window(kind, result, tiles_ref, upper_ref, bottom_ref):
+    levels, inner = upper_ref.shape[1:3]
+    width = result.shape[1]
+    to_tiles(tiles_ref, result)
+    for z in range(levels):
+        to = (z + WZ // 2) % levels
+        for r in range(WLAT):
+            line = strided_rows(tiles_ref, z * WLAT + r, WLON, GROUP)[:, :width]
+            if r < inner:
+                upper_ref[kind, to, r] = line
+            else:
+                bottom_ref[kind, to, r - inner] = line.astype(bf16)
+
+
+def attend(
+    x_tiles, dy_tiles, own, cot, lat, right, first, params, add_ref, d_bias_ref, prior, upper, bottom
 ):
-    tokens, width = x_ref.shape
-    windows = tokens // COUNT
+    gain_ref, shift_ref, qkv_weight_ref, qkv_bias_ref, proj_weight_ref, proj_bias_ref = params
+    width = own.shape[-1]
     head_dim = width // HEADS
     scale = 1.0 / math.sqrt(head_dim)
-    xf = x_ref[...].astype(f32)
+    xf = gather_window(0, first, own, lat, right, x_tiles)
+    dyf = gather_window(1, first, cot, lat, right, dy_tiles)
+    dy = dyf.astype(bf16)
     mean_value = jnp.mean(xf, axis=-1, keepdims=True)
     centered = xf - mean_value
     inverse = lax.rsqrt(jnp.mean(centered * centered, axis=-1, keepdims=True) + epsilon)
@@ -144,50 +176,41 @@
         (matmul(normed, weights[i]) + qkv_bias_ref[:, i * width : (i + 1) * width]).astype(bf16)
         for i in range(3)
     ]
-    dy = dy_ref[...]
     proj_weight = proj_weight_ref[...]
     d_attn = matmul(dy, proj_weight, ((1,), (1,))).astype(bf16)
-    tiles = [(0, 4), (4, 2)]
-    whole = []
-    for w in range(windows):
-        rows = slice(w * COUNT, (w + 1) * COUNT)
-        per_tile = []
-        for first, heads in tiles:
-            lanes = slice(first * head_dim, (first + heads) * head_dim)
-            masks = [head_lanes(heads * head_dim, h) for h in range(heads)]
-            masks_b = [m.astype(bf16) for m in masks]
-            qt, kt, vt, at = q[rows, lanes], k[rows, lanes], v[rows, lanes], d_attn[rows, lanes]
-            q_stack = jnp.concatenate([qt * m for m in masks_b], axis=0)
-            a_stack = jnp.concatenate([at * m for m in masks_b], axis=0)
-
-            def by_head(stacked):
-                total = stacked[:COUNT] * masks[0]
-                for h in range(1, heads):
-                    total = total + stacked[h * COUNT : (h + 1) * COUNT] * masks[h]
-                return total
-
-            at_rows = slice(first * COUNT, (first + heads) * COUNT)
-            scores = matmul(q_stack, kt, ((1,), (1,))) * scale + add_ref[at_rows, :]
-            top = jnp.max(scores, axis=-1, keepdims=True)
-            e = jnp.exp(scores - top)
-            probs_f = e * (1.0 / jnp.sum(e, axis=-1, keepdims=True))
-            probs = probs_f.astype(bf16)
-            attn = by_head(matmul(probs, vt)).astype(bf16)
-            d_probs = matmul(a_stack, vt, ((1,), (1,)))
-            d_scores = probs_f * (d_probs - jnp.sum(probs_f * d_probs, axis=-1, keepdims=True))
-            if w == 0:
-                d_bias_ref[at_rows, :] = d_scores
-            else:
-                d_bias_ref[at_rows, :] += d_scores
-            d_scores_b = d_scores.astype(bf16)
-            d_v = matmul(probs, a_stack, ((0,), (0,))).astype(bf16)
-            d_q = (by_head(matmul(d_scores_b, kt)) * scale).astype(bf16)
-            d_k = (matmul(d_scores_b, q_stack, ((0,), (0,))) * scale).astype(bf16)
-            per_tile.append((attn, d_q, d_k, d_v))
-        whole.append([jnp.concatenate([t[i] for t in per_tile], axis=1) for i in range(4)])
-    attn, d_q, d_k, d_v = [jnp.concatenate([t[i] for t in whole], axis=0) for i in range(4)]
-    to_tiles(result_ref, xf + matmul(attn, proj_weight) + proj_bias_ref[...])
-    to_grid(result_ref, out_ref, bottom_ref, 0)
+    per_tile = []
+    for head, heads in ((0, 4), (4, 2)):
+        lanes = slice(head * head_dim, (head + heads) * head_dim)
+        masks = [head_lanes(heads * head_dim, h) for h in range(heads)]
+        masks_b = [m.astype(bf16) for m in masks]
+        qt, kt, vt, at = q[:, lanes], k[:, lanes], v[:, lanes], d_attn[:, lanes]
+        q_stack = jnp.concatenate([qt * m for m in masks_b], axis=0)
+        a_stack = jnp.concatenate([at * m for m in masks_b], axis=0)
+
+        def by_head(stacked):
+            total = stacked[:COUNT] * masks[0]
+            for h in range(1, heads):
+                total = total + stacked[h * COUNT : (h + 1) * COUNT] * masks[h]
+            return total
+
+        rows = slice(head * COUNT, (head + heads) * COUNT)
+        scores = matmul(q_stack, kt, ((1,), (1,))) * scale + add_ref[rows, :]
+        top = jnp.max(scores, axis=-1, keepdims=True)
+        e = jnp.exp(scores - top)
+        probs_f = e * (1.0 / jnp.sum(e, axis=-1, keepdims=True))
+        probs = probs_f.astype(bf16)
+        attn = by_head(matmul(probs, vt)).astype(bf16)
+        d_probs = matmul(a_stack, vt, ((1,), (1,)))
+        d_scores = probs_f * (d_probs - jnp.sum(probs_f * d_probs, axis=-1, keepdims=True))
+        d_bias_ref[rows, :] = d_scores if prior is None else d_scores + prior[rows, :]
+        d_scores_b = d_scores.astype(bf16)
+        d_v = matmul(probs, a_stack, ((0,), (0,))).astype(bf16)
+        d_q = (by_head(matmul(d_scores_b, kt)) * scale).astype(bf16)
+        d_k = (matmul(d_scores_b, q_stack, ((0,), (0,))) * scale).astype(bf16)
+        per_tile.append((attn, d_q, d_k, d_v))
+    attn, d_q, d_k, d_v = [jnp.concatenate([t[i] for t in per_tile], axis=1) for i in range(4)]
+    out = xf + matmul(attn, proj_weight) + proj_bias_ref[...]
+    scatter_window(0, out, x_tiles, upper, bottom)
     d_parts = (d_q, d_k, d_v)
     d_normed = sum(matmul(d_parts[i], weights[i], ((1,), (1,))) for i in range(3))
     d_xhat = d_normed * gain
@@ -196,8 +219,7 @@
         - jnp.mean(d_xhat, axis=-1, keepdims=True)
         - xhat * jnp.mean(d_xhat * xhat, axis=-1, keepdims=True)
     )
-    to_tiles(result_ref, dy.astype(f32) + d_centered)
-    to_grid(result_ref, grad_ref, bottom_ref, 1)
+    scatter_window(1, dyf + d_centered, dy_tiles, upper, bottom)
     d_qkv = jnp.concatenate(d_parts, axis=1)
     qkv_weight_grad = matmul(normed, d_qkv, ((0,), (0,)))
     proj_weight_grad = matmul(attn, dy, ((0,), (0,)))
@@ -207,39 +229,40 @@
             jnp.sum(d_normed * xhat, axis=0, keepdims=True),
             jnp.sum(d_normed, axis=0, keepdims=True),
             jnp.sum(d_qkv.astype(f32), axis=0, keepdims=True),
-            jnp.sum(dy.astype(f32), axis=0, keepdims=True),
+            jnp.sum(dyf, axis=0, keepdims=True),
         ],
         axis=1,
+    )
+    return matrix, vector
+
+
+def first_kernel(own, cot, lat, *rest):
+    params, (add, upper, bottom, d_bias, matrix_ref, vector_ref, x_tiles, dy_tiles) = rest[:6], rest[6:]
+    matrix_ref[...], vector_ref[...] = attend(
+        x_tiles, dy_tiles, own, cot, lat, None, HALF_LON, params, add, d_bias, None, upper, bottom
+    )
+
+
+def second_kernel(place_ref, own, cot, lat, right, *rest):
+    params, (add, prior, prior_matrix, prior_vector) = rest[:6], rest[6:10]
+    upper, bottom, mine_ref, other_ref, x_tiles, dy_tiles, d_bias, parts_ref = rest[10:]
+    first = own.shape[2] - HALF_LON
+    matrix, vector = attend(
+        x_tiles, dy_tiles, own, cot, lat, right, first, params, add, d_bias, prior, upper, bottom
     )
     skewed = jnp.zeros((HEADS * GROUP, SPREAD), f32)
     for i in range(WLON):
         part = jnp.concatenate(
-            [
-                d_bias_ref[h * COUNT + i * GROUP : h * COUNT + (i + 1) * GROUP, :]
-                for h in range(HEADS)
-            ],
+            [d_bias[h * COUNT + i * GROUP : h * COUNT + (i + 1) * GROUP, :] for h in range(HEADS)],
             axis=0,
         )
         part = jnp.concatenate([part, jnp.zeros((HEADS * GROUP, SPREAD - COUNT), f32)], axis=1)
         shift = GROUP * (WLON - 1 - i)
         skewed = skewed + (part if shift == 0 else pltpu.roll(part, shift, 1))
-    pack(parts_ref, matrix, vector, skewed)
+    pack(parts_ref, matrix + prior_matrix[...], vector + prior_vector[...], skewed)
     core = place_ref[1]
     mine_ref[...] = parts_ref[core]
     other_ref[...] = parts_ref[1 - core].astype(bf16)
-
-
-def to_grid(result_ref, grid_ref, bottom_ref, kind):
-    levels, rows, cols, width = grid_ref.shape
-    for z in range(levels):
-        for r in range(rows):
-            line = strided_rows(result_ref, z * rows + r, cols, levels * rows)[:, :width]
-            to = (z + WZ // 2) % levels
-            if r < rows - HALF_LAT:
-                grid_ref[to, r + HALF_LAT] = line
-            else:
-                bottom_ref[kind, to, r - rows + HALF_LAT] = line.astype(bf16)
-                grid_ref[to, r - rows + HALF_LAT] = jnp.zeros_like(line)
 
 
 def table_slots(pieces, pairs):
@@ -304,12 +327,11 @@
         skewed_ref[2, 2 * p : 2 * p + 2, :] = wide_ref[
             d2 % cores, d2 // cores, rows : rows + 2, at2 : at2 + LANES
         ]
-    skewed = bias_factor * jnp.concatenate(
+    skewed = jnp.concatenate(
         [strided_rows(skewed_ref, a, HEADS, GROUP) for a in range(GROUP)], axis=0
     )
-    sides = [
-        matmul(skewed, order_of_skew(z), ((1,), (1,)), lax.Precision.HIGHEST) for z in range(WZ)
-    ]
+    skewed = (skewed * bias_factor).astype(bf16)
+    sides = [matmul(skewed, order_of_skew(z).astype(bf16), ((1,), (1,))) for z in range(WZ)]
     table = jnp.concatenate(
         [
             sides[zm][(zn * WLAT + ln) * HEADS : (zn * WLAT + ln + 1) * HEADS]
@@ -320,7 +342,7 @@
         axis=1,
     )
     for h in range(HEADS):
-        table_ref[h] = table[h : h + 1]
+        table_ref[0, h] = table[h : h + 1]
     count = (3 * width + wide) // LANES
     vector = jnp.concatenate(
         [wide_ref[d % cores, d // cores, rows : rows + 1, 5 * LANES :] for d in range(count)], axis=1
@@ -402,85 +424,92 @@
     lon_count = lax.axis_size("lon")
     total = levels * rows * cols
     place = jnp.stack([lax.axis_index("lat"), lax.axis_index("lon") % CORES]).astype(jnp.int32)
-    lat_halo = jnp.stack([a[:, :HALF_LAT, HALF_LON:] for a in (tokens, cotangent)])
-    lon_halo = jnp.stack([a[:, HALF_LAT:, :HALF_LON] for a in (tokens, cotangent)])
-    corner = jnp.stack([a[:, :HALF_LAT, :HALF_LON] for a in (tokens, cotangent)])
-    lat_halo = to_neighbour(lat_halo, ("lat",), (-1,))
-    corner = to_neighbour(corner, ("lat", "lon"), (-1, -1))
-    lon_halo = to_neighbour(lon_halo, ("lon",), (-1,))
-
-    add = call(
+    lat_halo = to_neighbour(
+        jnp.stack([a[:, :HALF_LAT] for a in (tokens, cotangent)]), ("lat",), (-1,)
+    )
+    table = earth_bias.transpose(0, 2, 1, 3)
+    add, qkv_weight, proj_weight = call(
         bias_kernel,
-        struct((HEADS * COUNT, COUNT)),
+        (
+            struct((HEADS * COUNT, COUNT)),
+            struct(qkv_weight.shape, bf16),
+            struct(proj_weight.shape, bf16),
+        ),
         "bias",
         [place, lat_valid],
-        [earth_bias.reshape(HEADS, 1, -1)],
-        [pltpu.VMEM((WZ, HEADS * GROUP, SIDE), f32), pltpu.VMEM((SPREAD // LANES, HEADS * GROUP, LANES), f32)],
-    )
-
-    def windows_of(kind, array):
-        own = jnp.concatenate([array[:, HALF_LAT:, HALF_LON:], lat_halo[kind]], axis=1)
-        side = jnp.concatenate([lon_halo[kind], corner[kind]], axis=1)
-        moved = jnp.roll(jnp.concatenate([own, side], axis=2), -(WZ // 2), axis=0)
-        return moved.transpose(2, 0, 1, 3).reshape(total, width)
+        [table, qkv_weight, proj_weight],
+        [
+            pltpu.VMEM((WZ, HEADS * GROUP, SIDE), f32),
+            pltpu.VMEM((SPREAD // LANES, HEADS * GROUP, LANES), f32),
+        ],
+    )
+    lat_halo, add, qkv_weight, proj_weight = lax.optimization_barrier(
+        (lat_halo, add, qkv_weight, proj_weight)
+    )
+    own_side = jnp.stack([a[:, HALF_LAT:, :HALF_LON] for a in (tokens, cotangent)])
+    right_halo = to_neighbour(
+        jnp.concatenate([own_side, lat_halo[:, :, :, :HALF_LON]], axis=2), ("lon",), (-1,)
+    )
 
     half = lon_count // CORES
     across = wide + width
-    out, grad, bottom, mine, other = call(
-        attention_kernel,
-        (
-            struct(tokens.shape),
-            struct(tokens.shape),
-            struct((2, levels, HALF_LAT, cols, width), bf16),
-            struct((half, 8, across)),
-            struct((half, 8, across), bf16),
-        ),
-        "attention",
+    params = [
+        norm_gain_vector[None],
+        norm_bias_vector[None],
+        qkv_weight,
+        qkv_bias[None],
+        proj_weight,
+        proj_bias[None],
+    ]
+    upper = struct((2, levels, rows - HALF_LAT, WLON, width))
+    bottom = struct((2, levels, HALF_LAT, WLON, width), bf16)
+    tiles = pltpu.VMEM((pl.cdiv(width, LANES), COUNT, LANES), f32)
+    d_bias = (HEADS * COUNT, COUNT)
+    upper_a, bottom_a, *prior = call(
+        first_kernel,
+        (upper, bottom, struct(d_bias), struct((width, across)), struct((1, 3 * width + wide))),
+        "first",
+        [],
+        [tokens, cotangent, lat_halo, *params, add],
+        [tiles, tiles],
+    )
+    upper_b, bottom_b, mine, other = call(
+        second_kernel,
+        (upper, bottom, struct((half, 8, across)), struct((half, 8, across), bf16)),
+        "second",
         [place],
-        [
-            windows_of(0, tokens),
-            windows_of(1, cotangent),
-            norm_gain_vector[None],
-            norm_bias_vector[None],
-            qkv_weight,
-            qkv_bias[None],
-            proj_weight,
-            proj_bias[None],
-            add,
-        ],
-        [
-            pltpu.VMEM((HEADS * COUNT, COUNT), f32),
-            pltpu.VMEM((CORES, half, 8, across), f32),
-            pltpu.VMEM((pl.cdiv(width, LANES), total, LANES), f32),
-        ],
+        [tokens, cotangent, lat_halo, right_halo, *params, add, *prior],
+        [tiles, tiles, pltpu.VMEM(d_bias, f32), pltpu.VMEM((CORES, half, 8, across), f32)],
     )
 
     pair = (mine + swap_cores(other).astype(f32)).astype(bf16)
     by_lon = jnp.sum(lax.all_to_all(pair, "lon", 0, 0, axis_index_groups=same_core()).astype(f32), axis=0)
-    top = to_neighbour(bottom, ("lat",), (1,))
-    by_lon, top = lax.optimization_barrier((by_lon, top))
     by_lat = spread_to_all(by_lon.astype(bf16), "lat", lat_count)
+    top = to_neighbour(jnp.concatenate([bottom_a, bottom_b], axis=3), ("lat",), (1,))
+    by_lat, top = lax.optimization_barrier((by_lat, top))
     edge = cols - HALF_LON
-    right = jnp.concatenate(
-        [top[:, :, :, edge:], jnp.stack([a[:, HALF_LAT:, edge:] for a in (out, grad)]).astype(bf16)],
-        axis=2,
-    )
+    right = jnp.concatenate([top[:, :, :, edge:], upper_b[:, :, :, HALF_LON:].astype(bf16)], axis=2)
     left = to_neighbour(right, ("lon",), (1,))
-    by_lat, left = lax.optimization_barrier((by_lat, left))
     by_lat = jnp.sum(by_lat.astype(f32), axis=0)
     row = lax.broadcasted_iota(jnp.int32, by_lat.shape, 0)
     column = lax.broadcasted_iota(jnp.int32, by_lat.shape, 1)
     is_table = (row >= width // lon_count) & (column < 5 * LANES)
     done = jnp.where(is_table, by_lon, by_lat).astype(bf16)
     mine = spread_to_all(done, "lon", half, same_core())
+    mine, left = lax.optimization_barrier((mine, left))
     other = swap_cores(mine)
 
-    def owned(kind, array):
-        upper = jnp.concatenate([left[kind, :, :HALF_LAT], top[kind, :, :, :edge]], axis=2)
-        lower = jnp.concatenate(
-            [left[kind, :, HALF_LAT:].astype(f32), array[:, HALF_LAT:, :edge]], axis=2
+    def owned(kind):
+        above = jnp.concatenate([left[kind, :, :HALF_LAT], top[kind, :, :, :edge]], axis=2)
+        below = jnp.concatenate(
+            [
+                left[kind, :, HALF_LAT:].astype(f32),
+                upper_a[kind],
+                upper_b[kind, :, :, :HALF_LON],
+            ],
+            axis=2,
         )
-        return jnp.concatenate([upper.astype(f32), lower], axis=1)
+        return jnp.concatenate([above.astype(f32), below], axis=1)
 
     norm_by = 1.0 / math.sqrt(total * lat_count * lon_count)
 
@@ -492,7 +521,7 @@
         (
             struct((width, wide)),
             struct((width, width)),
-            struct((HEADS, 1, earth_bias.shape[-1])),
+            struct(table.shape),
             struct((1, width)),
             struct((1, width)),
             struct((1, wide)),
@@ -504,15 +533,15 @@
         [pltpu.VMEM((CORES, half, 8, across), f32), pltpu.VMEM((SPREAD // LANES, HEADS * GROUP, LANES), f32)],
     )
     return (
-        owned(0, out),
-        owned(1, grad),
+        owned(0),
+        owned(1),
         gain[0],
         shift[0],
         qkv_weight_grad,
         qkv_bias_grad[0],
         proj_weight_grad,
         proj_bias_grad[0],
-        table.reshape(earth_bias.shape),
+        table.transpose(0, 2, 1, 3),
     )
 
 

time: 100 us -> 101 us (1.010)
  starting transfers between devices: 50.1 us -> 53.8 us
  waiting for transfers between devices: 31.2 us -> 28.9 us
  local copies, waits for them, and re-layouts: 5.8 us -> 4.67 us
    all_to_all x2, waiting for transfers between devices: 13.7 us -> 2.15 us  [spread_to_all(): return lax.all_to_all(wide, axis, 0, 0, axis_index_groups=groups)]
    ppermute x4, waiting for transfers between devices: 7.96 us -> 15.7 us  [to_neighbour(): lax.ppermute(value, axes[0], [(i, (i + steps[0]) % n) for i in range(n)])]
    ppermute x1 -> x0, starting transfers between devices: 5.88 us -> none  [to_neighbour(): return lax.ppermute(value, axes, pairs)]
    all_to_all x2, starting transfers between devices: 9.2 us -> 13.9 us  [spread_to_all(): return lax.all_to_all(wide, axis, 0, 0, axis_index_groups=groups)]
    ppermute x4, starting transfers between devices: 20.5 us -> 25.2 us  [to_neighbour(): lax.ppermute(value, axes[0], [(i, (i + steps[0]) % n) for i in range(n)])]
    all_to_all x1, waiting for transfers between devices: 7.97 us -> 9.92 us  [local(): lax.all_to_all(pair, 'lon', 0, 0, axis_index_groups=same_core()).astype(f32)]
    slice x5 -> x2, local copies, waits for them, and re-layouts: 1.13 us -> 0.02 us  [the longest x1 0.01 us: local(): upper_b[:, :, :, HALF_LON:].astype(bf16)]
    pallas_call x3 -> x4, Pallas kernels: 8.18 us -> 8.62 us  [call(): pl.pallas_call(kernel, out_shape=out_shape, in_specs=[smem] * len(scalars...]
  transfers between devices with their start and end apart: 10 -> 9, of which waited for: 7 -> 6; matrix products, arithmetic and copies ran while one was open for 3% -> 2% of each run, Pallas kernels for 2% -> 4%
where the time goes in v4:
time: 101 us; the launch traced here: 100 us
  starting transfers between devices  53.8 us (53%)
  waiting for transfers between devices  28.9 us (29%)
  Pallas kernels  8.62 us (9%)
  local copies, waits for them, and re-layouts  4.67 us (5%)
  other arithmetic  3.27 us (3%)
    ppermute x4, starting transfers between devices, to_neighbour(): lax.ppermute(value, axes[0], [(i, (i + steps[0]) % n) for i in range(n)])  25.2 us
    ppermute x4, waiting for transfers between devices, to_neighbour(): lax.ppermute(value, axes[0], [(i, (i + steps[0]) % n) for i in range(n)])  15.7 us
    all_to_all x2, starting transfers between devices, spread_to_all(): return lax.all_to_all(wide, axis, 0, 0, axis_index_groups=groups)  13.9 us
    all_to_all x1, waiting for transfers between devices, local(): lax.all_to_all(pair, 'lon', 0, 0, axis_index_groups=same_core()).astype(f32)  9.92 us
    pallas_call x4, Pallas kernels, call(): pl.pallas_call(kernel, out_shape=out_shape, in_specs=[smem] * len(scalars...  8.62 us
    ppermute x2, starting transfers between devices, swap_cores(): return lax.ppermute(value, 'lon', [(i, i ^ 1) for i in range(count)])  7.48 us
    all_to_all x1, starting transfers between devices, local(): lax.all_to_all(pair, 'lon', 0, 0, axis_index_groups=same_core()).astype(f32)  7.19 us
    unnamed x20, local copies, waits for them, and re-layouts  2.23 us
  transfers between devices with their start and end apart: 9, of which 6 were waited for; matrix products, arithmetic and copies ran while one was open for 2% of the time, Pallas kernels for 4%

profile of v4, /device:TPU:1, one launch (start us, length us, event | category | flops | bytes accessed | tf_op | source)
XLA Modules:
  0.0 100.2 jit_solution(494650669038266561)
XLA Ops:
  0.7 1.0 slice_bitcast_fusion.4
  1.7 13.8 %collective-permute-start = (bf16[2,2,3,24,192]{4,3,2,1,0:T(8,128)(2,1)S(1)}, bf16[2,2,3,24,192]{4,3,2,1,0:T(8,128)(2,1)S(1)}, u32[]{:S(2)}, u32[]{:S(2)}) collective-permute-start(bf16[2,2,3,24,192]{4,3,2,1,0:T(8,128)(2,1)S(1)} %pad_maximum_fusion), channel_id=1, source_target_pairs={{0,480},{32,0},{64,32},{96,64},{128,96},{160,128},{192,160},{224,1... | collective-permute-start | bytes 331784 | tf_op jit(solution)/shard_map/ppermute | solution.py:399
  15.6 0.1 pad_add_fusion.place_ref.refs_0_
  15.7 0.6 copy-done.8
  16.3 0.9 copy-done.4
  17.2 1.5 %bias.1 = (f32[864,144]{1,0:T(8,128)S(1)}, bf16[192,576]{1,0:T(8,128)(2,1)S(1)}, bf16[192,192]{1,0:T(8,128)(2,1)S(1)}) custom-call(s32[2]{0:T(128)S(1)} %pad_add_fusion.place_ref.refs_0_, s32[96]{0:T(128)S(1)} %copy-done.8, f32[1,6,1,3312]{3,2,1,0:T(1,128)S(1)} %bitcast.42, bf16[192,576]{1,0:T(8,128)(2,1)S(1)} %copy-done.2, bf16[192,192]{1,0:T(8,128)(2,1)S(1)} %copy-done.3), custom_call_target="tpu_custom_call" | custom-call | tf_op jit(solution)/shard_map/bias/pallas_call | solution.py:363
  18.7 2.5 %collective-permute-done.lat = bf16[2,2,3,24,192]{4,3,2,1,0:T(8,128)(2,1)S(1)} collective-permute-done((bf16[2,2,3,24,192]{4,3,2,1,0:T(8,128)(2,1)S(1)}, bf16[2,2,3,24,192]{4,3,2,1,0:T(8,128)(2,1)S(1)}, u32[]{:S(2)}, u32[]{:S(2)}) %collective-permute-start) | collective-permute-done | bytes 110624 | tf_op jit(solution)/shard_map/ppermute | solution.py:399
  21.2 3.5 %collective-permute-start.1 = (bf16[2,2,6,6,192]{4,3,2,1,0:T(8,128)(2,1)S(1)}, bf16[2,2,6,6,192]{4,3,2,1,0:T(8,128)(2,1)S(1)}, u32[]{:S(2)}, u32[]{:S(2)}) collective-permute-start(bf16[2,2,6,6,192]{4,3,2,1,0:T(8,128)(2,1)S(1)} %pad_maximum_fusion.2), channel_id=1, source_target_pairs={{0,31},{1,0},{2,1},{3,2},{4,3},{5,4},{6,5},{7,6},{8,7},{9,8},{10,9... | collective-permute-start | bytes 165896 | tf_op jit(solution)/shard_map/ppermute | solution.py:399
  24.8 0.7 copy-done.5
  25.4 2.3 %first.1 = (f32[2,2,3,12,192]{4,3,2,1,0:T(8,128)S(1)}, bf16[2,2,3,12,192]{4,3,2,1,0:T(8,128)(2,1)S(1)}, f32[864,144]{1,0:T(8,128)S(1)}, f32[192,768]{1,0:T(8,128)S(1)}, f32[1,1152]{1,0:T(1,128)S(1)}) custom-call(bf16[2,6,24,192]{3,2,1,0:T(8,128)(2,1)S(1)} %copy-done, bf16[2,6,24,192]{3,2,1,0:T(8,128)(2,1)S(1)} %copy-done.1, ...), custom_call_target="tpu_custom_call" | custom-call | tf_op jit(solution)/shard_map/first/pallas_call | solution.py:363
  27.7 3.1 %second.1 = (f32[2,2,3,12,192]{4,3,2,1,0:T(8,128)S(1)}, bf16[2,2,3,12,192]{4,3,2,1,0:T(8,128)(2,1)S(1)}, f32[16,8,768]{2,1,0:T(8,128)S(1)}, bf16[16,8,768]{2,1,0:T(8,128)(2,1)S(1)}) custom-call(s32[2]{0:T(128)S(1)} %pad_add_fusion.place_ref.refs_0_, bf16[2,6,24,192]{3,2,1,0:T(8,128)(2,1)S(1)} %copy-done, bf16[2,6,24,192]{3,2,1,0:T(8,128)(2,1)S(1)} %copy-done.1, ...), custom_call_target="tpu_custom_call" | custom-call | tf_op jit(solution)/shard_map/second/pallas_call | solution.py:363
  30.8 2.4 %collective-permute-start.2 = (bf16[16,8,768]{2,1,0:T(8,128)(2,1)S(1)}, bf16[16,8,768]{2,1,0:T(8,128)(2,1)S(1)}, u32[]{:S(2)}, u32[]{:S(2)}) collective-permute-start(bf16[16,8,768]{2,1,0:T(8,128)(2,1)S(1)} %get-tuple-element.47), channel_id=1, source_target_pairs={{0,1},{1,0},{2,3},{3,2},{4,5},{5,4},{6,7},{7,6},{8,9},{9,8},{10,11... | collective-permute-start | bytes 589832 | tf_op jit(solution)/shard_map/ppermute | solution.py:382
  33.2 1.0 %collective-permute-done.2 = bf16[16,8,768]{2,1,0:T(8,128)(2,1)S(1)} collective-permute-done((bf16[16,8,768]{2,1,0:T(8,128)(2,1)S(1)}, bf16[16,8,768]{2,1,0:T(8,128)(2,1)S(1)}, u32[]{:S(2)}, u32[]{:S(2)}) %collective-permute-start.2) | collective-permute-done | bytes 196640 | tf_op jit(solution)/shard_map/ppermute | solution.py:382
  34.3 0.7 add_convert_fusion
  35.0 7.2 %all-to-all-start = ((bf16[16,8,768]{2,1,0:T(8,128)(2,1)}), bf16[16,8,768]{2,1,0:T(8,128)(2,1)S(1)}, u32[]{:S(2)}, u32[]{:S(2)}) async-start(bf16[16,8,768]{2,1,0:T(8,128)(2,1)} %add_convert_fusion), calls=%async_computation | async-start | bytes 393216 | tf_op jit(solution)/shard_map/all_to_all | solution.py:486
  42.2 9.9 %all-to-all-done = bf16[16,8,768]{2,1,0:T(8,128)(2,1)S(1)} async-done(((bf16[16,8,768]{2,1,0:T(8,128)(2,1)}), bf16[16,8,768]{2,1,0:T(8,128)(2,1)S(1)}, u32[]{:S(2)}, u32[]{:S(2)}) %all-to-all-start) | async-done | bytes 196640 | tf_op jit(solution)/shard_map/all_to_all | solution.py:486
  52.2 0.7 broadcast_in_dim.28
  52.9 7.9 %all-to-all-start.1 = ((bf16[16,8,768]{2,1,0:T(8,128)(2,1)}), bf16[16,8,768]{2,1,0:T(8,128)(2,1)S(1)}, u32[]{:S(2)}, u32[]{:S(2)}) async-start(bf16[16,8,768]{2,1,0:T(8,128)(2,1)} %broadcast_in_dim.28), calls=%async_computation.1 | async-start | bytes 393216 | tf_op jit(solution)/shard_map/all_to_all | solution.py:392
  60.8 0.1 pad_maximum_fusion.1
  60.8 3.3 %collective-permute-start.3 = (bf16[2,2,3,24,192]{4,3,2,1,0:T(8,128)(2,1)S(1)}, bf16[2,2,3,24,192]{4,3,2,1,0:T(8,128)(2,1)S(1)}, u32[]{:S(2)}, u32[]{:S(2)}) collective-permute-start(bf16[2,2,3,24,192]{4,3,2,1,0:T(8,128)(2,1)S(1)} %pad_maximum_fusion.1), channel_id=1, source_target_pairs={{0,32},{32,64},{64,96},{96,128},{128,160},{160,192},{192,224},{224... | collective-permute-start | bytes 331784 | tf_op jit(solution)/shard_map/ppermute | solution.py:399
  64.1 11.1 %collective-permute-done.3 = bf16[2,2,3,24,192]{4,3,2,1,0:T(8,128)(2,1)S(1)} collective-permute-done((bf16[2,2,3,24,192]{4,3,2,1,0:T(8,128)(2,1)S(1)}, bf16[2,2,3,24,192]{4,3,2,1,0:T(8,128)(2,1)S(1)}, u32[]{:S(2)}, u32[]{:S(2)}) %collective-permute-start.3) | collective-permute-done | bytes 110624 | tf_op jit(solution)/shard_map/ppermute | solution.py:399
  75.3 0.1 select_convert_fusion
  75.4 0.7 broadcast_in_dim.29
  76.1 6.0 %all-to-all-start.2 = ((bf16[16,8,768]{2,1,0:T(8,128)(2,1)}), bf16[16,8,768]{2,1,0:T(8,128)(2,1)S(1)}, u32[]{:S(2)}, u32[]{:S(2)}) async-start(bf16[16,8,768]{2,1,0:T(8,128)(2,1)} %broadcast_in_dim.29), calls=%async_computation.2 | async-start | bytes 393216 | tf_op jit(solution)/shard_map/all_to_all | solution.py:392
  82.2 4.6 %collective-permute-start.4 = (bf16[2,2,6,6,192]{4,3,2,1,0:T(8,128)(2,1)S(1)}, bf16[2,2,6,6,192]{4,3,2,1,0:T(8,128)(2,1)S(1)}, u32[]{:S(2)}, u32[]{:S(2)}) collective-permute-start(bf16[2,2,6,6,192]{4,3,2,1,0:T(8,128)(2,1)S(1)} %pad_maximum_fusion.3), channel_id=1, source_target_pairs={{0,1},{1,2},{2,3},{3,4},{4,5},{5,6},{6,7},{7,8},{8,9},{9,10},{10,1... | collective-permute-start | bytes 165896 | tf_op jit(solution)/shard_map/ppermute | solution.py:399
  86.8 2.2 %collective-permute-done.4 = bf16[2,2,6,6,192]{4,3,2,1,0:T(8,128)(2,1)S(1)} collective-permute-done((bf16[2,2,6,6,192]{4,3,2,1,0:T(8,128)(2,1)S(1)}, bf16[2,2,6,6,192]{4,3,2,1,0:T(8,128)(2,1)S(1)}, u32[]{:S(2)}, u32[]{:S(2)}) %collective-permute-start.4) | collective-permute-done | bytes 55328 | tf_op jit(solution)/shard_map/ppermute | solution.py:399
  89.0 2.1 %all-to-all-done.2.refs_1_ = bf16[16,8,768]{2,1,0:T(8,128)(2,1)S(1)} async-done(((bf16[16,8,768]{2,1,0:T(8,128)(2,1)}), bf16[16,8,768]{2,1,0:T(8,128)(2,1)S(1)}, u32[]{:S(2)}, u32[]{:S(2)}) %all-to-all-start.2) | async-done | bytes 196640 | tf_op jit(solution)/shard_map/all_to_all | solution.py:392
  91.1 5.1 %collective-permute-start.5 = (bf16[16,8,768]{2,1,0:T(8,128)(2,1)S(1)}, bf16[16,8,768]{2,1,0:T(8,128)(2,1)S(1)}, u32[]{:S(2)}, u32[]{:S(2)}) collective-permute-start(bf16[16,8,768]{2,1,0:T(8,128)(2,1)S(1)} %all-to-all-done.2.refs_1_), channel_id=1, source_target_pairs={{0,1},{1,0},{2,3},{3,2},{4,5},{5,4},{6,7},{7,6},{8,9},{9,8},{10,11... | collective-permute-start | bytes 589832 | tf_op jit(solution)/shard_map/ppermute | solution.py:382
  96.3 0.8 maximum_maximum_fusion.1
  97.1 0.8 maximum_maximum_fusion
  97.8 1.7 %unpack.1 = (f32[192,576]{1,0:T(8,128)}, f32[192,192]{1,0:T(8,128)}, f32[1,6,1,3312]{3,2,1,0:T(1,128)}, f32[1,192]{1,0:T(1,128)}, f32[1,192]{1,0:T(1,128)}, /*index=5*/f32[1,576]{1,0:T(1,128)S(1)}, f32[1,192]{1,0:T(1,128)}) custom-call(s32[2]{0:T(128)S(1)} %pad_add_fusion.place_ref.refs_0_, bf16[16,8,768]{2,1,0:T(8,128)(2,1)S(1)} %all-to-all-done.2.refs_1_, ...), custom_call_target="tpu_custom_call" | custom-call | tf_op jit(solution)/shard_map/unpack/pallas_call | solution.py:363
  99.6 0.6 reduce
  (38 shorter events, 0.4 us)
Async XLA Ops:
  0.6 15.0 %copy-start.2 = (bf16[192,576]{1,0:T(8,128)(2,1)S(1)}, bf16[192,576]{1,0:T(8,128)(2,1)}, u32[]{:S(2)}) copy-start(bf16[192,576]{1,0:T(8,128)(2,1)} %qkv_weight_ref.1) | copy-start | bytes 663556
  1.6 13.9 %copy-start = (bf16[2,6,24,192]{3,2,1,0:T(8,128)(2,1)S(1)}, bf16[2,6,24,192]{3,2,1,0:T(8,128)(2,1)}, u32[]{:S(2)}) copy-start(bf16[2,6,24,192]{3,2,1,0:T(8,128)(2,1)} %own.3) | copy-start | bytes 331780
  1.6 13.9 %copy-start.1 = (bf16[2,6,24,192]{3,2,1,0:T(8,128)(2,1)S(1)}, bf16[2,6,24,192]{3,2,1,0:T(8,128)(2,1)}, u32[]{:S(2)}) copy-start(bf16[2,6,24,192]{3,2,1,0:T(8,128)(2,1)} %cot.3) | copy-start | bytes 331780
  1.7 14.0 %copy-start.3 = (bf16[192,192]{1,0:T(8,128)(2,1)S(1)}, bf16[192,192]{1,0:T(8,128)(2,1)}, u32[]{:S(2)}) copy-start(bf16[192,192]{1,0:T(8,128)(2,1)} %proj_weight_ref.1) | copy-start | bytes 221188
  1.7 19.5 %collective-permute-start = (bf16[2,2,3,24,192]{4,3,2,1,0:T(8,128)(2,1)S(1)}, bf16[2,2,3,24,192]{4,3,2,1,0:T(8,128)(2,1)S(1)}, u32[]{:S(2)}, u32[]{:S(2)}) collective-permute-start(bf16[2,2,3,24,192]{4,3,2,1,0:T(8,128)(2,1)S(1)} %pad_maximum_fusion), channel_id=1, source_target_pairs={{0,480},{32,0},{64,32},{96,64},{128,96},{160,128},{192,160},{224,1... | collective-permute-start | bytes 331784 | tf_op jit(solution)/shard_map/ppermute | solution.py:399
  15.7 0.7 copy-start.8
  16.3 0.9 copy-start.4
  21.2 3.5 %copy-start.9 = (f32[576]{0:T(1024)S(1)}, f32[576]{0:T(1024)}, u32[]{:S(2)}) copy-start(f32[576]{0:T(1024)} %param.15) | copy-start | bytes 6916
  21.2 3.6 %copy-start.6 = (f32[192]{0:T(256)S(1)}, f32[192]{0:T(256)}, u32[]{:S(2)}) copy-start(f32[192]{0:T(256)} %param.13) | copy-start | bytes 2308
  21.2 3.6 %copy-start.7 = (f32[192]{0:T(256)S(1)}, f32[192]{0:T(256)}, u32[]{:S(2)}) copy-start(f32[192]{0:T(256)} %param.17) | copy-start | bytes 2308
  21.2 6.5 %collective-permute-start.1 = (bf16[2,2,6,6,192]{4,3,2,1,0:T(8,128)(2,1)S(1)}, bf16[2,2,6,6,192]{4,3,2,1,0:T(8,128)(2,1)S(1)}, u32[]{:S(2)}, u32[]{:S(2)}) collective-permute-start(bf16[2,2,6,6,192]{4,3,2,1,0:T(8,128)(2,1)S(1)} %pad_maximum_fusion.2), channel_id=1, source_target_pairs={{0,31},{1,0},{2,1},{3,2},{4,3},{5,4},{6,5},{7,6},{8,7},{9,8},{10,9... | collective-permute-start | bytes 165896 | tf_op jit(solution)/shard_map/ppermute | solution.py:399
  24.7 0.7 copy-start.5
  30.8 3.5 %collective-permute-start.2 = (bf16[16,8,768]{2,1,0:T(8,128)(2,1)S(1)}, bf16[16,8,768]{2,1,0:T(8,128)(2,1)S(1)}, u32[]{:S(2)}, u32[]{:S(2)}) collective-permute-start(bf16[16,8,768]{2,1,0:T(8,128)(2,1)S(1)} %get-tuple-element.47), channel_id=1, source_target_pairs={{0,1},{1,0},{2,3},{3,2},{4,5},{5,4},{6,7},{7,6},{8,9},{9,8},{10,11... | collective-permute-start | bytes 589832 | tf_op jit(solution)/shard_map/ppermute | solution.py:382
  35.0 17.1 %all-to-all-start = ((bf16[16,8,768]{2,1,0:T(8,128)(2,1)}), bf16[16,8,768]{2,1,0:T(8,128)(2,1)S(1)}, u32[]{:S(2)}, u32[]{:S(2)}) async-start(bf16[16,8,768]{2,1,0:T(8,128)(2,1)} %add_convert_fusion), calls=%async_computation | async-start | bytes 393216 | tf_op jit(solution)/shard_map/all_to_all | solution.py:486
  52.9 22.4 %all-to-all-start.1 = ((bf16[16,8,768]{2,1,0:T(8,128)(2,1)}), bf16[16,8,768]{2,1,0:T(8,128)(2,1)S(1)}, u32[]{:S(2)}, u32[]{:S(2)}) async-start(bf16[16,8,768]{2,1,0:T(8,128)(2,1)} %broadcast_in_dim.28), calls=%async_computation.1 | async-start | bytes 393216 | tf_op jit(solution)/shard_map/all_to_all | solution.py:392
  60.8 14.4 %collective-permute-start.3 = (bf16[2,2,3,24,192]{4,3,2,1,0:T(8,128)(2,1)S(1)}, bf16[2,2,3,24,192]{4,3,2,1,0:T(8,128)(2,1)S(1)}, u32[]{:S(2)}, u32[]{:S(2)}) collective-permute-start(bf16[2,2,3,24,192]{4,3,2,1,0:T(8,128)(2,1)S(1)} %pad_maximum_fusion.1), channel_id=1, source_target_pairs={{0,32},{32,64},{64,96},{96,128},{128,160},{160,192},{192,224},{224... | collective-permute-start | bytes 331784 | tf_op jit(solution)/shard_map/ppermute | solution.py:399
  76.1 15.1 %all-to-all-start.2 = ((bf16[16,8,768]{2,1,0:T(8,128)(2,1)}), bf16[16,8,768]{2,1,0:T(8,128)(2,1)S(1)}, u32[]{:S(2)}, u32[]{:S(2)}) async-start(bf16[16,8,768]{2,1,0:T(8,128)(2,1)} %broadcast_in_dim.29), calls=%async_computation.2 | async-start | bytes 393216 | tf_op jit(solution)/shard_map/all_to_all | solution.py:392
  82.2 6.8 %collective-permute-start.4 = (bf16[2,2,6,6,192]{4,3,2,1,0:T(8,128)(2,1)S(1)}, bf16[2,2,6,6,192]{4,3,2,1,0:T(8,128)(2,1)S(1)}, u32[]{:S(2)}, u32[]{:S(2)}) collective-permute-start(bf16[2,2,6,6,192]{4,3,2,1,0:T(8,128)(2,1)S(1)} %pad_maximum_fusion.3), channel_id=1, source_target_pairs={{0,1},{1,2},{2,3},{3,4},{4,5},{5,6},{6,7},{7,8},{8,9},{9,10},{10,1... | collective-permute-start | bytes 165896 | tf_op jit(solution)/shard_map/ppermute | solution.py:399
  91.1 6.7 %collective-permute-start.5 = (bf16[16,8,768]{2,1,0:T(8,128)(2,1)S(1)}, bf16[16,8,768]{2,1,0:T(8,128)(2,1)S(1)}, u32[]{:S(2)}, u32[]{:S(2)}) collective-permute-start(bf16[16,8,768]{2,1,0:T(8,128)(2,1)S(1)} %all-to-all-done.2.refs_1_), channel_id=1, source_target_pairs={{0,1},{1,0},{2,3},{3,2},{4,5},{5,4},{6,7},{7,6},{8,9},{9,8},{10,11... | collective-permute-start | bytes 589832 | tf_op jit(solution)/shard_map/ppermute | solution.py:382

commit v5 on v4

--- a/solution.py
+++ b/solution.py
@@ -56,16 +56,11 @@
     place_ref,
     valid_ref,
     table_ref,
-    qkv_weight_ref,
-    proj_weight_ref,
-    add_ref,
-    qkv_out_ref,
-    proj_out_ref,
-    sides_ref,
-    skewed_ref,
+    *rest,
 ):
-    qkv_out_ref[...] = qkv_weight_ref[...]
-    proj_out_ref[...] = proj_weight_ref[...]
+    params, add_ref, params_out, (sides_ref, skewed_ref) = rest[:6], rest[6], rest[7:13], rest[13:]
+    for ref, to in zip(params, params_out):
+        to[...] = ref[...]
     for zn in range(WZ):
         for zm in range(WZ):
             for ln in range(WLAT):
@@ -121,42 +116,128 @@
     return (lane // 32 == h).astype(f32)
 
 
+def unpacked(packed_ref, at, kind):
+    low = packed_ref[(*at, kind)].astype(f32)
+    high = packed_ref[(*at, 2)].astype(f32)
+    return [low, high if kind == 0 else pltpu.roll(high, LANES // 2, 1)]
+
+
 def gather_window(kind, first, own_ref, lat_ref, right_ref, tiles_ref):
     levels, rows, cols, width = own_ref.shape
     inner = rows - HALF_LAT
     for z in range(levels):
         src = (z + WZ // 2) % levels
         for r in range(rows):
-            line = own_ref[src, HALF_LAT + r] if r < inner else lat_ref[kind, src, r - inner]
-            line = line.astype(f32)[first:]
+            if r < inner:
+                line = own_ref[src, HALF_LAT + r].astype(f32)
+                high = jnp.concatenate(
+                    [line[:, LANES:], jnp.zeros((cols, -width % LANES), f32)], axis=1
+                )
+                line = [line[:, :LANES], high]
+            else:
+                line = unpacked(lat_ref, (src, r - inner), kind)
             if right_ref is None:
-                line = line[:WLON]
+                line = [part[first : first + WLON] for part in line]
             else:
-                line = jnp.concatenate([line, right_ref[kind, src, r].astype(f32)], axis=0)
-            line = jnp.concatenate([line, jnp.zeros((WLON, -width % LANES), f32)], axis=1)
-            for t in range(tiles_ref.shape[0]):
-                tiles_ref[t, pl.ds(z * rows + r, WLON, stride=GROUP), :] = line[
-                    :, t * LANES : (t + 1) * LANES
-                ]
-    return jnp.concatenate([tiles_ref[t] for t in range(tiles_ref.shape[0])], axis=1)[:, :width]
-
-
-def scatter_window(kind, result, tiles_ref, upper_ref, bottom_ref):
+                ends = unpacked(right_ref, (src, r), kind)
+                line = [jnp.concatenate([p[first:], e], axis=0) for p, e in zip(line, ends)]
+            for t, part in enumerate(line):
+                tiles_ref[t, pl.ds(z * rows + r, WLON, stride=GROUP), :] = part
+    return jnp.concatenate([tiles_ref[0], tiles_ref[1]], axis=1)[:, :width]
+
+
+def pack_line(packed_ref, at, kind, low, high):
+    packed_ref[(*at, kind)] = low.astype(bf16)
+    half = LANES // 2
+    if kind == 0:
+        packed_ref[(*at, 2, slice(None), slice(0, half))] = high[:, :half].astype(bf16)
+    else:
+        moved = pltpu.roll(high, half, 1)
+        packed_ref[(*at, 2, slice(None), slice(half, LANES))] = moved[:, half:].astype(bf16)
+
+
+def scatter_window(kind, result, tiles_ref, upper_ref, bottom_ref, side_ref):
     levels, inner = upper_ref.shape[1:3]
     width = result.shape[1]
     to_tiles(tiles_ref, result)
     for z in range(levels):
         to = (z + WZ // 2) % levels
         for r in range(WLAT):
-            line = strided_rows(tiles_ref, z * WLAT + r, WLON, GROUP)[:, :width]
+            low, high = [
+                tiles_ref[t, pl.ds(z * WLAT + r, WLON, stride=GROUP), :] for t in range(2)
+            ]
+            if side_ref is not None:
+                pack_line(side_ref, (to, r), kind, low[HALF_LON:], high[HALF_LON:])
             if r < inner:
-                upper_ref[kind, to, r] = line
+                upper_ref[kind, to, r] = jnp.concatenate([low, high], axis=1)[:, :width]
             else:
-                bottom_ref[kind, to, r - inner] = line.astype(bf16)
+                pack_line(bottom_ref, (to, r - inner), kind, low, high)
+
+
+def packed_lines(tokens, cotangent):
+    high = jnp.concatenate([tokens[..., LANES:], cotangent[..., LANES:]], axis=-1)
+    return jnp.stack([tokens[..., :LANES], cotangent[..., :LANES], high], axis=2)
+
+
+def cut_kernel(tokens_ref, cot_ref, packed_ref):
+    for z in range(packed_ref.shape[0]):
+        for r in range(packed_ref.shape[1]):
+            lines = [ref[z, r] for ref in (tokens_ref, cot_ref)]
+            for k in range(2):
+                packed_ref[z, r, k] = lines[k][:, :LANES]
+            packed_ref[z, r, 2] = jnp.concatenate([line[:, LANES:] for line in lines], axis=1)
+
+
+def owned_kernel(top_ref, left_ref, upper_a_ref, upper_b_ref, out_ref, grad_ref):
+    levels, rows, cols, width = out_ref.shape
+    for kind, ref in enumerate((out_ref, grad_ref)):
+        for z in range(levels):
+            for r in range(rows):
+                if r < HALF_LAT:
+                    ref[z, r] = jnp.concatenate(unpacked(top_ref, (z, r), kind), axis=1)[:, :width]
+                else:
+                    line = unpacked(left_ref, (z, r - HALF_LAT), kind)
+                    own = [u[kind, z, r - HALF_LAT] for u in (upper_a_ref, upper_b_ref)]
+                    parts = [jnp.concatenate(line, axis=1)[:, :width], own[0], own[1][:HALF_LON]]
+                    ref[z, r] = jnp.concatenate(parts, axis=0)
+
+
+def pair_kernel(mine_ref, other_ref, sum_ref):
+    sum_ref[...] = (mine_ref[...] + other_ref[...].astype(f32)).astype(bf16)
+
+
+def spread(piece_ref, out_ref, sem):
+    copies = [pltpu.make_async_copy(piece_ref, out_ref.at[d], sem.at[d]) for d in range(out_ref.shape[0])]
+    for copy in copies:
+        copy.start()
+    for copy in copies:
+        copy.wait()
+
+
+def sum_pieces(pieces_ref):
+    total = pieces_ref[0].astype(f32)
+    for d in range(1, pieces_ref.shape[0]):
+        total = total + pieces_ref[d].astype(f32)
+    return total
+
+
+def lon_kernel(pieces_ref, piece_ref, out_ref, sem):
+    piece_ref[...] = sum_pieces(pieces_ref).astype(bf16)
+    spread(piece_ref, out_ref, sem)
+
+
+def lat_kernel(rows, pieces_ref, by_lon_ref, out_ref, piece_ref, sem):
+    shape = piece_ref.shape
+    row = lax.broadcasted_iota(jnp.int32, shape, 0)
+    column = lax.broadcasted_iota(jnp.int32, shape, 1)
+    is_table = (row >= rows) & (column < 5 * LANES)
+    total = jnp.where(is_table, by_lon_ref[...].astype(f32), sum_pieces(pieces_ref))
+    piece_ref[...] = total.astype(bf16)
+    spread(piece_ref, out_ref, sem)
 
 
 def attend(
-    x_tiles, dy_tiles, own, cot, lat, right, first, params, add_ref, d_bias_ref, prior, upper, bottom
+    x_tiles, dy_tiles, own, cot, lat, right, first, params, add_ref, d_bias_ref, prior, *grids
 ):
     gain_ref, shift_ref, qkv_weight_ref, qkv_bias_ref, proj_weight_ref, proj_bias_ref = params
     width = own.shape[-1]
@@ -210,7 +291,7 @@
         per_tile.append((attn, d_q, d_k, d_v))
     attn, d_q, d_k, d_v = [jnp.concatenate([t[i] for t in per_tile], axis=1) for i in range(4)]
     out = xf + matmul(attn, proj_weight) + proj_bias_ref[...]
-    scatter_window(0, out, x_tiles, upper, bottom)
+    scatter_window(0, out, x_tiles, *grids)
     d_parts = (d_q, d_k, d_v)
     d_normed = sum(matmul(d_parts[i], weights[i], ((1,), (1,))) for i in range(3))
     d_xhat = d_normed * gain
@@ -219,7 +300,7 @@
         - jnp.mean(d_xhat, axis=-1, keepdims=True)
         - xhat * jnp.mean(d_xhat * xhat, axis=-1, keepdims=True)
     )
-    scatter_window(1, dyf + d_centered, dy_tiles, upper, bottom)
+    scatter_window(1, dyf + d_centered, dy_tiles, *grids)
     d_qkv = jnp.concatenate(d_parts, axis=1)
     qkv_weight_grad = matmul(normed, d_qkv, ((0,), (0,)))
     proj_weight_grad = matmul(attn, dy, ((0,), (0,)))
@@ -239,16 +320,16 @@
 def first_kernel(own, cot, lat, *rest):
     params, (add, upper, bottom, d_bias, matrix_ref, vector_ref, x_tiles, dy_tiles) = rest[:6], rest[6:]
     matrix_ref[...], vector_ref[...] = attend(
-        x_tiles, dy_tiles, own, cot, lat, None, HALF_LON, params, add, d_bias, None, upper, bottom
+        x_tiles, dy_tiles, own, cot, lat, None, HALF_LON, params, add, d_bias, None, upper, bottom, None
     )
 
 
 def second_kernel(place_ref, own, cot, lat, right, *rest):
     params, (add, prior, prior_matrix, prior_vector) = rest[:6], rest[6:10]
-    upper, bottom, mine_ref, other_ref, x_tiles, dy_tiles, d_bias, parts_ref = rest[10:]
+    upper, bottom, side, mine_ref, other_ref, x_tiles, dy_tiles, d_bias, parts_ref = rest[10:]
     first = own.shape[2] - HALF_LON
     matrix, vector = attend(
-        x_tiles, dy_tiles, own, cot, lat, right, first, params, add, d_bias, prior, upper, bottom
+        x_tiles, dy_tiles, own, cot, lat, right, first, params, add, d_bias, prior, upper, bottom, side
     )
     skewed = jnp.zeros((HEADS * GROUP, SPREAD), f32)
     for i in range(WLON):
@@ -350,20 +431,25 @@
     vector = vector * norm_by
     gain_ref[...] = vector[:, :width]
     shift_ref[...] = vector[:, width : 2 * width]
-    qkv_bias_ref[...] = vector[:, 2 * width : 2 * width + wide]
+    qkv_bias_ref[...] = vector[0, 2 * width : 2 * width + wide]
     proj_bias_ref[...] = vector[:, 2 * width + wide :]
 
 
 VMEM_LIMIT = 48 * 1024 * 1024
 
 
-def call(kernel, out_shape, name, scalars, arrays, scratch=()):
+def call(kernel, out_shape, name, scalars, arrays, scratch=(), in_space=pltpu.VMEM, out_spaces=None):
     smem = pl.BlockSpec(memory_space=pltpu.SMEM)
-    vmem = pl.BlockSpec(memory_space=pltpu.VMEM)
+    vmem = pl.BlockSpec(memory_space=in_space)
+    if out_spaces is None:
+        out_specs = jax.tree.map(lambda _: pl.BlockSpec(memory_space=pltpu.VMEM), out_shape)
+    else:
+        out_specs = jax.tree.map(lambda space: pl.BlockSpec(memory_space=space), out_spaces)
     return pl.pallas_call(
         kernel,
         out_shape=out_shape,
         in_specs=[smem] * len(scalars) + [vmem] * len(arrays),
+        out_specs=out_specs,
         scratch_shapes=scratch,
         compiler_params=pltpu.CompilerParams(vmem_limit_bytes=VMEM_LIMIT),
         name=name,
@@ -385,11 +471,6 @@
 def same_core():
     count = lax.axis_size("lon")
     return [list(range(c, count, CORES)) for c in range(CORES)]
-
-
-def spread_to_all(piece, axis, count, groups=None):
-    wide = jnp.broadcast_to(piece[None], (count,) + piece.shape)
-    return lax.all_to_all(wide, axis, 0, 0, axis_index_groups=groups)
 
 
 def to_neighbour(value, axes, steps):
@@ -424,35 +505,14 @@
     lon_count = lax.axis_size("lon")
     total = levels * rows * cols
     place = jnp.stack([lax.axis_index("lat"), lax.axis_index("lon") % CORES]).astype(jnp.int32)
+    def packed(count, columns):
+        return struct((levels, count, 3, columns, LANES), bf16)
+
+    cuts = lax.optimization_barrier(tuple(a[:, :HALF_LAT] for a in (tokens, cotangent)))
     lat_halo = to_neighbour(
-        jnp.stack([a[:, :HALF_LAT] for a in (tokens, cotangent)]), ("lat",), (-1,)
+        call(cut_kernel, packed(HALF_LAT, cols), "cut", [], list(cuts)), ("lat",), (-1,)
     )
     table = earth_bias.transpose(0, 2, 1, 3)
-    add, qkv_weight, proj_weight = call(
-        bias_kernel,
-        (
-            struct((HEADS * COUNT, COUNT)),
-            struct(qkv_weight.shape, bf16),
-            struct(proj_weight.shape, bf16),
-        ),
-        "bias",
-        [place, lat_valid],
-        [table, qkv_weight, proj_weight],
-        [
-            pltpu.VMEM((WZ, HEADS * GROUP, SIDE), f32),
-            pltpu.VMEM((SPREAD // LANES, HEADS * GROUP, LANES), f32),
-        ],
-    )
-    lat_halo, add, qkv_weight, proj_weight = lax.optimization_barrier(
-        (lat_halo, add, qkv_weight, proj_weight)
-    )
-    own_side = jnp.stack([a[:, HALF_LAT:, :HALF_LON] for a in (tokens, cotangent)])
-    right_halo = to_neighbour(
-        jnp.concatenate([own_side, lat_halo[:, :, :, :HALF_LON]], axis=2), ("lon",), (-1,)
-    )
-
-    half = lon_count // CORES
-    across = wide + width
     params = [
         norm_gain_vector[None],
         norm_bias_vector[None],
@@ -461,8 +521,28 @@
         proj_weight,
         proj_bias[None],
     ]
+    add, *params = call(
+        bias_kernel,
+        (struct((HEADS * COUNT, COUNT)), *[struct(p.shape, p.dtype) for p in params]),
+        "bias",
+        [place, lat_valid],
+        [table, *params],
+        [
+            pltpu.VMEM((WZ, HEADS * GROUP, SIDE), f32),
+            pltpu.VMEM((SPREAD // LANES, HEADS * GROUP, LANES), f32),
+        ],
+    )
+    lat_halo, add = lax.optimization_barrier((lat_halo, add))
+    own_side = packed_lines(*[a[:, HALF_LAT:, :HALF_LON] for a in (tokens, cotangent)])
+    right_halo = to_neighbour(
+        jnp.concatenate([own_side, lat_halo[:, :, :, :HALF_LON]], axis=1), ("lon",), (-1,)
+    )
+
+    half = lon_count // CORES
+    across = wide + width
     upper = struct((2, levels, rows - HALF_LAT, WLON, width))
-    bottom = struct((2, levels, HALF_LAT, WLON, width), bf16)
+    bottom = packed(HALF_LAT, WLON)
+    side = packed(rows, WLON - HALF_LON)
     tiles = pltpu.VMEM((pl.cdiv(width, LANES), COUNT, LANES), f32)
     d_bias = (HEADS * COUNT, COUNT)
     upper_a, bottom_a, *prior = call(
@@ -473,43 +553,58 @@
         [tokens, cotangent, lat_halo, *params, add],
         [tiles, tiles],
     )
-    upper_b, bottom_b, mine, other = call(
+    upper_b, bottom_b, side_b, mine, other = call(
         second_kernel,
-        (upper, bottom, struct((half, 8, across)), struct((half, 8, across), bf16)),
+        (upper, bottom, side, struct((half, 8, across)), struct((half, 8, across), bf16)),
         "second",
         [place],
         [tokens, cotangent, lat_halo, right_halo, *params, add, *prior],
         [tiles, tiles, pltpu.VMEM(d_bias, f32), pltpu.VMEM((CORES, half, 8, across), f32)],
     )
 
-    pair = (mine + swap_cores(other).astype(f32)).astype(bf16)
-    by_lon = jnp.sum(lax.all_to_all(pair, "lon", 0, 0, axis_index_groups=same_core()).astype(f32), axis=0)
-    by_lat = spread_to_all(by_lon.astype(bf16), "lat", lat_count)
-    top = to_neighbour(jnp.concatenate([bottom_a, bottom_b], axis=3), ("lat",), (1,))
+    pieces = struct((half, 8, across), bf16)
+    piece = struct((8, across), bf16)
+    pair = call(pair_kernel, pieces, "pair", [], [mine, swap_cores(other)])
+    pair = lax.all_to_all(pair, "lon", 0, 0, axis_index_groups=same_core())
+    left = to_neighbour(side_b, ("lon",), (1,))
+    pair, left = lax.optimization_barrier((pair, left))
+    by_lon, pair = call(
+        lon_kernel,
+        (piece, struct((lat_count, 8, across), bf16)),
+        "lon",
+        [],
+        [pair],
+        [pltpu.SemaphoreType.DMA((lat_count,))],
+        out_spaces=(pltpu.VMEM, pl.ANY),
+    )
+    by_lat = lax.all_to_all(pair, "lat", 0, 0)
+    inner = rows - HALF_LAT
+    bottom = [left[:, inner:], bottom_a, bottom_b[:, :, :, :HALF_LON]]
+    top = to_neighbour(jnp.concatenate(bottom, axis=3), ("lat",), (1,))
     by_lat, top = lax.optimization_barrier((by_lat, top))
-    edge = cols - HALF_LON
-    right = jnp.concatenate([top[:, :, :, edge:], upper_b[:, :, :, HALF_LON:].astype(bf16)], axis=2)
-    left = to_neighbour(right, ("lon",), (1,))
-    by_lat = jnp.sum(by_lat.astype(f32), axis=0)
-    row = lax.broadcasted_iota(jnp.int32, by_lat.shape, 0)
-    column = lax.broadcasted_iota(jnp.int32, by_lat.shape, 1)
-    is_table = (row >= width // lon_count) & (column < 5 * LANES)
-    done = jnp.where(is_table, by_lon, by_lat).astype(bf16)
-    mine = spread_to_all(done, "lon", half, same_core())
-    mine, left = lax.optimization_barrier((mine, left))
+
+    def lat_sum(*refs):
+        lat_kernel(width // lon_count, *refs)
+
+    mine = call(
+        lat_sum,
+        pieces,
+        "lat",
+        [],
+        [by_lat, by_lon],
+        [pltpu.VMEM((8, across), bf16), pltpu.SemaphoreType.DMA((half,))],
+        out_spaces=pl.ANY,
+    )
+    mine = lax.all_to_all(mine, "lon", 0, 0, axis_index_groups=same_core())
+    block_out, token_grad = call(
+        owned_kernel,
+        (struct(tokens.shape), struct(tokens.shape)),
+        "owned",
+        [],
+        [top, left, upper_a, upper_b],
+    )
+    mine, block_out, token_grad = lax.optimization_barrier((mine, block_out, token_grad))
     other = swap_cores(mine)
-
-    def owned(kind):
-        above = jnp.concatenate([left[kind, :, :HALF_LAT], top[kind, :, :, :edge]], axis=2)
-        below = jnp.concatenate(
-            [
-                left[kind, :, HALF_LAT:].astype(f32),
-                upper_a[kind],
-                upper_b[kind, :, :, :HALF_LON],
-            ],
-            axis=2,
-        )
-        return jnp.concatenate([above.astype(f32), below], axis=1)
 
     norm_by = 1.0 / math.sqrt(total * lat_count * lon_count)
 
@@ -524,7 +619,7 @@
             struct(table.shape),
             struct((1, width)),
             struct((1, width)),
-            struct((1, wide)),
+            struct((wide,)),
             struct((1, width)),
         ),
         "unpack",
@@ -533,12 +628,12 @@
         [pltpu.VMEM((CORES, half, 8, across), f32), pltpu.VMEM((SPREAD // LANES, HEADS * GROUP, LANES), f32)],
     )
     return (
-        owned(0),
-        owned(1),
+        block_out,
+        token_grad,
         gain[0],
         shift[0],
         qkv_weight_grad,
-        qkv_bias_grad[0],
+        qkv_bias_grad,
         proj_weight_grad,
         proj_bias_grad[0],
         table.transpose(0, 2, 1, 3),

time: 101 us -> 96.2 us (0.952)
  waiting for transfers between devices: 28.9 us -> 25 us
  Pallas kernels: 8.62 us -> 12 us
  other arithmetic: 3.27 us -> 0.24 us
  local copies, waits for them, and re-layouts: 4.67 us -> 1.68 us
  starting transfers between devices: 53.8 us -> 55.7 us
    ppermute x4, waiting for transfers between devices: 15.7 us -> 10.1 us  [to_neighbour(): lax.ppermute(value, axes[0], [(i, (i + steps[0]) % n) for i in range(n)])]
    pallas_call x4 -> x9, Pallas kernels: 8.62 us -> 12 us  [call(): pl.pallas_call(kernel, out_shape=out_shape, in_specs=[smem] * len(scalars...]
    concatenate x5 -> x2, other arithmetic: 1.62 us -> 0.08 us  [the longest x1 0.06 us: local(): top = to_neighbour(jnp.concatenate(bottom, axis=3), ('lat',), (1,))]
    unnamed x20, local copies, waits for them, and re-layouts: 2.23 us -> 0.7 us
    broadcast_in_dim x2 -> x0, local copies, waits for them, and re-layouts: 1.39 us -> none  [spread_to_all(): wide = jnp.broadcast_to(piece[None], (count,) + piece.shape)]
    ppermute x2, waiting for transfers between devices: 1.05 us -> 2.1 us  [swap_cores(): return lax.ppermute(value, 'lon', [(i, i ^ 1) for i in range(count)])]
  transfers between devices with their start and end apart: 9 -> 9, of which waited for: 6 -> 6; matrix products, arithmetic and copies ran while one was open for 2% -> 0% of each run, Pallas kernels for 4% -> 5%
where the time goes in v5:
time: 96.2 us; the launch traced here: 95.5 us
  starting transfers between devices  55.7 us (58%)
  waiting for transfers between devices  25 us (26%)
  Pallas kernels  12 us (12%)
  local copies, waits for them, and re-layouts  1.68 us (2%)
    ppermute x4, starting transfers between devices, to_neighbour(): lax.ppermute(value, axes[0], [(i, (i + steps[0]) % n) for i in range(n)])  26 us
    pallas_call x9, Pallas kernels, call(): pl.pallas_call(kernel, out_shape=out_shape, in_specs=[smem] * len(scalars...  12 us
    ppermute x4, waiting for transfers between devices, to_neighbour(): lax.ppermute(value, axes[0], [(i, (i + steps[0]) % n) for i in range(n)])  10.1 us
    all_to_all x1, waiting for transfers between devices, local(): mine = lax.all_to_all(mine, 'lon', 0, 0, axis_index_groups=same_core())  8.18 us
    ppermute x2, starting transfers between devices, swap_cores(): return lax.ppermute(value, 'lon', [(i, i ^ 1) for i in range(count)])  7.94 us
    all_to_all x1, starting transfers between devices, local(): by_lat = lax.all_to_all(pair, 'lat', 0, 0)  7.86 us
    all_to_all x1, starting transfers between devices, local(): mine = lax.all_to_all(mine, 'lon', 0, 0, axis_index_groups=same_core())  7.11 us
    all_to_all x1, starting transfers between devices, local(): pair = lax.all_to_all(pair, 'lon', 0, 0, axis_index_groups=same_core())  6.8 us
  transfers between devices with their start and end apart: 9, of which 6 were waited for; matrix products, arithmetic and copies ran while one was open for 0% of the time, Pallas kernels for 5%

profile of v5, /device:TPU:1, one launch (start us, length us, event | category | flops | bytes accessed | tf_op | source)
XLA Modules:
  0.0 95.5 jit_solution(5151636171545796343)
XLA Ops:
  0.7 0.9 slice.33.tokens_ref
  1.6 0.0 copy-done.1
  1.7 0.1 cut.1
  1.7 13.8 %collective-permute-start = (bf16[2,3,3,24,128]{4,3,2,1,0:T(8,128)(2,1)S(1)}, bf16[2,3,3,24,128]{4,3,2,1,0:T(8,128)(2,1)S(1)}, u32[]{:S(2)}, u32[]{:S(2)}) collective-permute-start(bf16[2,3,3,24,128]{4,3,2,1,0:T(8,128)(2,1)S(1)} %cut.1), channel_id=1, source_target_pairs={{0,480},{32,0},{64,32},{96,64},{128,96},{160,128},{192,160},{224,1... | collective-permute-start | bytes 331784 | tf_op jit(solution)/shard_map/ppermute | solution.py:480
  15.7 0.1 maximum_bitcast_fusion
  15.7 0.1 pad_add_fusion.place_ref.refs_0_
  15.8 0.6 copy-done.6
  16.4 0.0 copy-done.7
  16.4 0.1 copy-done.5
  16.5 1.5 %bias.1 = (f32[864,144]{1,0:T(8,128)S(1)}, f32[1,192]{1,0:T(1,128)S(1)}, f32[1,192]{1,0:T(1,128)S(1)}, bf16[192,576]{1,0:T(8,128)(2,1)S(1)}, f32[1,576]{1,0:T(1,...) custom-call(s32[2]{0:T(128)S(1)} %pad_add_fusion.place_ref.refs_0_, s32[96]{0:T(128)S(1)} %copy-done.8, ...), custom_call_target="tpu_custom_call" | custom-call | tf_op jit(solution)/shard_map/bias/pallas_call | solution.py:448
  18.1 5.1 %collective-permute-start.1 = (bf16[2,6,3,6,128]{4,3,2,1,0:T(8,128)(2,1)S(1)}, bf16[2,6,3,6,128]{4,3,2,1,0:T(8,128)(2,1)S(1)}, u32[]{:S(2)}, u32[]{:S(2)}) collective-permute-start(bf16[2,6,3,6,128]{4,3,2,1,0:T(8,128)(2,1)S(1)} %pad_maximum_fusion.1), channel_id=1, source_target_pairs={{0,31},{1,0},{2,1},{3,2},{4,3},{5,4},{6,5},{7,6},{8,7},{9,8},{10,9... | collective-permute-start | bytes 165896 | tf_op jit(solution)/shard_map/ppermute | solution.py:480
  23.1 2.3 %first.1 = (f32[2,2,3,12,192]{4,3,2,1,0:T(8,128)S(1)}, bf16[2,3,3,12,128]{4,3,2,1,0:T(8,128)(2,1)S(1)}, f32[864,144]{1,0:T(8,128)S(1)}, f32[192,768]{1,0:T(8,128)S(1)}, f32[1,1152]{1,0:T(1,128)S(1)}) custom-call(bf16[2,6,24,192]{3,2,1,0:T(8,128)(2,1)S(1)} %copy-done, bf16[2,6,24,192]{3,2,1,0:T(8,128)(2,1)S(1)} %copy-done.1, ...), custom_call_target="tpu_custom_call" | custom-call | tf_op jit(solution)/shard_map/first/pallas_call | solution.py:448
  25.5 3.0 %second.1 = (f32[2,2,3,12,192]{4,3,2,1,0:T(8,128)S(1)}, bf16[2,3,3,12,128]{4,3,2,1,0:T(8,128)(2,1)S(1)}, bf16[2,6,3,6,128]{4,3,2,1,0:T(8,128)(2,1)S(1)}, f32[16,...) custom-call(s32[2]{0:T(128)S(1)} %pad_add_fusion.place_ref.refs_0_, bf16[2,6,24,192]{3,2,1,0:T(8,128)(2,1)S(1)} %copy-done, ...), custom_call_target="tpu_custom_call" | custom-call | tf_op jit(solution)/shard_map/second/pallas_call | solution.py:448
  28.5 3.2 %collective-permute-start.2 = (bf16[16,8,768]{2,1,0:T(8,128)(2,1)S(1)}, bf16[16,8,768]{2,1,0:T(8,128)(2,1)S(1)}, u32[]{:S(2)}, u32[]{:S(2)}) collective-permute-start(bf16[16,8,768]{2,1,0:T(8,128)(2,1)S(1)} %get-tuple-element.63), channel_id=1, source_target_pairs={{0,1},{1,0},{2,3},{3,2},{4,5},{5,4},{6,7},{7,6},{8,9},{9,8},{10,11... | collective-permute-start | bytes 589832 | tf_op jit(solution)/shard_map/ppermute | solution.py:468
  31.8 1.0 %collective-permute-done.2.other_ref = bf16[16,8,768]{2,1,0:T(8,128)(2,1)S(1)} collective-permute-done((bf16[16,8,768]{2,1,0:T(8,128)(2,1)S(1)}, bf16[16,8,768]{2,1,0:T(8,128)(2,1)S(1)}, u32[]{:S(2)}, u32[]{:S(2)}) %collective-permute-start.2) | collective-permute-done | bytes 196640 | tf_op jit(solution)/shard_map/ppermute | solution.py:468
  32.8 0.7 pair.1
  33.6 6.8 %all-to-all-start = ((bf16[16,8,768]{2,1,0:T(8,128)(2,1)}), bf16[16,8,768]{2,1,0:T(8,128)(2,1)S(1)}, u32[]{:S(2)}, u32[]{:S(2)}) async-start(bf16[16,8,768]{2,1,0:T(8,128)(2,1)} %pair.1), calls=%async_computation | async-start | bytes 393216 | tf_op jit(solution)/shard_map/all_to_all | solution.py:568
  40.4 3.9 %collective-permute-start.3 = (bf16[2,6,3,6,128]{4,3,2,1,0:T(8,128)(2,1)S(1)}, bf16[2,6,3,6,128]{4,3,2,1,0:T(8,128)(2,1)S(1)}, u32[]{:S(2)}, u32[]{:S(2)}) collective-permute-start(bf16[2,6,3,6,128]{4,3,2,1,0:T(8,128)(2,1)S(1)} %get-tuple-element.64), channel_id=1, source_target_pairs={{0,1},{1,2},{2,3},{3,4},{4,5},{5,6},{6,7},{7,8},{8,9},{9,10},{10,1... | collective-permute-start | bytes 165896 | tf_op jit(solution)/shard_map/ppermute | solution.py:480
  44.2 1.5 %collective-permute-done.3.left_ref = bf16[2,6,3,6,128]{4,3,2,1,0:T(8,128)(2,1)S(1)} collective-permute-done((bf16[2,6,3,6,128]{4,3,2,1,0:T(8,128)(2,1)S(1)}, bf16[2,6,3,6,128]{4,3,2,1,0:T(8,128)(2,1)S(1)}, u32[]{:S(2)}, u32[]{:S(2)}) %collective-permute-start.3) | collective-permute-done | bytes 55328 | tf_op jit(solution)/shard_map/ppermute | solution.py:480
  45.7 4.6 %all-to-all-done.pieces_ref = bf16[16,8,768]{2,1,0:T(8,128)(2,1)S(1)} async-done(((bf16[16,8,768]{2,1,0:T(8,128)(2,1)}), bf16[16,8,768]{2,1,0:T(8,128)(2,1)S(1)}, u32[]{:S(2)}, u32[]{:S(2)}) %all-to-all-start) | async-done | bytes 196640 | tf_op jit(solution)/shard_map/all_to_all | solution.py:568
  50.3 0.8 lon.1
  51.1 7.9 %all-to-all-start.1 = ((bf16[16,8,768]{2,1,0:T(8,128)(2,1)}), bf16[16,8,768]{2,1,0:T(8,128)(2,1)S(1)}, u32[]{:S(2)}, u32[]{:S(2)}) async-start(bf16[16,8,768]{2,1,0:T(8,128)(2,1)} %get-tuple-element.66), calls=%async_computation.1 | async-start | bytes 393216 | tf_op jit(solution)/shard_map/all_to_all | solution.py:580
  59.0 0.1 pad_maximum_fusion
  59.1 3.3 %collective-permute-start.4 = (bf16[2,3,3,24,128]{4,3,2,1,0:T(8,128)(2,1)S(1)}, bf16[2,3,3,24,128]{4,3,2,1,0:T(8,128)(2,1)S(1)}, u32[]{:S(2)}, u32[]{:S(2)}) collective-permute-start(bf16[2,3,3,24,128]{4,3,2,1,0:T(8,128)(2,1)S(1)} %pad_maximum_fusion), channel_id=1, source_target_pairs={{0,32},{32,64},{64,96},{96,128},{128,160},{160,192},{192,224},{224... | collective-permute-start | bytes 331784 | tf_op jit(solution)/shard_map/ppermute | solution.py:480
  62.4 8.6 %collective-permute-done.4.top_ref = bf16[2,3,3,24,128]{4,3,2,1,0:T(8,128)(2,1)S(1)} collective-permute-done((bf16[2,3,3,24,128]{4,3,2,1,0:T(8,128)(2,1)S(1)}, bf16[2,3,3,24,128]{4,3,2,1,0:T(8,128)(2,1)S(1)}, u32[]{:S(2)}, u32[]{:S(2)}) %collective-permute-start.4) | collective-permute-done | bytes 110624 | tf_op jit(solution)/shard_map/ppermute | solution.py:480
  71.0 0.8 lat.1
  71.8 7.1 %all-to-all-start.2 = ((bf16[16,8,768]{2,1,0:T(8,128)(2,1)}), bf16[16,8,768]{2,1,0:T(8,128)(2,1)S(1)}, u32[]{:S(2)}, u32[]{:S(2)}) async-start(bf16[16,8,768]{2,1,0:T(8,128)(2,1)} %lat.1), calls=%async_computation.2 | async-start | bytes 393216 | tf_op jit(solution)/shard_map/all_to_all | solution.py:598
  79.0 0.9 owned.1
  79.8 8.2 %all-to-all-done.2.refs_1_ = bf16[16,8,768]{2,1,0:T(8,128)(2,1)S(1)} async-done(((bf16[16,8,768]{2,1,0:T(8,128)(2,1)}), bf16[16,8,768]{2,1,0:T(8,128)(2,1)S(1)}, u32[]{:S(2)}, u32[]{:S(2)}) %all-to-all-start.2) | async-done | bytes 196640 | tf_op jit(solution)/shard_map/all_to_all | solution.py:598
  88.0 4.7 %collective-permute-start.5 = (bf16[16,8,768]{2,1,0:T(8,128)(2,1)S(1)}, bf16[16,8,768]{2,1,0:T(8,128)(2,1)S(1)}, u32[]{:S(2)}, u32[]{:S(2)}) collective-permute-start(bf16[16,8,768]{2,1,0:T(8,128)(2,1)S(1)} %all-to-all-done.2.refs_1_), channel_id=1, source_target_pairs={{0,1},{1,0},{2,3},{3,2},{4,5},{5,4},{6,7},{7,6},{8,9},{9,8},{10,11... | collective-permute-start | bytes 589832 | tf_op jit(solution)/shard_map/ppermute | solution.py:468
  92.7 1.0 %collective-permute-done.5.refs_2_ = bf16[16,8,768]{2,1,0:T(8,128)(2,1)S(1)} collective-permute-done((bf16[16,8,768]{2,1,0:T(8,128)(2,1)S(1)}, bf16[16,8,768]{2,1,0:T(8,128)(2,1)S(1)}, u32[]{:S(2)}, u32[]{:S(2)}) %collective-permute-start.5) | collective-permute-done | bytes 196640 | tf_op jit(solution)/shard_map/ppermute | solution.py:468
  93.8 1.8 %unpack.1 = (f32[192,576]{1,0:T(8,128)}, f32[192,192]{1,0:T(8,128)}, f32[1,6,1,3312]{3,2,1,0:T(1,128)}, f32[1,192]{1,0:T(1,128)}, f32[1,192]{1,0:T(1,128)}, /*index=5*/f32[576]{0:T(1024)}, f32[1,192]{1,0:T(1,128)}) custom-call(s32[2]{0:T(128)S(1)} %pad_add_fusion.place_ref.refs_0_, bf16[16,8,768]{2,1,0:T(8,128)(2,1)S(1)} %all-to-all-done.2.refs_1_, ...), custom_call_target="tpu_custom_call" | custom-call | tf_op jit(solution)/shard_map/unpack/pallas_call | solution.py:448
  (28 shorter events, 0.1 us)
Async XLA Ops:
  0.6 0.9 copy-start.1
  1.6 14.0 %copy-start.9 = (f32[576]{0:T(1024)S(1)}, f32[576]{0:T(1024)}, u32[]{:S(2)}) copy-start(f32[576]{0:T(1024)} %param.15) | copy-start | bytes 6916
  1.6 14.2 %copy-start.3 = (bf16[192,192]{1,0:T(8,128)(2,1)S(1)}, bf16[192,192]{1,0:T(8,128)(2,1)}, u32[]{:S(2)}) copy-start(bf16[192,192]{1,0:T(8,128)(2,1)} %rest_4_.1) | copy-start | bytes 221188
  1.6 14.2 %copy-start.4 = (f32[1,1,6,3312]{3,1,2,0:T(1,128)S(1)}, f32[1,1,6,3312]{3,1,2,0:T(1,128)}, u32[]{:S(2)}) copy-start(f32[1,1,6,3312]{3,1,2,0:T(1,128)} %param.18) | copy-start | bytes 238468
  1.6 13.9 %copy-start = (bf16[2,6,24,192]{3,2,1,0:T(8,128)(2,1)S(1)}, bf16[2,6,24,192]{3,2,1,0:T(8,128)(2,1)}, u32[]{:S(2)}) copy-start(bf16[2,6,24,192]{3,2,1,0:T(8,128)(2,1)} %own.3) | copy-start | bytes 331780
  1.6 14.2 %copy-start.2 = (bf16[192,576]{1,0:T(8,128)(2,1)S(1)}, bf16[192,576]{1,0:T(8,128)(2,1)}, u32[]{:S(2)}) copy-start(bf16[192,576]{1,0:T(8,128)(2,1)} %rest_2_.1) | copy-start | bytes 663556
  1.7 16.3 %collective-permute-start = (bf16[2,3,3,24,128]{4,3,2,1,0:T(8,128)(2,1)S(1)}, bf16[2,3,3,24,128]{4,3,2,1,0:T(8,128)(2,1)S(1)}, u32[]{:S(2)}, u32[]{:S(2)}) collective-permute-start(bf16[2,3,3,24,128]{4,3,2,1,0:T(8,128)(2,1)S(1)} %cut.1), channel_id=1, source_target_pairs={{0,480},{32,0},{64,32},{96,64},{128,96},{160,128},{192,160},{224,1... | collective-permute-start | bytes 331784 | tf_op jit(solution)/shard_map/ppermute | solution.py:480
  15.7 0.7 copy-start.6
  15.7 0.7 copy-start.7
  15.8 0.7 copy-start.5
  15.8 0.7 copy-start.8
  18.1 7.4 %collective-permute-start.1 = (bf16[2,6,3,6,128]{4,3,2,1,0:T(8,128)(2,1)S(1)}, bf16[2,6,3,6,128]{4,3,2,1,0:T(8,128)(2,1)S(1)}, u32[]{:S(2)}, u32[]{:S(2)}) collective-permute-start(bf16[2,6,3,6,128]{4,3,2,1,0:T(8,128)(2,1)S(1)} %pad_maximum_fusion.1), channel_id=1, source_target_pairs={{0,31},{1,0},{2,1},{3,2},{4,3},{5,4},{6,5},{7,6},{8,7},{9,8},{10,9... | collective-permute-start | bytes 165896 | tf_op jit(solution)/shard_map/ppermute | solution.py:480
  28.5 4.3 %collective-permute-start.2 = (bf16[16,8,768]{2,1,0:T(8,128)(2,1)S(1)}, bf16[16,8,768]{2,1,0:T(8,128)(2,1)S(1)}, u32[]{:S(2)}, u32[]{:S(2)}) collective-permute-start(bf16[16,8,768]{2,1,0:T(8,128)(2,1)S(1)} %get-tuple-element.63), channel_id=1, source_target_pairs={{0,1},{1,0},{2,3},{3,2},{4,5},{5,4},{6,7},{7,6},{8,9},{9,8},{10,11... | collective-permute-start | bytes 589832 | tf_op jit(solution)/shard_map/ppermute | solution.py:468
  33.6 16.7 %all-to-all-start = ((bf16[16,8,768]{2,1,0:T(8,128)(2,1)}), bf16[16,8,768]{2,1,0:T(8,128)(2,1)S(1)}, u32[]{:S(2)}, u32[]{:S(2)}) async-start(bf16[16,8,768]{2,1,0:T(8,128)(2,1)} %pair.1), calls=%async_computation | async-start | bytes 393216 | tf_op jit(solution)/shard_map/all_to_all | solution.py:568
  40.4 5.3 %collective-permute-start.3 = (bf16[2,6,3,6,128]{4,3,2,1,0:T(8,128)(2,1)S(1)}, bf16[2,6,3,6,128]{4,3,2,1,0:T(8,128)(2,1)S(1)}, u32[]{:S(2)}, u32[]{:S(2)}) collective-permute-start(bf16[2,6,3,6,128]{4,3,2,1,0:T(8,128)(2,1)S(1)} %get-tuple-element.64), channel_id=1, source_target_pairs={{0,1},{1,2},{2,3},{3,4},{4,5},{5,6},{6,7},{7,8},{8,9},{9,10},{10,1... | collective-permute-start | bytes 165896 | tf_op jit(solution)/shard_map/ppermute | solution.py:480
  51.1 19.9 %all-to-all-start.1 = ((bf16[16,8,768]{2,1,0:T(8,128)(2,1)}), bf16[16,8,768]{2,1,0:T(8,128)(2,1)S(1)}, u32[]{:S(2)}, u32[]{:S(2)}) async-start(bf16[16,8,768]{2,1,0:T(8,128)(2,1)} %get-tuple-element.66), calls=%async_computation.1 | async-start | bytes 393216 | tf_op jit(solution)/shard_map/all_to_all | solution.py:580
  59.1 11.9 %collective-permute-start.4 = (bf16[2,3,3,24,128]{4,3,2,1,0:T(8,128)(2,1)S(1)}, bf16[2,3,3,24,128]{4,3,2,1,0:T(8,128)(2,1)S(1)}, u32[]{:S(2)}, u32[]{:S(2)}) collective-permute-start(bf16[2,3,3,24,128]{4,3,2,1,0:T(8,128)(2,1)S(1)} %pad_maximum_fusion), channel_id=1, source_target_pairs={{0,32},{32,64},{64,96},{96,128},{128,160},{160,192},{192,224},{224... | collective-permute-start | bytes 331784 | tf_op jit(solution)/shard_map/ppermute | solution.py:480
  71.8 16.2 %all-to-all-start.2 = ((bf16[16,8,768]{2,1,0:T(8,128)(2,1)}), bf16[16,8,768]{2,1,0:T(8,128)(2,1)S(1)}, u32[]{:S(2)}, u32[]{:S(2)}) async-start(bf16[16,8,768]{2,1,0:T(8,128)(2,1)} %lat.1), calls=%async_computation.2 | async-start | bytes 393216 | tf_op jit(solution)/shard_map/all_to_all | solution.py:598
  88.0 5.7 %collective-permute-start.5 = (bf16[16,8,768]{2,1,0:T(8,128)(2,1)S(1)}, bf16[16,8,768]{2,1,0:T(8,128)(2,1)S(1)}, u32[]{:S(2)}, u32[]{:S(2)}) collective-permute-start(bf16[16,8,768]{2,1,0:T(8,128)(2,1)S(1)} %all-to-all-done.2.refs_1_), channel_id=1, source_target_pairs={{0,1},{1,0},{2,3},{3,2},{4,5},{5,4},{6,7},{7,6},{8,9},{9,8},{10,11... | collective-permute-start | bytes 589832 | tf_op jit(solution)/shard_map/ppermute | solution.py:468

commit v6 on v5

--- a/solution.py
+++ b/solution.py
@@ -60,7 +60,7 @@
 ):
     params, add_ref, params_out, (sides_ref, skewed_ref) = rest[:6], rest[6], rest[7:13], rest[13:]
     for ref, to in zip(params, params_out):
-        to[...] = ref[...]
+        to[...] = ref[...].reshape(to.shape)
     for zn in range(WZ):
         for zm in range(WZ):
             for ln in range(WLAT):
@@ -68,9 +68,16 @@
                 row = (zn * WLAT + ln) * HEADS
                 for h in range(HEADS):
                     sides_ref[zm, row + h : row + h + 1, :] = table_ref[0, h, :, at : at + SIDE]
-    skewed = sum(
-        matmul(sides_ref[z], order_of_skew(z), precision=lax.Precision.HIGHEST) for z in range(WZ)
-    )
+    skewed = 0.0
+    for z in range(WZ):
+        left = sides_ref[z]
+        parts = []
+        for _ in range(3):
+            parts.append(left.astype(bf16))
+            left = left - parts[-1].astype(f32)
+        placed = matmul(jnp.concatenate(parts, axis=0), order_of_skew(z).astype(bf16))
+        high, middle, low = [placed[k * HEADS * GROUP : (k + 1) * HEADS * GROUP] for k in range(3)]
+        skewed = skewed + ((high + middle) + low)
     to_tiles(skewed_ref, skewed)
     skewed = jnp.concatenate(
         [strided_rows(skewed_ref, h, GROUP, HEADS) for h in range(HEADS)], axis=0
@@ -122,7 +129,7 @@
     return [low, high if kind == 0 else pltpu.roll(high, LANES // 2, 1)]
 
 
-def gather_window(kind, first, own_ref, lat_ref, right_ref, tiles_ref):
+def gather_window(kind, first, own_ref, lat_ref, ends_refs, tiles_ref):
     levels, rows, cols, width = own_ref.shape
     inner = rows - HALF_LAT
     for z in range(levels):
@@ -133,14 +140,15 @@
                 high = jnp.concatenate(
                     [line[:, LANES:], jnp.zeros((cols, -width % LANES), f32)], axis=1
                 )
-                line = [line[:, :LANES], high]
+                line = [part[first:] for part in (line[:, :LANES], high)]
             else:
                 line = unpacked(lat_ref, (src, r - inner), kind)
-            if right_ref is None:
-                line = [part[first : first + WLON] for part in line]
+                line = [part[first - HALF_LON :] for part in line]
+            if not ends_refs:
+                line = [part[:WLON] for part in line]
             else:
-                ends = unpacked(right_ref, (src, r), kind)
-                line = [jnp.concatenate([p[first:], e], axis=0) for p, e in zip(line, ends)]
+                ends = unpacked(ends_refs[r // inner], (src, r % inner), kind)
+                line = [jnp.concatenate([p, e], axis=0) for p, e in zip(line, ends)]
             for t, part in enumerate(line):
                 tiles_ref[t, pl.ds(z * rows + r, WLON, stride=GROUP), :] = part
     return jnp.concatenate([tiles_ref[0], tiles_ref[1]], axis=1)[:, :width]
@@ -179,13 +187,14 @@
     return jnp.stack([tokens[..., :LANES], cotangent[..., :LANES], high], axis=2)
 
 
-def cut_kernel(tokens_ref, cot_ref, packed_ref):
-    for z in range(packed_ref.shape[0]):
-        for r in range(packed_ref.shape[1]):
-            lines = [ref[z, r] for ref in (tokens_ref, cot_ref)]
-            for k in range(2):
-                packed_ref[z, r, k] = lines[k][:, :LANES]
-            packed_ref[z, r, 2] = jnp.concatenate([line[:, LANES:] for line in lines], axis=1)
+def cut_kernel(tokens_ref, cot_ref, near_ref, rest_ref):
+    for z in range(near_ref.shape[0]):
+        for r in range(near_ref.shape[1]):
+            lines = [ref[z, r].astype(f32) for ref in (tokens_ref, cot_ref)]
+            high = jnp.concatenate([line[:, LANES:] for line in lines], axis=1)
+            for k, part in enumerate([line[:, :LANES] for line in lines] + [high]):
+                near_ref[z, r, k] = part[:HALF_LON].astype(bf16)
+                rest_ref[z, r, k] = part[HALF_LON:].astype(bf16)
 
 
 def owned_kernel(top_ref, left_ref, upper_a_ref, upper_b_ref, out_ref, grad_ref):
@@ -237,14 +246,14 @@
 
 
 def attend(
-    x_tiles, dy_tiles, own, cot, lat, right, first, params, add_ref, d_bias_ref, prior, *grids
+    x_tiles, dy_tiles, own, cot, lat, ends, first, params, add_ref, d_bias_ref, prior, *grids
 ):
     gain_ref, shift_ref, qkv_weight_ref, qkv_bias_ref, proj_weight_ref, proj_bias_ref = params
     width = own.shape[-1]
     head_dim = width // HEADS
     scale = 1.0 / math.sqrt(head_dim)
-    xf = gather_window(0, first, own, lat, right, x_tiles)
-    dyf = gather_window(1, first, cot, lat, right, dy_tiles)
+    xf = gather_window(0, first, own, lat, ends, x_tiles)
+    dyf = gather_window(1, first, cot, lat, ends, dy_tiles)
     dy = dyf.astype(bf16)
     mean_value = jnp.mean(xf, axis=-1, keepdims=True)
     centered = xf - mean_value
@@ -320,16 +329,16 @@
 def first_kernel(own, cot, lat, *rest):
     params, (add, upper, bottom, d_bias, matrix_ref, vector_ref, x_tiles, dy_tiles) = rest[:6], rest[6:]
     matrix_ref[...], vector_ref[...] = attend(
-        x_tiles, dy_tiles, own, cot, lat, None, HALF_LON, params, add, d_bias, None, upper, bottom, None
-    )
-
-
-def second_kernel(place_ref, own, cot, lat, right, *rest):
+        x_tiles, dy_tiles, own, cot, lat, (), HALF_LON, params, add, d_bias, None, upper, bottom, None
+    )
+
+
+def second_kernel(place_ref, own, cot, lat, corner, lon, *rest):
     params, (add, prior, prior_matrix, prior_vector) = rest[:6], rest[6:10]
     upper, bottom, side, mine_ref, other_ref, x_tiles, dy_tiles, d_bias, parts_ref = rest[10:]
     first = own.shape[2] - HALF_LON
     matrix, vector = attend(
-        x_tiles, dy_tiles, own, cot, lat, right, first, params, add, d_bias, prior, upper, bottom, side
+        x_tiles, dy_tiles, own, cot, lat, (lon, corner), first, params, add, d_bias, prior, upper, bottom, side
     )
     skewed = jnp.zeros((HEADS * GROUP, SPREAD), f32)
     for i in range(WLON):
@@ -438,7 +447,7 @@
 VMEM_LIMIT = 48 * 1024 * 1024
 
 
-def call(kernel, out_shape, name, scalars, arrays, scratch=(), in_space=pltpu.VMEM, out_spaces=None):
+def call(kernel, out_shape, name, scalars, arrays, scratch=(), in_space=pltpu.VMEM, out_spaces=None, cost=None):
     smem = pl.BlockSpec(memory_space=pltpu.SMEM)
     vmem = pl.BlockSpec(memory_space=in_space)
     if out_spaces is None:
@@ -452,6 +461,7 @@
         out_specs=out_specs,
         scratch_shapes=scratch,
         compiler_params=pltpu.CompilerParams(vmem_limit_bytes=VMEM_LIMIT),
+        cost_estimate=cost,
         name=name,
     )(*scalars, *arrays)
 
@@ -509,21 +519,22 @@
         return struct((levels, count, 3, columns, LANES), bf16)
 
     cuts = lax.optimization_barrier(tuple(a[:, :HALF_LAT] for a in (tokens, cotangent)))
-    lat_halo = to_neighbour(
-        call(cut_kernel, packed(HALF_LAT, cols), "cut", [], list(cuts)), ("lat",), (-1,)
-    )
+    near, rest = call(
+        cut_kernel,
+        (packed(HALF_LAT, HALF_LON), packed(HALF_LAT, cols - HALF_LON)),
+        "cut",
+        [],
+        list(cuts),
+        cost=pl.CostEstimate(flops=5_000_000_000, bytes_accessed=2_000_000, transcendentals=0),
+    )
+    side = packed_lines(*[a[:, HALF_LAT:, :HALF_LON] for a in (tokens, cotangent)])
+    lat_halo = to_neighbour(rest, ("lat",), (-1,))
     table = earth_bias.transpose(0, 2, 1, 3)
-    params = [
-        norm_gain_vector[None],
-        norm_bias_vector[None],
-        qkv_weight,
-        qkv_bias[None],
-        proj_weight,
-        proj_bias[None],
-    ]
+    params = [norm_gain_vector, norm_bias_vector, qkv_weight, qkv_bias, proj_weight, proj_bias]
+    rows_of = [(1, p.size) if p.ndim == 1 else p.shape for p in params]
     add, *params = call(
         bias_kernel,
-        (struct((HEADS * COUNT, COUNT)), *[struct(p.shape, p.dtype) for p in params]),
+        (struct((HEADS * COUNT, COUNT)), *[struct(r, p.dtype) for r, p in zip(rows_of, params)]),
         "bias",
         [place, lat_valid],
         [table, *params],
@@ -532,11 +543,9 @@
             pltpu.VMEM((SPREAD // LANES, HEADS * GROUP, LANES), f32),
         ],
     )
-    lat_halo, add = lax.optimization_barrier((lat_halo, add))
-    own_side = packed_lines(*[a[:, HALF_LAT:, :HALF_LON] for a in (tokens, cotangent)])
-    right_halo = to_neighbour(
-        jnp.concatenate([own_side, lat_halo[:, :, :, :HALF_LON]], axis=1), ("lon",), (-1,)
-    )
+    near, side, add = lax.optimization_barrier((near, side, add))
+    corner = to_neighbour(near, ("lat", "lon"), (-1, -1))
+    lon_halo = to_neighbour(side, ("lon",), (-1,))
 
     half = lon_count // CORES
     across = wide + width
@@ -558,7 +567,7 @@
         (upper, bottom, side, struct((half, 8, across)), struct((half, 8, across), bf16)),
         "second",
         [place],
-        [tokens, cotangent, lat_halo, right_halo, *params, add, *prior],
+        [tokens, cotangent, lat_halo, corner, lon_halo, *params, add, *prior],
         [tiles, tiles, pltpu.VMEM(d_bias, f32), pltpu.VMEM((CORES, half, 8, across), f32)],
     )
 

time: 96.2 us -> 93.7 us (0.974)
  starting transfers between devices: 55.7 us -> 53.2 us
    all_to_all x1, starting transfers between devices: 7.86 us -> 3.53 us  [local(): by_lat = lax.all_to_all(pair, 'lat', 0, 0)]
    ppermute x0 -> x1, starting transfers between devices: none -> 3.29 us  [to_neighbour(): return lax.ppermute(value, axes, pairs)]
    all_to_all x1, starting transfers between devices: 6.8 us -> 5.57 us  [local(): pair = lax.all_to_all(pair, 'lon', 0, 0, axis_index_groups=same_core())]
  transfers between devices with their start and end apart: 9 -> 10, of which waited for: 6 -> 6; matrix products, arithmetic and copies ran while one was open for 0% -> 0% of each run, Pallas kernels for 5% -> 5%
where the time goes in v6:
time: 93.7 us; the launch traced here: 93 us
  starting transfers between devices  53.2 us (57%)
  waiting for transfers between devices  25.1 us (27%)
  Pallas kernels  11.9 us (13%)
  local copies, waits for them, and re-layouts  1.67 us (2%)
  between operations  0.94 us (1%)
    ppermute x4, starting transfers between devices, to_neighbour(): lax.ppermute(value, axes[0], [(i, (i + steps[0]) % n) for i in range(n)])  25.2 us
    pallas_call x9, Pallas kernels, call(): pl.pallas_call(kernel, out_shape=out_shape, in_specs=[smem] * len(scalars...  11.9 us
    ppermute x4, waiting for transfers between devices, to_neighbour(): lax.ppermute(value, axes[0], [(i, (i + steps[0]) % n) for i in range(n)])  10.2 us
    ppermute x2, starting transfers between devices, swap_cores(): return lax.ppermute(value, 'lon', [(i, i ^ 1) for i in range(count)])  8.58 us
    all_to_all x1, waiting for transfers between devices, local(): mine = lax.all_to_all(mine, 'lon', 0, 0, axis_index_groups=same_core())  8.23 us
    all_to_all x1, starting transfers between devices, local(): mine = lax.all_to_all(mine, 'lon', 0, 0, axis_index_groups=same_core())  6.97 us
    all_to_all x1, starting transfers between devices, local(): pair = lax.all_to_all(pair, 'lon', 0, 0, axis_index_groups=same_core())  5.57 us
    all_to_all x1, waiting for transfers between devices, local(): pair = lax.all_to_all(pair, 'lon', 0, 0, axis_index_groups=same_core())  4.6 us
  transfers between devices with their start and end apart: 10, of which 6 were waited for; matrix products, arithmetic and copies ran while one was open for 0% of the time, Pallas kernels for 5%

profile of v6, /device:TPU:1, one launch (start us, length us, event | category | flops | bytes accessed | tf_op | source)
XLA Modules:
  0.0 93.0 jit_solution(6862437045515353145)
XLA Ops:
  0.7 0.9 %slice.30.tokens_ref = bf16[2,3,24,192]{3,2,1,0:T(8,128)(2,1)S(1)} slice(bf16[2,6,24,192]{3,2,1,0:T(8,128)(2,1)} %own.3), slice={[0:2], [0:3], [0:24], [0:192]} | slice | bytes 110592 | tf_op jit(solution)/shard_map/slice | solution.py:521
  1.6 0.1 cut.1
  1.7 13.8 %collective-permute-start = (bf16[2,3,3,18,128]{4,3,2,1,0:T(8,128)(2,1)S(1)}, bf16[2,3,3,18,128]{4,3,2,1,0:T(8,128)(2,1)S(1)}, u32[]{:S(2)}, u32[]{:S(2)}) collective-permute-start(bf16[2,3,3,18,128]{4,3,2,1,0:T(8,128)(2,1)S(1)} %get-tuple-element.53), channel_id=1, source_target_pairs={{0,480},{32,0},{64,32},{96,64},{128,96},{160,128},{192,160},{224,1... | collective-permute-start | bytes 248840 | tf_op jit(solution)/shard_map/ppermute | solution.py:490
  15.6 0.1 maximum_bitcast_fusion
  15.8 0.1 pad_add_fusion.place_ref.refs_0_
  15.9 0.4 copy-done.7
  16.3 0.2 copy-done.5
  16.4 0.1 copy-done.6
  16.5 1.4 %bias.1 = (f32[864,144]{1,0:T(8,128)S(1)}, f32[1,192]{1,0:T(1,128)S(1)}, f32[1,192]{1,0:T(1,128)S(1)}, bf16[192,576]{1,0:T(8,128)(2,1)S(1)}, f32[1,576]{1,0:T(1,...) custom-call(s32[2]{0:T(128)S(1)} %pad_add_fusion.place_ref.refs_0_, s32[96]{0:T(128)S(1)} %copy-done.9, ...), custom_call_target="tpu_custom_call" | custom-call | tf_op jit(solution)/shard_map/bias/pallas_call | solution.py:457
  17.9 3.3 %collective-permute-start.1 = (bf16[2,3,3,6,128]{4,3,2,1,0:T(8,128)(2,1)S(1)}, bf16[2,3,3,6,128]{4,3,2,1,0:T(8,128)(2,1)S(1)}, u32[]{:S(2)}, u32[]{:S(2)}) collective-permute-start(bf16[2,3,3,6,128]{4,3,2,1,0:T(8,128)(2,1)S(1)} %get-tuple-element.56), channel_id=1, source_target_pairs={{0,511},{1,480},{2,481},{3,482},{4,483},{5,484},{6,485},{7,486},{8... | collective-permute-start | bytes 82952 | tf_op jit(solution)/shard_map/ppermute | solution.py:497
  21.2 4.4 %collective-permute-start.2 = (bf16[2,3,3,6,128]{4,3,2,1,0:T(8,128)(2,1)S(1)}, bf16[2,3,3,6,128]{4,3,2,1,0:T(8,128)(2,1)S(1)}, u32[]{:S(2)}, u32[]{:S(2)}) collective-permute-start(bf16[2,3,3,6,128]{4,3,2,1,0:T(8,128)(2,1)S(1)} %pad_maximum_fusion.1), channel_id=1, source_target_pairs={{0,31},{1,0},{2,1},{3,2},{4,3},{5,4},{6,5},{7,6},{8,7},{9,8},{10,9... | collective-permute-start | bytes 82952 | tf_op jit(solution)/shard_map/ppermute | solution.py:490
  25.6 2.3 %first.1 = (f32[2,2,3,12,192]{4,3,2,1,0:T(8,128)S(1)}, bf16[2,3,3,12,128]{4,3,2,1,0:T(8,128)(2,1)S(1)}, f32[864,144]{1,0:T(8,128)S(1)}, f32[192,768]{1,0:T(8,128)S(1)}, f32[1,1152]{1,0:T(1,128)S(1)}) custom-call(bf16[2,6,24,192]{3,2,1,0:T(8,128)(2,1)S(1)} %copy-done, bf16[2,6,24,192]{3,2,1,0:T(8,128)(2,1)S(1)} %copy-done.1, ...), custom_call_target="tpu_custom_call" | custom-call | tf_op jit(solution)/shard_map/first/pallas_call | solution.py:457
  27.9 3.1 %second.1 = (f32[2,2,3,12,192]{4,3,2,1,0:T(8,128)S(1)}, bf16[2,3,3,12,128]{4,3,2,1,0:T(8,128)(2,1)S(1)}, bf16[2,6,3,6,128]{4,3,2,1,0:T(8,128)(2,1)S(1)}, f32[16,...) custom-call(s32[2]{0:T(128)S(1)} %pad_add_fusion.place_ref.refs_0_, bf16[2,6,24,192]{3,2,1,0:T(8,128)(2,1)S(1)} %copy-done, ...), custom_call_target="tpu_custom_call" | custom-call | tf_op jit(solution)/shard_map/second/pallas_call | solution.py:457
  31.0 3.9 %collective-permute-start.3 = (bf16[16,8,768]{2,1,0:T(8,128)(2,1)S(1)}, bf16[16,8,768]{2,1,0:T(8,128)(2,1)S(1)}, u32[]{:S(2)}, u32[]{:S(2)}) collective-permute-start(bf16[16,8,768]{2,1,0:T(8,128)(2,1)S(1)} %get-tuple-element.69), channel_id=1, source_target_pairs={{0,1},{1,0},{2,3},{3,2},{4,5},{5,4},{6,7},{7,6},{8,9},{9,8},{10,11... | collective-permute-start | bytes 589832 | tf_op jit(solution)/shard_map/ppermute | solution.py:478
  35.0 1.0 %collective-permute-done.3.other_ref = bf16[16,8,768]{2,1,0:T(8,128)(2,1)S(1)} collective-permute-done((bf16[16,8,768]{2,1,0:T(8,128)(2,1)S(1)}, bf16[16,8,768]{2,1,0:T(8,128)(2,1)S(1)}, u32[]{:S(2)}, u32[]{:S(2)}) %collective-permute-start.3) | collective-permute-done | bytes 196640 | tf_op jit(solution)/shard_map/ppermute | solution.py:478
  36.0 0.7 pair.1
  36.7 5.6 %all-to-all-start = ((bf16[16,8,768]{2,1,0:T(8,128)(2,1)}), bf16[16,8,768]{2,1,0:T(8,128)(2,1)S(1)}, u32[]{:S(2)}, u32[]{:S(2)}) async-start(bf16[16,8,768]{2,1,0:T(8,128)(2,1)} %pair.1), calls=%async_computation | async-start | bytes 393216 | tf_op jit(solution)/shard_map/all_to_all | solution.py:577
  42.3 3.9 %collective-permute-start.4 = (bf16[2,6,3,6,128]{4,3,2,1,0:T(8,128)(2,1)S(1)}, bf16[2,6,3,6,128]{4,3,2,1,0:T(8,128)(2,1)S(1)}, u32[]{:S(2)}, u32[]{:S(2)}) collective-permute-start(bf16[2,6,3,6,128]{4,3,2,1,0:T(8,128)(2,1)S(1)} %get-tuple-element.70), channel_id=1, source_target_pairs={{0,1},{1,2},{2,3},{3,4},{4,5},{5,6},{6,7},{7,8},{8,9},{9,10},{10,1... | collective-permute-start | bytes 165896 | tf_op jit(solution)/shard_map/ppermute | solution.py:490
  46.2 1.5 %collective-permute-done.4.left_ref = bf16[2,6,3,6,128]{4,3,2,1,0:T(8,128)(2,1)S(1)} collective-permute-done((bf16[2,6,3,6,128]{4,3,2,1,0:T(8,128)(2,1)S(1)}, bf16[2,6,3,6,128]{4,3,2,1,0:T(8,128)(2,1)S(1)}, u32[]{:S(2)}, u32[]{:S(2)}) %collective-permute-start.4) | collective-permute-done | bytes 55328 | tf_op jit(solution)/shard_map/ppermute | solution.py:490
  47.7 4.6 %all-to-all-done.pieces_ref = bf16[16,8,768]{2,1,0:T(8,128)(2,1)S(1)} async-done(((bf16[16,8,768]{2,1,0:T(8,128)(2,1)}), bf16[16,8,768]{2,1,0:T(8,128)(2,1)S(1)}, u32[]{:S(2)}, u32[]{:S(2)}) %all-to-all-start) | async-done | bytes 196640 | tf_op jit(solution)/shard_map/all_to_all | solution.py:577
  52.3 0.8 lon.1
  53.1 3.5 %all-to-all-start.1 = ((bf16[16,8,768]{2,1,0:T(8,128)(2,1)}), bf16[16,8,768]{2,1,0:T(8,128)(2,1)S(1)}, u32[]{:S(2)}, u32[]{:S(2)}) async-start(bf16[16,8,768]{2,1,0:T(8,128)(2,1)} %get-tuple-element.72), calls=%async_computation.1 | async-start | bytes 393216 | tf_op jit(solution)/shard_map/all_to_all | solution.py:589
  56.7 0.1 pad_maximum_fusion
  56.7 3.1 %collective-permute-start.5 = (bf16[2,3,3,24,128]{4,3,2,1,0:T(8,128)(2,1)S(1)}, bf16[2,3,3,24,128]{4,3,2,1,0:T(8,128)(2,1)S(1)}, u32[]{:S(2)}, u32[]{:S(2)}) collective-permute-start(bf16[2,3,3,24,128]{4,3,2,1,0:T(8,128)(2,1)S(1)} %pad_maximum_fusion), channel_id=1, source_target_pairs={{0,32},{32,64},{64,96},{96,128},{128,160},{160,192},{192,224},{224... | collective-permute-start | bytes 331784 | tf_op jit(solution)/shard_map/ppermute | solution.py:490
  59.9 8.7 %collective-permute-done.5.top_ref = bf16[2,3,3,24,128]{4,3,2,1,0:T(8,128)(2,1)S(1)} collective-permute-done((bf16[2,3,3,24,128]{4,3,2,1,0:T(8,128)(2,1)S(1)}, bf16[2,3,3,24,128]{4,3,2,1,0:T(8,128)(2,1)S(1)}, u32[]{:S(2)}, u32[]{:S(2)}) %collective-permute-start.5) | collective-permute-done | bytes 110624 | tf_op jit(solution)/shard_map/ppermute | solution.py:490
  68.6 0.8 lat.1
  69.5 7.0 %all-to-all-start.2 = ((bf16[16,8,768]{2,1,0:T(8,128)(2,1)}), bf16[16,8,768]{2,1,0:T(8,128)(2,1)S(1)}, u32[]{:S(2)}, u32[]{:S(2)}) async-start(bf16[16,8,768]{2,1,0:T(8,128)(2,1)} %lat.1), calls=%async_computation.2 | async-start | bytes 393216 | tf_op jit(solution)/shard_map/all_to_all | solution.py:607
  76.5 0.9 owned.1
  77.3 8.2 %all-to-all-done.2.refs_1_ = bf16[16,8,768]{2,1,0:T(8,128)(2,1)S(1)} async-done(((bf16[16,8,768]{2,1,0:T(8,128)(2,1)}), bf16[16,8,768]{2,1,0:T(8,128)(2,1)S(1)}, u32[]{:S(2)}, u32[]{:S(2)}) %all-to-all-start.2) | async-done | bytes 196640 | tf_op jit(solution)/shard_map/all_to_all | solution.py:607
  85.5 4.6 %collective-permute-start.6 = (bf16[16,8,768]{2,1,0:T(8,128)(2,1)S(1)}, bf16[16,8,768]{2,1,0:T(8,128)(2,1)S(1)}, u32[]{:S(2)}, u32[]{:S(2)}) collective-permute-start(bf16[16,8,768]{2,1,0:T(8,128)(2,1)S(1)} %all-to-all-done.2.refs_1_), channel_id=1, source_target_pairs={{0,1},{1,0},{2,3},{3,2},{4,5},{5,4},{6,7},{7,6},{8,9},{9,8},{10,11... | collective-permute-start | bytes 589832 | tf_op jit(solution)/shard_map/ppermute | solution.py:478
  90.2 1.0 %collective-permute-done.6.refs_2_ = bf16[16,8,768]{2,1,0:T(8,128)(2,1)S(1)} collective-permute-done((bf16[16,8,768]{2,1,0:T(8,128)(2,1)S(1)}, bf16[16,8,768]{2,1,0:T(8,128)(2,1)S(1)}, u32[]{:S(2)}, u32[]{:S(2)}) %collective-permute-start.6) | collective-permute-done | bytes 196640 | tf_op jit(solution)/shard_map/ppermute | solution.py:478
  91.2 1.7 %unpack.1 = (f32[192,576]{1,0:T(8,128)}, f32[192,192]{1,0:T(8,128)}, f32[1,6,1,3312]{3,2,1,0:T(1,128)}, f32[1,192]{1,0:T(1,128)}, f32[1,192]{1,0:T(1,128)}, /*index=5*/f32[576]{0:T(1024)}, f32[1,192]{1,0:T(1,128)}) custom-call(s32[2]{0:T(128)S(1)} %pad_add_fusion.place_ref.refs_0_, bf16[16,8,768]{2,1,0:T(8,128)(2,1)S(1)} %all-to-all-done.2.refs_1_, ...), custom_call_target="tpu_custom_call" | custom-call | tf_op jit(solution)/shard_map/unpack/pallas_call | solution.py:457
  (28 shorter events, 0.1 us)
Async XLA Ops:
  0.6 0.9 %copy-start.1 = (bf16[2,6,24,192]{3,2,1,0:T(8,128)(2,1)S(1)}, bf16[2,6,24,192]{3,2,1,0:T(8,128)(2,1)}, u32[]{:S(2)}) copy-start(bf16[2,6,24,192]{3,2,1,0:T(8,128)(2,1)} %cot.3) | copy-start | bytes 331780
  1.6 14.0 %copy-start = (bf16[2,6,24,192]{3,2,1,0:T(8,128)(2,1)S(1)}, bf16[2,6,24,192]{3,2,1,0:T(8,128)(2,1)}, u32[]{:S(2)}) copy-start(bf16[2,6,24,192]{3,2,1,0:T(8,128)(2,1)} %own.3) | copy-start | bytes 331780
  1.6 14.2 %copy-start.3 = (bf16[192,192]{1,0:T(8,128)(2,1)S(1)}, bf16[192,192]{1,0:T(8,128)(2,1)}, u32[]{:S(2)}) copy-start(bf16[192,192]{1,0:T(8,128)(2,1)} %rest_4_.1) | copy-start | bytes 221188
  1.6 14.2 %copy-start.4 = (f32[1,1,6,3312]{3,1,2,0:T(1,128)S(1)}, f32[1,1,6,3312]{3,1,2,0:T(1,128)}, u32[]{:S(2)}) copy-start(f32[1,1,6,3312]{3,1,2,0:T(1,128)} %param.18) | copy-start | bytes 238468
  1.7 14.1 %copy-start.2 = (bf16[192,576]{1,0:T(8,128)(2,1)S(1)}, bf16[192,576]{1,0:T(8,128)(2,1)}, u32[]{:S(2)}) copy-start(bf16[192,576]{1,0:T(8,128)(2,1)} %rest_2_.1) | copy-start | bytes 663556
  1.7 23.8 %collective-permute-start = (bf16[2,3,3,18,128]{4,3,2,1,0:T(8,128)(2,1)S(1)}, bf16[2,3,3,18,128]{4,3,2,1,0:T(8,128)(2,1)S(1)}, u32[]{:S(2)}, u32[]{:S(2)}) collective-permute-start(bf16[2,3,3,18,128]{4,3,2,1,0:T(8,128)(2,1)S(1)} %get-tuple-element.53), channel_id=1, source_target_pairs={{0,480},{32,0},{64,32},{96,64},{128,96},{160,128},{192,160},{224,1... | collective-permute-start | bytes 248840 | tf_op jit(solution)/shard_map/ppermute | solution.py:490
  15.6 0.7 copy-start.7
  15.6 0.7 copy-start.8
  15.7 0.7 copy-start.5
  15.8 0.7 copy-start.6
  15.8 0.7 copy-start.9
  17.9 10.1 %collective-permute-start.1 = (bf16[2,3,3,6,128]{4,3,2,1,0:T(8,128)(2,1)S(1)}, bf16[2,3,3,6,128]{4,3,2,1,0:T(8,128)(2,1)S(1)}, u32[]{:S(2)}, u32[]{:S(2)}) collective-permute-start(bf16[2,3,3,6,128]{4,3,2,1,0:T(8,128)(2,1)S(1)} %get-tuple-element.56), channel_id=1, source_target_pairs={{0,511},{1,480},{2,481},{3,482},{4,483},{5,484},{6,485},{7,486},{8... | collective-permute-start | bytes 82952 | tf_op jit(solution)/shard_map/ppermute | solution.py:497
  21.2 6.8 %collective-permute-start.2 = (bf16[2,3,3,6,128]{4,3,2,1,0:T(8,128)(2,1)S(1)}, bf16[2,3,3,6,128]{4,3,2,1,0:T(8,128)(2,1)S(1)}, u32[]{:S(2)}, u32[]{:S(2)}) collective-permute-start(bf16[2,3,3,6,128]{4,3,2,1,0:T(8,128)(2,1)S(1)} %pad_maximum_fusion.1), channel_id=1, source_target_pairs={{0,31},{1,0},{2,1},{3,2},{4,3},{5,4},{6,5},{7,6},{8,7},{9,8},{10,9... | collective-permute-start | bytes 82952 | tf_op jit(solution)/shard_map/ppermute | solution.py:490
  31.0 5.0 %collective-permute-start.3 = (bf16[16,8,768]{2,1,0:T(8,128)(2,1)S(1)}, bf16[16,8,768]{2,1,0:T(8,128)(2,1)S(1)}, u32[]{:S(2)}, u32[]{:S(2)}) collective-permute-start(bf16[16,8,768]{2,1,0:T(8,128)(2,1)S(1)} %get-tuple-element.69), channel_id=1, source_target_pairs={{0,1},{1,0},{2,3},{3,2},{4,5},{5,4},{6,7},{7,6},{8,9},{9,8},{10,11... | collective-permute-start | bytes 589832 | tf_op jit(solution)/shard_map/ppermute | solution.py:478
  36.7 15.5 %all-to-all-start = ((bf16[16,8,768]{2,1,0:T(8,128)(2,1)}), bf16[16,8,768]{2,1,0:T(8,128)(2,1)S(1)}, u32[]{:S(2)}, u32[]{:S(2)}) async-start(bf16[16,8,768]{2,1,0:T(8,128)(2,1)} %pair.1), calls=%async_computation | async-start | bytes 393216 | tf_op jit(solution)/shard_map/all_to_all | solution.py:577
  42.3 5.3 %collective-permute-start.4 = (bf16[2,6,3,6,128]{4,3,2,1,0:T(8,128)(2,1)S(1)}, bf16[2,6,3,6,128]{4,3,2,1,0:T(8,128)(2,1)S(1)}, u32[]{:S(2)}, u32[]{:S(2)}) collective-permute-start(bf16[2,6,3,6,128]{4,3,2,1,0:T(8,128)(2,1)S(1)} %get-tuple-element.70), channel_id=1, source_target_pairs={{0,1},{1,2},{2,3},{3,4},{4,5},{5,6},{6,7},{7,8},{8,9},{9,10},{10,1... | collective-permute-start | bytes 165896 | tf_op jit(solution)/shard_map/ppermute | solution.py:490
  53.1 15.5 %all-to-all-start.1 = ((bf16[16,8,768]{2,1,0:T(8,128)(2,1)}), bf16[16,8,768]{2,1,0:T(8,128)(2,1)S(1)}, u32[]{:S(2)}, u32[]{:S(2)}) async-start(bf16[16,8,768]{2,1,0:T(8,128)(2,1)} %get-tuple-element.72), calls=%async_computation.1 | async-start | bytes 393216 | tf_op jit(solution)/shard_map/all_to_all | solution.py:589
  56.7 11.9 %collective-permute-start.5 = (bf16[2,3,3,24,128]{4,3,2,1,0:T(8,128)(2,1)S(1)}, bf16[2,3,3,24,128]{4,3,2,1,0:T(8,128)(2,1)S(1)}, u32[]{:S(2)}, u32[]{:S(2)}) collective-permute-start(bf16[2,3,3,24,128]{4,3,2,1,0:T(8,128)(2,1)S(1)} %pad_maximum_fusion), channel_id=1, source_target_pairs={{0,32},{32,64},{64,96},{96,128},{128,160},{160,192},{192,224},{224... | collective-permute-start | bytes 331784 | tf_op jit(solution)/shard_map/ppermute | solution.py:490
  69.5 16.1 %all-to-all-start.2 = ((bf16[16,8,768]{2,1,0:T(8,128)(2,1)}), bf16[16,8,768]{2,1,0:T(8,128)(2,1)S(1)}, u32[]{:S(2)}, u32[]{:S(2)}) async-start(bf16[16,8,768]{2,1,0:T(8,128)(2,1)} %lat.1), calls=%async_computation.2 | async-start | bytes 393216 | tf_op jit(solution)/shard_map/all_to_all | solution.py:607
  85.5 5.7 %collective-permute-start.6 = (bf16[16,8,768]{2,1,0:T(8,128)(2,1)S(1)}, bf16[16,8,768]{2,1,0:T(8,128)(2,1)S(1)}, u32[]{:S(2)}, u32[]{:S(2)}) collective-permute-start(bf16[16,8,768]{2,1,0:T(8,128)(2,1)S(1)} %all-to-all-done.2.refs_1_), channel_id=1, source_target_pairs={{0,1},{1,0},{2,3},{3,2},{4,5},{5,4},{6,7},{7,6},{8,9},{9,8},{10,11... | collective-permute-start | bytes 589832 | tf_op jit(solution)/shard_map/ppermute | solution.py:478

commit v7 on v6

--- a/solution.py
+++ b/solution.py
@@ -215,12 +215,9 @@
     sum_ref[...] = (mine_ref[...] + other_ref[...].astype(f32)).astype(bf16)
 
 
-def spread(piece_ref, out_ref, sem):
-    copies = [pltpu.make_async_copy(piece_ref, out_ref.at[d], sem.at[d]) for d in range(out_ref.shape[0])]
-    for copy in copies:
-        copy.start()
-    for copy in copies:
-        copy.wait()
+def spread(piece, out_ref):
+    for d in range(out_ref.shape[0]):
+        out_ref[d] = piece
 
 
 def sum_pieces(pieces_ref):
@@ -230,19 +227,19 @@
     return total
 
 
-def lon_kernel(pieces_ref, piece_ref, out_ref, sem):
-    piece_ref[...] = sum_pieces(pieces_ref).astype(bf16)
-    spread(piece_ref, out_ref, sem)
-
-
-def lat_kernel(rows, pieces_ref, by_lon_ref, out_ref, piece_ref, sem):
-    shape = piece_ref.shape
+def lon_kernel(pieces_ref, piece_ref, out_ref):
+    piece = sum_pieces(pieces_ref).astype(bf16)
+    piece_ref[...] = piece
+    spread(piece, out_ref)
+
+
+def lat_kernel(rows, pieces_ref, by_lon_ref, out_ref):
+    shape = by_lon_ref.shape
     row = lax.broadcasted_iota(jnp.int32, shape, 0)
     column = lax.broadcasted_iota(jnp.int32, shape, 1)
     is_table = (row >= rows) & (column < 5 * LANES)
     total = jnp.where(is_table, by_lon_ref[...].astype(f32), sum_pieces(pieces_ref))
-    piece_ref[...] = total.astype(bf16)
-    spread(piece_ref, out_ref, sem)
+    spread(total.astype(bf16), out_ref)
 
 
 def attend(
@@ -583,14 +580,11 @@
         "lon",
         [],
         [pair],
-        [pltpu.SemaphoreType.DMA((lat_count,))],
-        out_spaces=(pltpu.VMEM, pl.ANY),
     )
     by_lat = lax.all_to_all(pair, "lat", 0, 0)
     inner = rows - HALF_LAT
     bottom = [left[:, inner:], bottom_a, bottom_b[:, :, :, :HALF_LON]]
     top = to_neighbour(jnp.concatenate(bottom, axis=3), ("lat",), (1,))
-    by_lat, top = lax.optimization_barrier((by_lat, top))
 
     def lat_sum(*refs):
         lat_kernel(width // lon_count, *refs)
@@ -601,8 +595,6 @@
         "lat",
         [],
         [by_lat, by_lon],
-        [pltpu.VMEM((8, across), bf16), pltpu.SemaphoreType.DMA((half,))],
-        out_spaces=pl.ANY,
     )
     mine = lax.all_to_all(mine, "lon", 0, 0, axis_index_groups=same_core())
     block_out, token_grad = call(
@@ -611,6 +603,7 @@
         "owned",
         [],
         [top, left, upper_a, upper_b],
+        cost=pl.CostEstimate(flops=5000000000, bytes_accessed=2_000_000, transcendentals=0),
     )
     mine, block_out, token_grad = lax.optimization_barrier((mine, block_out, token_grad))
     other = swap_cores(mine)

time: 93.7 us -> 91 us (0.971)
  waiting for transfers between devices: 25.1 us -> 22.8 us
    ppermute x4, waiting for transfers between devices: 10.2 us -> 1.47 us  [to_neighbour(): lax.ppermute(value, axes[0], [(i, (i + steps[0]) % n) for i in range(n)])]
    all_to_all x1, waiting for transfers between devices: 0.01 us -> 6.45 us  [local(): by_lat = lax.all_to_all(pair, 'lat', 0, 0)]
    all_to_all x1, starting transfers between devices: 6.97 us -> 3.55 us  [local(): mine = lax.all_to_all(mine, 'lon', 0, 0, axis_index_groups=same_core())]
    ppermute x2, starting transfers between devices: 8.58 us -> 11.9 us  [swap_cores(): return lax.ppermute(value, 'lon', [(i, i ^ 1) for i in range(count)])]
  transfers between devices with their start and end apart: 10 -> 10, of which waited for: 6 -> 6; matrix products, arithmetic and copies ran while one was open for 0% -> 0% of each run, Pallas kernels for 5% -> 6%
where the time goes in v7:
time: 91 us; the launch traced here: 90.3 us
  starting transfers between devices  53.1 us (58%)
  waiting for transfers between devices  22.8 us (25%)
  Pallas kernels  11.6 us (13%)
  local copies, waits for them, and re-layouts  1.67 us (2%)
  between operations  0.94 us (1%)
    ppermute x4, starting transfers between devices, to_neighbour(): lax.ppermute(value, axes[0], [(i, (i + steps[0]) % n) for i in range(n)])  25.2 us
    ppermute x2, starting transfers between devices, swap_cores(): return lax.ppermute(value, 'lon', [(i, i ^ 1) for i in range(count)])  11.9 us
    pallas_call x9, Pallas kernels, call(): pl.pallas_call(kernel, out_shape=out_shape, in_specs=[smem] * len(scalars...  11.6 us
    all_to_all x1, waiting for transfers between devices, local(): mine = lax.all_to_all(mine, 'lon', 0, 0, axis_index_groups=same_core())  8.17 us
    all_to_all x1, waiting for transfers between devices, local(): by_lat = lax.all_to_all(pair, 'lat', 0, 0)  6.45 us
    all_to_all x1, starting transfers between devices, local(): pair = lax.all_to_all(pair, 'lon', 0, 0, axis_index_groups=same_core())  5.59 us
    all_to_all x1, waiting for transfers between devices, local(): pair = lax.all_to_all(pair, 'lon', 0, 0, axis_index_groups=same_core())  4.6 us
    all_to_all x1, starting transfers between devices, local(): mine = lax.all_to_all(mine, 'lon', 0, 0, axis_index_groups=same_core())  3.55 us
  transfers between devices with their start and end apart: 10, of which 6 were waited for; matrix products, arithmetic and copies ran while one was open for 0% of the time, Pallas kernels for 6%

profile of v7, /device:TPU:1, one launch (start us, length us, event | category | flops | bytes accessed | tf_op | source)
XLA Modules:
  0.0 90.3 jit_solution(11217331283869527175)
XLA Ops:
  0.7 0.9 %slice.30.tokens_ref = bf16[2,3,24,192]{3,2,1,0:T(8,128)(2,1)S(1)} slice(bf16[2,6,24,192]{3,2,1,0:T(8,128)(2,1)} %own.3), slice={[0:2], [0:3], [0:24], [0:192]} | slice | bytes 110592 | tf_op jit(solution)/shard_map/slice | solution.py:518
  1.6 0.1 cut.1
  1.7 13.8 %collective-permute-start = (bf16[2,3,3,18,128]{4,3,2,1,0:T(8,128)(2,1)S(1)}, bf16[2,3,3,18,128]{4,3,2,1,0:T(8,128)(2,1)S(1)}, u32[]{:S(2)}, u32[]{:S(2)}) collective-permute-start(bf16[2,3,3,18,128]{4,3,2,1,0:T(8,128)(2,1)S(1)} %get-tuple-element.51), channel_id=1, source_target_pairs={{0,480},{32,0},{64,32},{96,64},{128,96},{160,128},{192,160},{224,1... | collective-permute-start | bytes 248840 | tf_op jit(solution)/shard_map/ppermute | solution.py:487
  15.6 0.1 maximum_bitcast_fusion
  15.8 0.1 pad_add_fusion.place_ref.refs_0_
  15.9 0.4 copy-done.7
  16.3 0.2 copy-done.5
  16.4 0.1 copy-done.6
  16.5 1.4 %bias.1 = (f32[864,144]{1,0:T(8,128)S(1)}, f32[1,192]{1,0:T(1,128)S(1)}, f32[1,192]{1,0:T(1,128)S(1)}, bf16[192,576]{1,0:T(8,128)(2,1)S(1)}, f32[1,576]{1,0:T(1,...) custom-call(s32[2]{0:T(128)S(1)} %pad_add_fusion.place_ref.refs_0_, s32[96]{0:T(128)S(1)} %copy-done.9, ...), custom_call_target="tpu_custom_call" | custom-call | tf_op jit(solution)/shard_map/bias/pallas_call | solution.py:454
  17.9 3.3 %collective-permute-start.1 = (bf16[2,3,3,6,128]{4,3,2,1,0:T(8,128)(2,1)S(1)}, bf16[2,3,3,6,128]{4,3,2,1,0:T(8,128)(2,1)S(1)}, u32[]{:S(2)}, u32[]{:S(2)}) collective-permute-start(bf16[2,3,3,6,128]{4,3,2,1,0:T(8,128)(2,1)S(1)} %get-tuple-element.54), channel_id=1, source_target_pairs={{0,511},{1,480},{2,481},{3,482},{4,483},{5,484},{6,485},{7,486},{8... | collective-permute-start | bytes 82952 | tf_op jit(solution)/shard_map/ppermute | solution.py:494
  21.2 4.4 %collective-permute-start.2 = (bf16[2,3,3,6,128]{4,3,2,1,0:T(8,128)(2,1)S(1)}, bf16[2,3,3,6,128]{4,3,2,1,0:T(8,128)(2,1)S(1)}, u32[]{:S(2)}, u32[]{:S(2)}) collective-permute-start(bf16[2,3,3,6,128]{4,3,2,1,0:T(8,128)(2,1)S(1)} %pad_maximum_fusion.1), channel_id=1, source_target_pairs={{0,31},{1,0},{2,1},{3,2},{4,3},{5,4},{6,5},{7,6},{8,7},{9,8},{10,9... | collective-permute-start | bytes 82952 | tf_op jit(solution)/shard_map/ppermute | solution.py:487
  25.6 2.3 %first.1 = (f32[2,2,3,12,192]{4,3,2,1,0:T(8,128)S(1)}, bf16[2,3,3,12,128]{4,3,2,1,0:T(8,128)(2,1)S(1)}, f32[864,144]{1,0:T(8,128)S(1)}, f32[192,768]{1,0:T(8,128)S(1)}, f32[1,1152]{1,0:T(1,128)S(1)}) custom-call(bf16[2,6,24,192]{3,2,1,0:T(8,128)(2,1)S(1)} %copy-done, bf16[2,6,24,192]{3,2,1,0:T(8,128)(2,1)S(1)} %copy-done.1, ...), custom_call_target="tpu_custom_call" | custom-call | tf_op jit(solution)/shard_map/first/pallas_call | solution.py:454
  27.9 3.1 %second.1 = (f32[2,2,3,12,192]{4,3,2,1,0:T(8,128)S(1)}, bf16[2,3,3,12,128]{4,3,2,1,0:T(8,128)(2,1)S(1)}, bf16[2,6,3,6,128]{4,3,2,1,0:T(8,128)(2,1)S(1)}, f32[16,...) custom-call(s32[2]{0:T(128)S(1)} %pad_add_fusion.place_ref.refs_0_, bf16[2,6,24,192]{3,2,1,0:T(8,128)(2,1)S(1)} %copy-done, ...), custom_call_target="tpu_custom_call" | custom-call | tf_op jit(solution)/shard_map/second/pallas_call | solution.py:454
  31.0 3.9 %collective-permute-start.3 = (bf16[16,8,768]{2,1,0:T(8,128)(2,1)S(1)}, bf16[16,8,768]{2,1,0:T(8,128)(2,1)S(1)}, u32[]{:S(2)}, u32[]{:S(2)}) collective-permute-start(bf16[16,8,768]{2,1,0:T(8,128)(2,1)S(1)} %get-tuple-element.67), channel_id=1, source_target_pairs={{0,1},{1,0},{2,3},{3,2},{4,5},{5,4},{6,7},{7,6},{8,9},{9,8},{10,11... | collective-permute-start | bytes 589832 | tf_op jit(solution)/shard_map/ppermute | solution.py:475
  35.0 1.0 %collective-permute-done.3.other_ref = bf16[16,8,768]{2,1,0:T(8,128)(2,1)S(1)} collective-permute-done((bf16[16,8,768]{2,1,0:T(8,128)(2,1)S(1)}, bf16[16,8,768]{2,1,0:T(8,128)(2,1)S(1)}, u32[]{:S(2)}, u32[]{:S(2)}) %collective-permute-start.3) | collective-permute-done | bytes 196640 | tf_op jit(solution)/shard_map/ppermute | solution.py:475
  36.0 0.7 pair.1
  36.7 5.6 %all-to-all-start = ((bf16[16,8,768]{2,1,0:T(8,128)(2,1)}), bf16[16,8,768]{2,1,0:T(8,128)(2,1)S(1)}, u32[]{:S(2)}, u32[]{:S(2)}) async-start(bf16[16,8,768]{2,1,0:T(8,128)(2,1)} %pair.1), calls=%async_computation | async-start | bytes 393216 | tf_op jit(solution)/shard_map/all_to_all | solution.py:574
  42.3 3.9 %collective-permute-start.4 = (bf16[2,6,3,6,128]{4,3,2,1,0:T(8,128)(2,1)S(1)}, bf16[2,6,3,6,128]{4,3,2,1,0:T(8,128)(2,1)S(1)}, u32[]{:S(2)}, u32[]{:S(2)}) collective-permute-start(bf16[2,6,3,6,128]{4,3,2,1,0:T(8,128)(2,1)S(1)} %get-tuple-element.68), channel_id=1, source_target_pairs={{0,1},{1,2},{2,3},{3,4},{4,5},{5,6},{6,7},{7,8},{8,9},{9,10},{10,1... | collective-permute-start | bytes 165896 | tf_op jit(solution)/shard_map/ppermute | solution.py:487
  46.2 1.5 %collective-permute-done.4.left_ref = bf16[2,6,3,6,128]{4,3,2,1,0:T(8,128)(2,1)S(1)} collective-permute-done((bf16[2,6,3,6,128]{4,3,2,1,0:T(8,128)(2,1)S(1)}, bf16[2,6,3,6,128]{4,3,2,1,0:T(8,128)(2,1)S(1)}, u32[]{:S(2)}, u32[]{:S(2)}) %collective-permute-start.4) | collective-permute-done | bytes 55328 | tf_op jit(solution)/shard_map/ppermute | solution.py:487
  47.7 4.6 %all-to-all-done.pieces_ref = bf16[16,8,768]{2,1,0:T(8,128)(2,1)S(1)} async-done(((bf16[16,8,768]{2,1,0:T(8,128)(2,1)}), bf16[16,8,768]{2,1,0:T(8,128)(2,1)S(1)}, u32[]{:S(2)}, u32[]{:S(2)}) %all-to-all-start) | async-done | bytes 196640 | tf_op jit(solution)/shard_map/all_to_all | solution.py:574
  52.3 0.7 lon.1
  53.0 3.5 %all-to-all-start.1 = ((bf16[16,8,768]{2,1,0:T(8,128)(2,1)}), bf16[16,8,768]{2,1,0:T(8,128)(2,1)S(1)}, u32[]{:S(2)}, u32[]{:S(2)}) async-start(bf16[16,8,768]{2,1,0:T(8,128)(2,1)} %get-tuple-element.70), calls=%async_computation.1 | async-start | bytes 393216 | tf_op jit(solution)/shard_map/all_to_all | solution.py:584
  56.5 0.1 pad_maximum_fusion
  56.6 3.1 %collective-permute-start.5 = (bf16[2,3,3,24,128]{4,3,2,1,0:T(8,128)(2,1)S(1)}, bf16[2,3,3,24,128]{4,3,2,1,0:T(8,128)(2,1)S(1)}, u32[]{:S(2)}, u32[]{:S(2)}) collective-permute-start(bf16[2,3,3,24,128]{4,3,2,1,0:T(8,128)(2,1)S(1)} %pad_maximum_fusion), channel_id=1, source_target_pairs={{0,32},{32,64},{64,96},{96,128},{128,160},{160,192},{192,224},{224... | collective-permute-start | bytes 331784 | tf_op jit(solution)/shard_map/ppermute | solution.py:487
  59.8 6.4 %all-to-all-done.1.refs_0_ = bf16[16,8,768]{2,1,0:T(8,128)(2,1)S(1)} async-done(((bf16[16,8,768]{2,1,0:T(8,128)(2,1)}), bf16[16,8,768]{2,1,0:T(8,128)(2,1)S(1)}, u32[]{:S(2)}, u32[]{:S(2)}) %all-to-all-start.1) | async-done | bytes 196640 | tf_op jit(solution)/shard_map/all_to_all | solution.py:584
  66.2 0.7 lat.1
  66.9 3.5 %all-to-all-start.2 = ((bf16[16,8,768]{2,1,0:T(8,128)(2,1)}), bf16[16,8,768]{2,1,0:T(8,128)(2,1)S(1)}, u32[]{:S(2)}, u32[]{:S(2)}) async-start(bf16[16,8,768]{2,1,0:T(8,128)(2,1)} %lat.1), calls=%async_computation.2 | async-start | bytes 393216 | tf_op jit(solution)/shard_map/all_to_all | solution.py:599
  70.5 0.9 owned.1
  71.3 8.2 %all-to-all-done.2.refs_1_ = bf16[16,8,768]{2,1,0:T(8,128)(2,1)S(1)} async-done(((bf16[16,8,768]{2,1,0:T(8,128)(2,1)}), bf16[16,8,768]{2,1,0:T(8,128)(2,1)S(1)}, u32[]{:S(2)}, u32[]{:S(2)}) %all-to-all-start.2) | async-done | bytes 196640 | tf_op jit(solution)/shard_map/all_to_all | solution.py:599
  79.5 8.0 %collective-permute-start.6 = (bf16[16,8,768]{2,1,0:T(8,128)(2,1)S(1)}, bf16[16,8,768]{2,1,0:T(8,128)(2,1)S(1)}, u32[]{:S(2)}, u32[]{:S(2)}) collective-permute-start(bf16[16,8,768]{2,1,0:T(8,128)(2,1)S(1)} %all-to-all-done.2.refs_1_), channel_id=1, source_target_pairs={{0,1},{1,0},{2,3},{3,2},{4,5},{5,4},{6,7},{7,6},{8,9},{9,8},{10,11... | collective-permute-start | bytes 589832 | tf_op jit(solution)/shard_map/ppermute | solution.py:475
  87.5 1.0 %collective-permute-done.6.refs_2_ = bf16[16,8,768]{2,1,0:T(8,128)(2,1)S(1)} collective-permute-done((bf16[16,8,768]{2,1,0:T(8,128)(2,1)S(1)}, bf16[16,8,768]{2,1,0:T(8,128)(2,1)S(1)}, u32[]{:S(2)}, u32[]{:S(2)}) %collective-permute-start.6) | collective-permute-done | bytes 196640 | tf_op jit(solution)/shard_map/ppermute | solution.py:475
  88.6 1.7 %unpack.1 = (f32[192,576]{1,0:T(8,128)}, f32[192,192]{1,0:T(8,128)}, f32[1,6,1,3312]{3,2,1,0:T(1,128)}, f32[1,192]{1,0:T(1,128)}, f32[1,192]{1,0:T(1,128)}, /*index=5*/f32[576]{0:T(1024)}, f32[1,192]{1,0:T(1,128)}) custom-call(s32[2]{0:T(128)S(1)} %pad_add_fusion.place_ref.refs_0_, bf16[16,8,768]{2,1,0:T(8,128)(2,1)S(1)} %all-to-all-done.2.refs_1_, ...), custom_call_target="tpu_custom_call" | custom-call | tf_op jit(solution)/shard_map/unpack/pallas_call | solution.py:454
  (28 shorter events, 0.1 us)
Async XLA Ops:
  0.6 0.9 %copy-start.1 = (bf16[2,6,24,192]{3,2,1,0:T(8,128)(2,1)S(1)}, bf16[2,6,24,192]{3,2,1,0:T(8,128)(2,1)}, u32[]{:S(2)}) copy-start(bf16[2,6,24,192]{3,2,1,0:T(8,128)(2,1)} %cot.3) | copy-start | bytes 331780
  1.6 14.0 %copy-start = (bf16[2,6,24,192]{3,2,1,0:T(8,128)(2,1)S(1)}, bf16[2,6,24,192]{3,2,1,0:T(8,128)(2,1)}, u32[]{:S(2)}) copy-start(bf16[2,6,24,192]{3,2,1,0:T(8,128)(2,1)} %own.3) | copy-start | bytes 331780
  1.6 14.2 %copy-start.3 = (bf16[192,192]{1,0:T(8,128)(2,1)S(1)}, bf16[192,192]{1,0:T(8,128)(2,1)}, u32[]{:S(2)}) copy-start(bf16[192,192]{1,0:T(8,128)(2,1)} %rest_4_.1) | copy-start | bytes 221188
  1.6 14.2 %copy-start.4 = (f32[1,1,6,3312]{3,1,2,0:T(1,128)S(1)}, f32[1,1,6,3312]{3,1,2,0:T(1,128)}, u32[]{:S(2)}) copy-start(f32[1,1,6,3312]{3,1,2,0:T(1,128)} %param.18) | copy-start | bytes 238468
  1.7 14.1 %copy-start.2 = (bf16[192,576]{1,0:T(8,128)(2,1)S(1)}, bf16[192,576]{1,0:T(8,128)(2,1)}, u32[]{:S(2)}) copy-start(bf16[192,576]{1,0:T(8,128)(2,1)} %rest_2_.1) | copy-start | bytes 663556
  1.7 23.8 %collective-permute-start = (bf16[2,3,3,18,128]{4,3,2,1,0:T(8,128)(2,1)S(1)}, bf16[2,3,3,18,128]{4,3,2,1,0:T(8,128)(2,1)S(1)}, u32[]{:S(2)}, u32[]{:S(2)}) collective-permute-start(bf16[2,3,3,18,128]{4,3,2,1,0:T(8,128)(2,1)S(1)} %get-tuple-element.51), channel_id=1, source_target_pairs={{0,480},{32,0},{64,32},{96,64},{128,96},{160,128},{192,160},{224,1... | collective-permute-start | bytes 248840 | tf_op jit(solution)/shard_map/ppermute | solution.py:487
  15.6 0.7 copy-start.7
  15.6 0.7 copy-start.8
  15.7 0.7 copy-start.5
  15.8 0.7 copy-start.6
  15.8 0.7 copy-start.9
  17.9 10.0 %collective-permute-start.1 = (bf16[2,3,3,6,128]{4,3,2,1,0:T(8,128)(2,1)S(1)}, bf16[2,3,3,6,128]{4,3,2,1,0:T(8,128)(2,1)S(1)}, u32[]{:S(2)}, u32[]{:S(2)}) collective-permute-start(bf16[2,3,3,6,128]{4,3,2,1,0:T(8,128)(2,1)S(1)} %get-tuple-element.54), channel_id=1, source_target_pairs={{0,511},{1,480},{2,481},{3,482},{4,483},{5,484},{6,485},{7,486},{8... | collective-permute-start | bytes 82952 | tf_op jit(solution)/shard_map/ppermute | solution.py:494
  21.2 6.8 %collective-permute-start.2 = (bf16[2,3,3,6,128]{4,3,2,1,0:T(8,128)(2,1)S(1)}, bf16[2,3,3,6,128]{4,3,2,1,0:T(8,128)(2,1)S(1)}, u32[]{:S(2)}, u32[]{:S(2)}) collective-permute-start(bf16[2,3,3,6,128]{4,3,2,1,0:T(8,128)(2,1)S(1)} %pad_maximum_fusion.1), channel_id=1, source_target_pairs={{0,31},{1,0},{2,1},{3,2},{4,3},{5,4},{6,5},{7,6},{8,7},{9,8},{10,9... | collective-permute-start | bytes 82952 | tf_op jit(solution)/shard_map/ppermute | solution.py:487
  31.0 5.0 %collective-permute-start.3 = (bf16[16,8,768]{2,1,0:T(8,128)(2,1)S(1)}, bf16[16,8,768]{2,1,0:T(8,128)(2,1)S(1)}, u32[]{:S(2)}, u32[]{:S(2)}) collective-permute-start(bf16[16,8,768]{2,1,0:T(8,128)(2,1)S(1)} %get-tuple-element.67), channel_id=1, source_target_pairs={{0,1},{1,0},{2,3},{3,2},{4,5},{5,4},{6,7},{7,6},{8,9},{9,8},{10,11... | collective-permute-start | bytes 589832 | tf_op jit(solution)/shard_map/ppermute | solution.py:475
  36.7 15.5 %all-to-all-start = ((bf16[16,8,768]{2,1,0:T(8,128)(2,1)}), bf16[16,8,768]{2,1,0:T(8,128)(2,1)S(1)}, u32[]{:S(2)}, u32[]{:S(2)}) async-start(bf16[16,8,768]{2,1,0:T(8,128)(2,1)} %pair.1), calls=%async_computation | async-start | bytes 393216 | tf_op jit(solution)/shard_map/all_to_all | solution.py:574
  42.3 5.3 %collective-permute-start.4 = (bf16[2,6,3,6,128]{4,3,2,1,0:T(8,128)(2,1)S(1)}, bf16[2,6,3,6,128]{4,3,2,1,0:T(8,128)(2,1)S(1)}, u32[]{:S(2)}, u32[]{:S(2)}) collective-permute-start(bf16[2,6,3,6,128]{4,3,2,1,0:T(8,128)(2,1)S(1)} %get-tuple-element.68), channel_id=1, source_target_pairs={{0,1},{1,2},{2,3},{3,4},{4,5},{5,6},{6,7},{7,8},{8,9},{9,10},{10,1... | collective-permute-start | bytes 165896 | tf_op jit(solution)/shard_map/ppermute | solution.py:487
  53.0 13.2 %all-to-all-start.1 = ((bf16[16,8,768]{2,1,0:T(8,128)(2,1)}), bf16[16,8,768]{2,1,0:T(8,128)(2,1)S(1)}, u32[]{:S(2)}, u32[]{:S(2)}) async-start(bf16[16,8,768]{2,1,0:T(8,128)(2,1)} %get-tuple-element.70), calls=%async_computation.1 | async-start | bytes 393216 | tf_op jit(solution)/shard_map/all_to_all | solution.py:584
  56.6 13.9 %collective-permute-start.5 = (bf16[2,3,3,24,128]{4,3,2,1,0:T(8,128)(2,1)S(1)}, bf16[2,3,3,24,128]{4,3,2,1,0:T(8,128)(2,1)S(1)}, u32[]{:S(2)}, u32[]{:S(2)}) collective-permute-start(bf16[2,3,3,24,128]{4,3,2,1,0:T(8,128)(2,1)S(1)} %pad_maximum_fusion), channel_id=1, source_target_pairs={{0,32},{32,64},{64,96},{96,128},{128,160},{160,192},{192,224},{224... | collective-permute-start | bytes 331784 | tf_op jit(solution)/shard_map/ppermute | solution.py:487
  66.9 12.6 %all-to-all-start.2 = ((bf16[16,8,768]{2,1,0:T(8,128)(2,1)}), bf16[16,8,768]{2,1,0:T(8,128)(2,1)S(1)}, u32[]{:S(2)}, u32[]{:S(2)}) async-start(bf16[16,8,768]{2,1,0:T(8,128)(2,1)} %lat.1), calls=%async_computation.2 | async-start | bytes 393216 | tf_op jit(solution)/shard_map/all_to_all | solution.py:599
  79.5 9.1 %collective-permute-start.6 = (bf16[16,8,768]{2,1,0:T(8,128)(2,1)S(1)}, bf16[16,8,768]{2,1,0:T(8,128)(2,1)S(1)}, u32[]{:S(2)}, u32[]{:S(2)}) collective-permute-start(bf16[16,8,768]{2,1,0:T(8,128)(2,1)S(1)} %all-to-all-done.2.refs_1_), channel_id=1, source_target_pairs={{0,1},{1,0},{2,3},{3,2},{4,5},{5,4},{6,7},{7,6},{8,9},{9,8},{10,11... | collective-permute-start | bytes 589832 | tf_op jit(solution)/shard_map/ppermute | solution.py:475

commit v8 on v7

--- a/solution.py
+++ b/solution.py
@@ -44,7 +44,7 @@
 def to_tiles(tiles_ref, value):
     for t in range(tiles_ref.shape[0]):
         part = value[:, t * LANES : (t + 1) * LANES]
-        tiles_ref[t, :, : part.shape[1]] = part
+        tiles_ref[t, : part.shape[0], : part.shape[1]] = part
 
 
 def strided_rows(tiles_ref, start, count, stride):
@@ -151,7 +151,7 @@
                 line = [jnp.concatenate([p, e], axis=0) for p, e in zip(line, ends)]
             for t, part in enumerate(line):
                 tiles_ref[t, pl.ds(z * rows + r, WLON, stride=GROUP), :] = part
-    return jnp.concatenate([tiles_ref[0], tiles_ref[1]], axis=1)[:, :width]
+    return jnp.concatenate([tiles_ref[t, :COUNT, :] for t in range(2)], axis=1)[:, :width]
 
 
 def pack_line(packed_ref, at, kind, low, high):
@@ -405,7 +405,7 @@
         piece = wide_ref[d % cores, d // cores, 0:rows, :] * norm_by
         qkv_ref[d * rows : (d + 1) * rows, :] = piece[:, :wide]
         proj_ref[d * rows : (d + 1) * rows, :] = piece[:, wide:]
-    for p, (d, at, d2, at2) in enumerate(table_slots(pieces, skewed_ref.shape[1] // 2)):
+    for p, (d, at, d2, at2) in enumerate(table_slots(pieces, HEADS * GROUP // 2)):
         for t in range(2):
             lanes = slice(at + t * LANES, at + (t + 1) * LANES)
             skewed_ref[t, 2 * p : 2 * p + 2, :] = wide_ref[
@@ -531,13 +531,13 @@
     rows_of = [(1, p.size) if p.ndim == 1 else p.shape for p in params]
     add, *params = call(
         bias_kernel,
-        (struct((HEADS * COUNT, COUNT)), *[struct(r, p.dtype) for r, p in zip(rows_of, params)]),
+        (struct((HEADS * COUNT + 8, COUNT)), *[struct(r, p.dtype) for r, p in zip(rows_of, params)]),
         "bias",
         [place, lat_valid],
         [table, *params],
         [
             pltpu.VMEM((WZ, HEADS * GROUP, SIDE), f32),
-            pltpu.VMEM((SPREAD // LANES, HEADS * GROUP, LANES), f32),
+            pltpu.VMEM((SPREAD // LANES, 8 * GROUP, LANES), f32),
         ],
     )
     near, side, add = lax.optimization_barrier((near, side, add))
@@ -549,7 +549,7 @@
     upper = struct((2, levels, rows - HALF_LAT, WLON, width))
     bottom = packed(HALF_LAT, WLON)
     side = packed(rows, WLON - HALF_LON)
-    tiles = pltpu.VMEM((pl.cdiv(width, LANES), COUNT, LANES), f32)
+    tiles = pltpu.VMEM((pl.cdiv(width, LANES), 16 * GROUP, LANES), f32)
     d_bias = (HEADS * COUNT, COUNT)
     upper_a, bottom_a, *prior = call(
         first_kernel,
@@ -565,7 +565,7 @@
         "second",
         [place],
         [tokens, cotangent, lat_halo, corner, lon_halo, *params, add, *prior],
-        [tiles, tiles, pltpu.VMEM(d_bias, f32), pltpu.VMEM((CORES, half, 8, across), f32)],
+        [tiles, tiles, pltpu.VMEM((HEADS * COUNT + 8, COUNT), f32), pltpu.VMEM((CORES, half, 8, across), f32)],
     )
 
     pieces = struct((half, 8, across), bf16)
@@ -627,7 +627,7 @@
         "unpack",
         [place],
         [mine, other],
-        [pltpu.VMEM((CORES, half, 8, across), f32), pltpu.VMEM((SPREAD // LANES, HEADS * GROUP, LANES), f32)],
+        [pltpu.VMEM((CORES, half, 8, across), f32), pltpu.VMEM((SPREAD // LANES, 8 * GROUP, LANES), f32)],
     )
     return (
         block_out,

time: 91 us -> 91 us (level)
  no operation moved by 1% of the time
where the time goes in v8:
time: 91 us; the launch traced here: 90.3 us
  starting transfers between devices  53.1 us (58%)
  waiting for transfers between devices  22.8 us (25%)
  Pallas kernels  11.7 us (13%)
  local copies, waits for them, and re-layouts  1.67 us (2%)
  between operations  0.94 us (1%)
    ppermute x4, starting transfers between devices, to_neighbour(): lax.ppermute(value, axes[0], [(i, (i + steps[0]) % n) for i in range(n)])  25.2 us
    ppermute x2, starting transfers between devices, swap_cores(): return lax.ppermute(value, 'lon', [(i, i ^ 1) for i in range(count)])  11.9 us
    pallas_call x9, Pallas kernels, call(): pl.pallas_call(kernel, out_shape=out_shape, in_specs=[smem] * len(scalars...  11.7 us
    all_to_all x1, waiting for transfers between devices, local(): mine = lax.all_to_all(mine, 'lon', 0, 0, axis_index_groups=same_core())  8.17 us
    all_to_all x1, waiting for transfers between devices, local(): by_lat = lax.all_to_all(pair, 'lat', 0, 0)  6.45 us
    all_to_all x1, starting transfers between devices, local(): pair = lax.all_to_all(pair, 'lon', 0, 0, axis_index_groups=same_core())  5.57 us
    all_to_all x1, waiting for transfers between devices, local(): pair = lax.all_to_all(pair, 'lon', 0, 0, axis_index_groups=same_core())  4.6 us
    all_to_all x1, starting transfers between devices, local(): mine = lax.all_to_all(mine, 'lon', 0, 0, axis_index_groups=same_core())  3.55 us
  transfers between devices with their start and end apart: 10, of which 6 were waited for; matrix products, arithmetic and copies ran while one was open for 0% of the time, Pallas kernels for 6%

profile of v8, /device:TPU:1, one launch (start us, length us, event | category | flops | bytes accessed | tf_op | source)
XLA Modules:
  0.0 90.3 jit_solution(8437064289998519608)
XLA Ops:
  0.7 0.9 %slice.30.tokens_ref = bf16[2,3,24,192]{3,2,1,0:T(8,128)(2,1)S(1)} slice(bf16[2,6,24,192]{3,2,1,0:T(8,128)(2,1)} %own.3), slice={[0:2], [0:3], [0:24], [0:192]} | slice | bytes 110592 | tf_op jit(solution)/shard_map/slice | solution.py:518
  1.6 0.1 cut.1
  1.7 13.8 %collective-permute-start = (bf16[2,3,3,18,128]{4,3,2,1,0:T(8,128)(2,1)S(1)}, bf16[2,3,3,18,128]{4,3,2,1,0:T(8,128)(2,1)S(1)}, u32[]{:S(2)}, u32[]{:S(2)}) collective-permute-start(bf16[2,3,3,18,128]{4,3,2,1,0:T(8,128)(2,1)S(1)} %get-tuple-element.51), channel_id=1, source_target_pairs={{0,480},{32,0},{64,32},{96,64},{128,96},{160,128},{192,160},{224,1... | collective-permute-start | bytes 248840 | tf_op jit(solution)/shard_map/ppermute | solution.py:487
  15.6 0.1 maximum_bitcast_fusion
  15.8 0.1 pad_add_fusion.place_ref.refs_0_
  15.9 0.4 copy-done.7
  16.3 0.2 copy-done.5
  16.4 0.1 copy-done.6
  16.5 1.3 %bias.1 = (f32[872,144]{1,0:T(8,128)S(1)}, f32[1,192]{1,0:T(1,128)S(1)}, f32[1,192]{1,0:T(1,128)S(1)}, bf16[192,576]{1,0:T(8,128)(2,1)S(1)}, f32[1,576]{1,0:T(1,...) custom-call(s32[2]{0:T(128)S(1)} %pad_add_fusion.place_ref.refs_0_, s32[96]{0:T(128)S(1)} %copy-done.9, ...), custom_call_target="tpu_custom_call" | custom-call | tf_op jit(solution)/shard_map/bias/pallas_call | solution.py:454
  17.9 3.3 %collective-permute-start.1 = (bf16[2,3,3,6,128]{4,3,2,1,0:T(8,128)(2,1)S(1)}, bf16[2,3,3,6,128]{4,3,2,1,0:T(8,128)(2,1)S(1)}, u32[]{:S(2)}, u32[]{:S(2)}) collective-permute-start(bf16[2,3,3,6,128]{4,3,2,1,0:T(8,128)(2,1)S(1)} %get-tuple-element.54), channel_id=1, source_target_pairs={{0,511},{1,480},{2,481},{3,482},{4,483},{5,484},{6,485},{7,486},{8... | collective-permute-start | bytes 82952 | tf_op jit(solution)/shard_map/ppermute | solution.py:494
  21.2 4.4 %collective-permute-start.2 = (bf16[2,3,3,6,128]{4,3,2,1,0:T(8,128)(2,1)S(1)}, bf16[2,3,3,6,128]{4,3,2,1,0:T(8,128)(2,1)S(1)}, u32[]{:S(2)}, u32[]{:S(2)}) collective-permute-start(bf16[2,3,3,6,128]{4,3,2,1,0:T(8,128)(2,1)S(1)} %pad_maximum_fusion.1), channel_id=1, source_target_pairs={{0,31},{1,0},{2,1},{3,2},{4,3},{5,4},{6,5},{7,6},{8,7},{9,8},{10,9... | collective-permute-start | bytes 82952 | tf_op jit(solution)/shard_map/ppermute | solution.py:487
  25.6 2.4 %first.1 = (f32[2,2,3,12,192]{4,3,2,1,0:T(8,128)S(1)}, bf16[2,3,3,12,128]{4,3,2,1,0:T(8,128)(2,1)S(1)}, f32[864,144]{1,0:T(8,128)S(1)}, f32[192,768]{1,0:T(8,128)S(1)}, f32[1,1152]{1,0:T(1,128)S(1)}) custom-call(bf16[2,6,24,192]{3,2,1,0:T(8,128)(2,1)S(1)} %copy-done, bf16[2,6,24,192]{3,2,1,0:T(8,128)(2,1)S(1)} %copy-done.1, ...), custom_call_target="tpu_custom_call" | custom-call | tf_op jit(solution)/shard_map/first/pallas_call | solution.py:454
  28.0 3.1 %second.1 = (f32[2,2,3,12,192]{4,3,2,1,0:T(8,128)S(1)}, bf16[2,3,3,12,128]{4,3,2,1,0:T(8,128)(2,1)S(1)}, bf16[2,6,3,6,128]{4,3,2,1,0:T(8,128)(2,1)S(1)}, f32[16,...) custom-call(s32[2]{0:T(128)S(1)} %pad_add_fusion.place_ref.refs_0_, bf16[2,6,24,192]{3,2,1,0:T(8,128)(2,1)S(1)} %copy-done, ...), custom_call_target="tpu_custom_call" | custom-call | tf_op jit(solution)/shard_map/second/pallas_call | solution.py:454
  31.1 3.9 %collective-permute-start.3 = (bf16[16,8,768]{2,1,0:T(8,128)(2,1)S(1)}, bf16[16,8,768]{2,1,0:T(8,128)(2,1)S(1)}, u32[]{:S(2)}, u32[]{:S(2)}) collective-permute-start(bf16[16,8,768]{2,1,0:T(8,128)(2,1)S(1)} %get-tuple-element.67), channel_id=1, source_target_pairs={{0,1},{1,0},{2,3},{3,2},{4,5},{5,4},{6,7},{7,6},{8,9},{9,8},{10,11... | collective-permute-start | bytes 589832 | tf_op jit(solution)/shard_map/ppermute | solution.py:475
  35.0 1.0 %collective-permute-done.3.other_ref = bf16[16,8,768]{2,1,0:T(8,128)(2,1)S(1)} collective-permute-done((bf16[16,8,768]{2,1,0:T(8,128)(2,1)S(1)}, bf16[16,8,768]{2,1,0:T(8,128)(2,1)S(1)}, u32[]{:S(2)}, u32[]{:S(2)}) %collective-permute-start.3) | collective-permute-done | bytes 196640 | tf_op jit(solution)/shard_map/ppermute | solution.py:475
  36.1 0.7 pair.1
  36.8 5.6 %all-to-all-start = ((bf16[16,8,768]{2,1,0:T(8,128)(2,1)}), bf16[16,8,768]{2,1,0:T(8,128)(2,1)S(1)}, u32[]{:S(2)}, u32[]{:S(2)}) async-start(bf16[16,8,768]{2,1,0:T(8,128)(2,1)} %pair.1), calls=%async_computation | async-start | bytes 393216 | tf_op jit(solution)/shard_map/all_to_all | solution.py:574
  42.4 3.9 %collective-permute-start.4 = (bf16[2,6,3,6,128]{4,3,2,1,0:T(8,128)(2,1)S(1)}, bf16[2,6,3,6,128]{4,3,2,1,0:T(8,128)(2,1)S(1)}, u32[]{:S(2)}, u32[]{:S(2)}) collective-permute-start(bf16[2,6,3,6,128]{4,3,2,1,0:T(8,128)(2,1)S(1)} %get-tuple-element.68), channel_id=1, source_target_pairs={{0,1},{1,2},{2,3},{3,4},{4,5},{5,6},{6,7},{7,8},{8,9},{9,10},{10,1... | collective-permute-start | bytes 165896 | tf_op jit(solution)/shard_map/ppermute | solution.py:487
  46.2 1.5 %collective-permute-done.4.left_ref = bf16[2,6,3,6,128]{4,3,2,1,0:T(8,128)(2,1)S(1)} collective-permute-done((bf16[2,6,3,6,128]{4,3,2,1,0:T(8,128)(2,1)S(1)}, bf16[2,6,3,6,128]{4,3,2,1,0:T(8,128)(2,1)S(1)}, u32[]{:S(2)}, u32[]{:S(2)}) %collective-permute-start.4) | collective-permute-done | bytes 55328 | tf_op jit(solution)/shard_map/ppermute | solution.py:487
  47.7 4.6 %all-to-all-done.pieces_ref = bf16[16,8,768]{2,1,0:T(8,128)(2,1)S(1)} async-done(((bf16[16,8,768]{2,1,0:T(8,128)(2,1)}), bf16[16,8,768]{2,1,0:T(8,128)(2,1)S(1)}, u32[]{:S(2)}, u32[]{:S(2)}) %all-to-all-start) | async-done | bytes 196640 | tf_op jit(solution)/shard_map/all_to_all | solution.py:574
  52.3 0.7 lon.1
  53.0 3.5 %all-to-all-start.1 = ((bf16[16,8,768]{2,1,0:T(8,128)(2,1)}), bf16[16,8,768]{2,1,0:T(8,128)(2,1)S(1)}, u32[]{:S(2)}, u32[]{:S(2)}) async-start(bf16[16,8,768]{2,1,0:T(8,128)(2,1)} %get-tuple-element.70), calls=%async_computation.1 | async-start | bytes 393216 | tf_op jit(solution)/shard_map/all_to_all | solution.py:584
  56.6 0.1 pad_maximum_fusion
  56.6 3.1 %collective-permute-start.5 = (bf16[2,3,3,24,128]{4,3,2,1,0:T(8,128)(2,1)S(1)}, bf16[2,3,3,24,128]{4,3,2,1,0:T(8,128)(2,1)S(1)}, u32[]{:S(2)}, u32[]{:S(2)}) collective-permute-start(bf16[2,3,3,24,128]{4,3,2,1,0:T(8,128)(2,1)S(1)} %pad_maximum_fusion), channel_id=1, source_target_pairs={{0,32},{32,64},{64,96},{96,128},{128,160},{160,192},{192,224},{224... | collective-permute-start | bytes 331784 | tf_op jit(solution)/shard_map/ppermute | solution.py:487
  59.8 6.4 %all-to-all-done.1.refs_0_ = bf16[16,8,768]{2,1,0:T(8,128)(2,1)S(1)} async-done(((bf16[16,8,768]{2,1,0:T(8,128)(2,1)}), bf16[16,8,768]{2,1,0:T(8,128)(2,1)S(1)}, u32[]{:S(2)}, u32[]{:S(2)}) %all-to-all-start.1) | async-done | bytes 196640 | tf_op jit(solution)/shard_map/all_to_all | solution.py:584
  66.2 0.7 lat.1
  66.9 3.5 %all-to-all-start.2 = ((bf16[16,8,768]{2,1,0:T(8,128)(2,1)}), bf16[16,8,768]{2,1,0:T(8,128)(2,1)S(1)}, u32[]{:S(2)}, u32[]{:S(2)}) async-start(bf16[16,8,768]{2,1,0:T(8,128)(2,1)} %lat.1), calls=%async_computation.2 | async-start | bytes 393216 | tf_op jit(solution)/shard_map/all_to_all | solution.py:599
  70.5 0.9 owned.1
  71.4 8.2 %all-to-all-done.2.refs_1_ = bf16[16,8,768]{2,1,0:T(8,128)(2,1)S(1)} async-done(((bf16[16,8,768]{2,1,0:T(8,128)(2,1)}), bf16[16,8,768]{2,1,0:T(8,128)(2,1)S(1)}, u32[]{:S(2)}, u32[]{:S(2)}) %all-to-all-start.2) | async-done | bytes 196640 | tf_op jit(solution)/shard_map/all_to_all | solution.py:599
  79.5 8.0 %collective-permute-start.6 = (bf16[16,8,768]{2,1,0:T(8,128)(2,1)S(1)}, bf16[16,8,768]{2,1,0:T(8,128)(2,1)S(1)}, u32[]{:S(2)}, u32[]{:S(2)}) collective-permute-start(bf16[16,8,768]{2,1,0:T(8,128)(2,1)S(1)} %all-to-all-done.2.refs_1_), channel_id=1, source_target_pairs={{0,1},{1,0},{2,3},{3,2},{4,5},{5,4},{6,7},{7,6},{8,9},{9,8},{10,11... | collective-permute-start | bytes 589832 | tf_op jit(solution)/shard_map/ppermute | solution.py:475
  87.5 1.0 %collective-permute-done.6.refs_2_ = bf16[16,8,768]{2,1,0:T(8,128)(2,1)S(1)} collective-permute-done((bf16[16,8,768]{2,1,0:T(8,128)(2,1)S(1)}, bf16[16,8,768]{2,1,0:T(8,128)(2,1)S(1)}, u32[]{:S(2)}, u32[]{:S(2)}) %collective-permute-start.6) | collective-permute-done | bytes 196640 | tf_op jit(solution)/shard_map/ppermute | solution.py:475
  88.6 1.8 %unpack.1 = (f32[192,576]{1,0:T(8,128)}, f32[192,192]{1,0:T(8,128)}, f32[1,6,1,3312]{3,2,1,0:T(1,128)}, f32[1,192]{1,0:T(1,128)}, f32[1,192]{1,0:T(1,128)}, /*index=5*/f32[576]{0:T(1024)}, f32[1,192]{1,0:T(1,128)}) custom-call(s32[2]{0:T(128)S(1)} %pad_add_fusion.place_ref.refs_0_, bf16[16,8,768]{2,1,0:T(8,128)(2,1)S(1)} %all-to-all-done.2.refs_1_, ...), custom_call_target="tpu_custom_call" | custom-call | tf_op jit(solution)/shard_map/unpack/pallas_call | solution.py:454
  (28 shorter events, 0.1 us)
Async XLA Ops:
  0.6 0.9 %copy-start.1 = (bf16[2,6,24,192]{3,2,1,0:T(8,128)(2,1)S(1)}, bf16[2,6,24,192]{3,2,1,0:T(8,128)(2,1)}, u32[]{:S(2)}) copy-start(bf16[2,6,24,192]{3,2,1,0:T(8,128)(2,1)} %cot.3) | copy-start | bytes 331780
  1.6 14.0 %copy-start = (bf16[2,6,24,192]{3,2,1,0:T(8,128)(2,1)S(1)}, bf16[2,6,24,192]{3,2,1,0:T(8,128)(2,1)}, u32[]{:S(2)}) copy-start(bf16[2,6,24,192]{3,2,1,0:T(8,128)(2,1)} %own.3) | copy-start | bytes 331780
  1.6 14.2 %copy-start.3 = (bf16[192,192]{1,0:T(8,128)(2,1)S(1)}, bf16[192,192]{1,0:T(8,128)(2,1)}, u32[]{:S(2)}) copy-start(bf16[192,192]{1,0:T(8,128)(2,1)} %rest_4_.1) | copy-start | bytes 221188
  1.6 14.2 %copy-start.4 = (f32[1,1,6,3312]{3,1,2,0:T(1,128)S(1)}, f32[1,1,6,3312]{3,1,2,0:T(1,128)}, u32[]{:S(2)}) copy-start(f32[1,1,6,3312]{3,1,2,0:T(1,128)} %param.18) | copy-start | bytes 238468
  1.7 14.1 %copy-start.2 = (bf16[192,576]{1,0:T(8,128)(2,1)S(1)}, bf16[192,576]{1,0:T(8,128)(2,1)}, u32[]{:S(2)}) copy-start(bf16[192,576]{1,0:T(8,128)(2,1)} %rest_2_.1) | copy-start | bytes 663556
  1.7 23.8 %collective-permute-start = (bf16[2,3,3,18,128]{4,3,2,1,0:T(8,128)(2,1)S(1)}, bf16[2,3,3,18,128]{4,3,2,1,0:T(8,128)(2,1)S(1)}, u32[]{:S(2)}, u32[]{:S(2)}) collective-permute-start(bf16[2,3,3,18,128]{4,3,2,1,0:T(8,128)(2,1)S(1)} %get-tuple-element.51), channel_id=1, source_target_pairs={{0,480},{32,0},{64,32},{96,64},{128,96},{160,128},{192,160},{224,1... | collective-permute-start | bytes 248840 | tf_op jit(solution)/shard_map/ppermute | solution.py:487
  15.6 0.7 copy-start.7
  15.6 0.7 copy-start.8
  15.7 0.7 copy-start.5
  15.8 0.7 copy-start.6
  15.8 0.7 copy-start.9
  17.9 10.1 %collective-permute-start.1 = (bf16[2,3,3,6,128]{4,3,2,1,0:T(8,128)(2,1)S(1)}, bf16[2,3,3,6,128]{4,3,2,1,0:T(8,128)(2,1)S(1)}, u32[]{:S(2)}, u32[]{:S(2)}) collective-permute-start(bf16[2,3,3,6,128]{4,3,2,1,0:T(8,128)(2,1)S(1)} %get-tuple-element.54), channel_id=1, source_target_pairs={{0,511},{1,480},{2,481},{3,482},{4,483},{5,484},{6,485},{7,486},{8... | collective-permute-start | bytes 82952 | tf_op jit(solution)/shard_map/ppermute | solution.py:494
  21.2 6.8 %collective-permute-start.2 = (bf16[2,3,3,6,128]{4,3,2,1,0:T(8,128)(2,1)S(1)}, bf16[2,3,3,6,128]{4,3,2,1,0:T(8,128)(2,1)S(1)}, u32[]{:S(2)}, u32[]{:S(2)}) collective-permute-start(bf16[2,3,3,6,128]{4,3,2,1,0:T(8,128)(2,1)S(1)} %pad_maximum_fusion.1), channel_id=1, source_target_pairs={{0,31},{1,0},{2,1},{3,2},{4,3},{5,4},{6,5},{7,6},{8,7},{9,8},{10,9... | collective-permute-start | bytes 82952 | tf_op jit(solution)/shard_map/ppermute | solution.py:487
  31.1 5.0 %collective-permute-start.3 = (bf16[16,8,768]{2,1,0:T(8,128)(2,1)S(1)}, bf16[16,8,768]{2,1,0:T(8,128)(2,1)S(1)}, u32[]{:S(2)}, u32[]{:S(2)}) collective-permute-start(bf16[16,8,768]{2,1,0:T(8,128)(2,1)S(1)} %get-tuple-element.67), channel_id=1, source_target_pairs={{0,1},{1,0},{2,3},{3,2},{4,5},{5,4},{6,7},{7,6},{8,9},{9,8},{10,11... | collective-permute-start | bytes 589832 | tf_op jit(solution)/shard_map/ppermute | solution.py:475
  36.8 15.5 %all-to-all-start = ((bf16[16,8,768]{2,1,0:T(8,128)(2,1)}), bf16[16,8,768]{2,1,0:T(8,128)(2,1)S(1)}, u32[]{:S(2)}, u32[]{:S(2)}) async-start(bf16[16,8,768]{2,1,0:T(8,128)(2,1)} %pair.1), calls=%async_computation | async-start | bytes 393216 | tf_op jit(solution)/shard_map/all_to_all | solution.py:574
  42.4 5.3 %collective-permute-start.4 = (bf16[2,6,3,6,128]{4,3,2,1,0:T(8,128)(2,1)S(1)}, bf16[2,6,3,6,128]{4,3,2,1,0:T(8,128)(2,1)S(1)}, u32[]{:S(2)}, u32[]{:S(2)}) collective-permute-start(bf16[2,6,3,6,128]{4,3,2,1,0:T(8,128)(2,1)S(1)} %get-tuple-element.68), channel_id=1, source_target_pairs={{0,1},{1,2},{2,3},{3,4},{4,5},{5,6},{6,7},{7,8},{8,9},{9,10},{10,1... | collective-permute-start | bytes 165896 | tf_op jit(solution)/shard_map/ppermute | solution.py:487
  53.0 13.2 %all-to-all-start.1 = ((bf16[16,8,768]{2,1,0:T(8,128)(2,1)}), bf16[16,8,768]{2,1,0:T(8,128)(2,1)S(1)}, u32[]{:S(2)}, u32[]{:S(2)}) async-start(bf16[16,8,768]{2,1,0:T(8,128)(2,1)} %get-tuple-element.70), calls=%async_computation.1 | async-start | bytes 393216 | tf_op jit(solution)/shard_map/all_to_all | solution.py:584
  56.6 13.9 %collective-permute-start.5 = (bf16[2,3,3,24,128]{4,3,2,1,0:T(8,128)(2,1)S(1)}, bf16[2,3,3,24,128]{4,3,2,1,0:T(8,128)(2,1)S(1)}, u32[]{:S(2)}, u32[]{:S(2)}) collective-permute-start(bf16[2,3,3,24,128]{4,3,2,1,0:T(8,128)(2,1)S(1)} %pad_maximum_fusion), channel_id=1, source_target_pairs={{0,32},{32,64},{64,96},{96,128},{128,160},{160,192},{192,224},{224... | collective-permute-start | bytes 331784 | tf_op jit(solution)/shard_map/ppermute | solution.py:487
  66.9 12.6 %all-to-all-start.2 = ((bf16[16,8,768]{2,1,0:T(8,128)(2,1)}), bf16[16,8,768]{2,1,0:T(8,128)(2,1)S(1)}, u32[]{:S(2)}, u32[]{:S(2)}) async-start(bf16[16,8,768]{2,1,0:T(8,128)(2,1)} %lat.1), calls=%async_computation.2 | async-start | bytes 393216 | tf_op jit(solution)/shard_map/all_to_all | solution.py:599
  79.5 9.1 %collective-permute-start.6 = (bf16[16,8,768]{2,1,0:T(8,128)(2,1)S(1)}, bf16[16,8,768]{2,1,0:T(8,128)(2,1)S(1)}, u32[]{:S(2)}, u32[]{:S(2)}) collective-permute-start(bf16[16,8,768]{2,1,0:T(8,128)(2,1)S(1)} %all-to-all-done.2.refs_1_), channel_id=1, source_target_pairs={{0,1},{1,0},{2,3},{3,2},{4,5},{5,4},{6,7},{7,6},{8,9},{9,8},{10,11... | collective-permute-start | bytes 589832 | tf_op jit(solution)/shard_map/ppermute | solution.py:475

commit v9 on v8

--- a/solution.py
+++ b/solution.py
@@ -228,17 +228,27 @@
 
 
 def lon_kernel(pieces_ref, piece_ref, out_ref):
-    piece = sum_pieces(pieces_ref).astype(bf16)
-    piece_ref[...] = piece
-    spread(piece, out_ref)
+    total = sum_pieces(pieces_ref)
+    piece_ref[...] = total.astype(bf16)
+    keep = out_ref.shape[2]
+    ends = [total[r : r + 1, keep:] for r in range(7)] + [jnp.zeros((1, LANES), f32)] * 3
+    last = [jnp.concatenate(ends[k : k + 5], axis=1) for k in (0, 5)]
+    spread(jnp.concatenate([total[:6, :keep], *last], axis=0).astype(bf16), out_ref)
 
 
 def lat_kernel(rows, pieces_ref, by_lon_ref, out_ref):
+    total = sum_pieces(pieces_ref)
+    keep = total.shape[1]
+    ends = [
+        total[6 + k // 5 : 7 + k // 5, k % 5 * LANES : (k % 5 + 1) * LANES] for k in range(8)
+    ]
+    start = jnp.concatenate([total[:6], jnp.zeros((2, keep), f32)], axis=0)
+    total = jnp.concatenate([start, jnp.concatenate(ends, axis=0)], axis=1)
     shape = by_lon_ref.shape
     row = lax.broadcasted_iota(jnp.int32, shape, 0)
     column = lax.broadcasted_iota(jnp.int32, shape, 1)
-    is_table = (row >= rows) & (column < 5 * LANES)
-    total = jnp.where(is_table, by_lon_ref[...].astype(f32), sum_pieces(pieces_ref))
+    is_table = (row >= rows) & (column < keep)
+    total = jnp.where(is_table, by_lon_ref[...].astype(f32), total)
     spread(total.astype(bf16), out_ref)
 
 
@@ -576,7 +586,7 @@
     pair, left = lax.optimization_barrier((pair, left))
     by_lon, pair = call(
         lon_kernel,
-        (piece, struct((lat_count, 8, across), bf16)),
+        (piece, struct((lat_count, 8, across - LANES), bf16)),
         "lon",
         [],
         [pair],

time: 91 us -> 91 us (level)
  no operation moved by 1% of the time
where the time goes in v9:
time: 91 us; the launch traced here: 90.4 us
  starting transfers between devices  53.3 us (59%)
  waiting for transfers between devices  22.6 us (25%)
  Pallas kernels  11.7 us (13%)
  local copies, waits for them, and re-layouts  1.67 us (2%)
  between operations  0.94 us (1%)
    ppermute x4, starting transfers between devices, to_neighbour(): lax.ppermute(value, axes[0], [(i, (i + steps[0]) % n) for i in range(n)])  25.2 us
    ppermute x2, starting transfers between devices, swap_cores(): return lax.ppermute(value, 'lon', [(i, i ^ 1) for i in range(count)])  12.2 us
    pallas_call x9, Pallas kernels, call(): pl.pallas_call(kernel, out_shape=out_shape, in_specs=[smem] * len(scalars...  11.7 us
    all_to_all x1, waiting for transfers between devices, local(): mine = lax.all_to_all(mine, 'lon', 0, 0, axis_index_groups=same_core())  8.12 us
    all_to_all x1, waiting for transfers between devices, local(): by_lat = lax.all_to_all(pair, 'lat', 0, 0)  6.33 us
    all_to_all x1, starting transfers between devices, local(): pair = lax.all_to_all(pair, 'lon', 0, 0, axis_index_groups=same_core())  5.57 us
    all_to_all x1, waiting for transfers between devices, local(): pair = lax.all_to_all(pair, 'lon', 0, 0, axis_index_groups=same_core())  4.6 us
    all_to_all x1, starting transfers between devices, local(): mine = lax.all_to_all(mine, 'lon', 0, 0, axis_index_groups=same_core())  3.52 us
  transfers between devices with their start and end apart: 10, of which 6 were waited for; matrix products, arithmetic and copies ran while one was open for 0% of the time, Pallas kernels for 6%

profile of v9, /device:TPU:1, one launch (start us, length us, event | category | flops | bytes accessed | tf_op | source)
XLA Modules:
  0.0 90.4 jit_solution(7828989500075438068)
XLA Ops:
  0.7 0.9 %slice.30.tokens_ref = bf16[2,3,24,192]{3,2,1,0:T(8,128)(2,1)S(1)} slice(bf16[2,6,24,192]{3,2,1,0:T(8,128)(2,1)} %own.3), slice={[0:2], [0:3], [0:24], [0:192]} | slice | bytes 110592 | tf_op jit(solution)/shard_map/slice | solution.py:528
  1.6 0.1 cut.1
  1.7 13.8 %collective-permute-start = (bf16[2,3,3,18,128]{4,3,2,1,0:T(8,128)(2,1)S(1)}, bf16[2,3,3,18,128]{4,3,2,1,0:T(8,128)(2,1)S(1)}, u32[]{:S(2)}, u32[]{:S(2)}) collective-permute-start(bf16[2,3,3,18,128]{4,3,2,1,0:T(8,128)(2,1)S(1)} %get-tuple-element.51), channel_id=1, source_target_pairs={{0,480},{32,0},{64,32},{96,64},{128,96},{160,128},{192,160},{224,1... | collective-permute-start | bytes 248840 | tf_op jit(solution)/shard_map/ppermute | solution.py:497
  15.6 0.1 maximum_bitcast_fusion
  15.8 0.1 pad_add_fusion.place_ref.refs_0_
  15.9 0.4 copy-done.7
  16.3 0.2 copy-done.5
  16.4 0.1 copy-done.6
  16.5 1.3 %bias.1 = (f32[872,144]{1,0:T(8,128)S(1)}, f32[1,192]{1,0:T(1,128)S(1)}, f32[1,192]{1,0:T(1,128)S(1)}, bf16[192,576]{1,0:T(8,128)(2,1)S(1)}, f32[1,576]{1,0:T(1,...) custom-call(s32[2]{0:T(128)S(1)} %pad_add_fusion.place_ref.refs_0_, s32[96]{0:T(128)S(1)} %copy-done.9, ...), custom_call_target="tpu_custom_call" | custom-call | tf_op jit(solution)/shard_map/bias/pallas_call | solution.py:464
  17.9 3.3 %collective-permute-start.1 = (bf16[2,3,3,6,128]{4,3,2,1,0:T(8,128)(2,1)S(1)}, bf16[2,3,3,6,128]{4,3,2,1,0:T(8,128)(2,1)S(1)}, u32[]{:S(2)}, u32[]{:S(2)}) collective-permute-start(bf16[2,3,3,6,128]{4,3,2,1,0:T(8,128)(2,1)S(1)} %get-tuple-element.54), channel_id=1, source_target_pairs={{0,511},{1,480},{2,481},{3,482},{4,483},{5,484},{6,485},{7,486},{8... | collective-permute-start | bytes 82952 | tf_op jit(solution)/shard_map/ppermute | solution.py:504
  21.2 4.4 %collective-permute-start.2 = (bf16[2,3,3,6,128]{4,3,2,1,0:T(8,128)(2,1)S(1)}, bf16[2,3,3,6,128]{4,3,2,1,0:T(8,128)(2,1)S(1)}, u32[]{:S(2)}, u32[]{:S(2)}) collective-permute-start(bf16[2,3,3,6,128]{4,3,2,1,0:T(8,128)(2,1)S(1)} %pad_maximum_fusion.1), channel_id=1, source_target_pairs={{0,31},{1,0},{2,1},{3,2},{4,3},{5,4},{6,5},{7,6},{8,7},{9,8},{10,9... | collective-permute-start | bytes 82952 | tf_op jit(solution)/shard_map/ppermute | solution.py:497
  25.6 2.4 %first.1 = (f32[2,2,3,12,192]{4,3,2,1,0:T(8,128)S(1)}, bf16[2,3,3,12,128]{4,3,2,1,0:T(8,128)(2,1)S(1)}, f32[864,144]{1,0:T(8,128)S(1)}, f32[192,768]{1,0:T(8,128)S(1)}, f32[1,1152]{1,0:T(1,128)S(1)}) custom-call(bf16[2,6,24,192]{3,2,1,0:T(8,128)(2,1)S(1)} %copy-done, bf16[2,6,24,192]{3,2,1,0:T(8,128)(2,1)S(1)} %copy-done.1, ...), custom_call_target="tpu_custom_call" | custom-call | tf_op jit(solution)/shard_map/first/pallas_call | solution.py:464
  28.0 3.1 %second.1 = (f32[2,2,3,12,192]{4,3,2,1,0:T(8,128)S(1)}, bf16[2,3,3,12,128]{4,3,2,1,0:T(8,128)(2,1)S(1)}, bf16[2,6,3,6,128]{4,3,2,1,0:T(8,128)(2,1)S(1)}, f32[16,...) custom-call(s32[2]{0:T(128)S(1)} %pad_add_fusion.place_ref.refs_0_, bf16[2,6,24,192]{3,2,1,0:T(8,128)(2,1)S(1)} %copy-done, ...), custom_call_target="tpu_custom_call" | custom-call | tf_op jit(solution)/shard_map/second/pallas_call | solution.py:464
  31.1 3.9 %collective-permute-start.3 = (bf16[16,8,768]{2,1,0:T(8,128)(2,1)S(1)}, bf16[16,8,768]{2,1,0:T(8,128)(2,1)S(1)}, u32[]{:S(2)}, u32[]{:S(2)}) collective-permute-start(bf16[16,8,768]{2,1,0:T(8,128)(2,1)S(1)} %get-tuple-element.67), channel_id=1, source_target_pairs={{0,1},{1,0},{2,3},{3,2},{4,5},{5,4},{6,7},{7,6},{8,9},{9,8},{10,11... | collective-permute-start | bytes 589832 | tf_op jit(solution)/shard_map/ppermute | solution.py:485
  35.0 1.0 %collective-permute-done.3.other_ref = bf16[16,8,768]{2,1,0:T(8,128)(2,1)S(1)} collective-permute-done((bf16[16,8,768]{2,1,0:T(8,128)(2,1)S(1)}, bf16[16,8,768]{2,1,0:T(8,128)(2,1)S(1)}, u32[]{:S(2)}, u32[]{:S(2)}) %collective-permute-start.3) | collective-permute-done | bytes 196640 | tf_op jit(solution)/shard_map/ppermute | solution.py:485
  36.1 0.7 pair.1
  36.8 5.6 %all-to-all-start = ((bf16[16,8,768]{2,1,0:T(8,128)(2,1)}), bf16[16,8,768]{2,1,0:T(8,128)(2,1)S(1)}, u32[]{:S(2)}, u32[]{:S(2)}) async-start(bf16[16,8,768]{2,1,0:T(8,128)(2,1)} %pair.1), calls=%async_computation | async-start | bytes 393216 | tf_op jit(solution)/shard_map/all_to_all | solution.py:584
  42.4 3.9 %collective-permute-start.4 = (bf16[2,6,3,6,128]{4,3,2,1,0:T(8,128)(2,1)S(1)}, bf16[2,6,3,6,128]{4,3,2,1,0:T(8,128)(2,1)S(1)}, u32[]{:S(2)}, u32[]{:S(2)}) collective-permute-start(bf16[2,6,3,6,128]{4,3,2,1,0:T(8,128)(2,1)S(1)} %get-tuple-element.68), channel_id=1, source_target_pairs={{0,1},{1,2},{2,3},{3,4},{4,5},{5,6},{6,7},{7,8},{8,9},{9,10},{10,1... | collective-permute-start | bytes 165896 | tf_op jit(solution)/shard_map/ppermute | solution.py:497
  46.2 1.5 %collective-permute-done.4.left_ref = bf16[2,6,3,6,128]{4,3,2,1,0:T(8,128)(2,1)S(1)} collective-permute-done((bf16[2,6,3,6,128]{4,3,2,1,0:T(8,128)(2,1)S(1)}, bf16[2,6,3,6,128]{4,3,2,1,0:T(8,128)(2,1)S(1)}, u32[]{:S(2)}, u32[]{:S(2)}) %collective-permute-start.4) | collective-permute-done | bytes 55328 | tf_op jit(solution)/shard_map/ppermute | solution.py:497
  47.7 4.6 %all-to-all-done.pieces_ref = bf16[16,8,768]{2,1,0:T(8,128)(2,1)S(1)} async-done(((bf16[16,8,768]{2,1,0:T(8,128)(2,1)}), bf16[16,8,768]{2,1,0:T(8,128)(2,1)S(1)}, u32[]{:S(2)}, u32[]{:S(2)}) %all-to-all-start) | async-done | bytes 196640 | tf_op jit(solution)/shard_map/all_to_all | solution.py:584
  52.3 0.7 lon.1
  53.0 3.5 %all-to-all-start.1 = ((bf16[16,8,640]{2,1,0:T(8,128)(2,1)}), bf16[16,8,640]{2,1,0:T(8,128)(2,1)S(1)}, u32[]{:S(2)}, u32[]{:S(2)}) async-start(bf16[16,8,640]{2,1,0:T(8,128)(2,1)} %get-tuple-element.70), calls=%async_computation.1 | async-start | bytes 327680 | tf_op jit(solution)/shard_map/all_to_all | solution.py:594
  56.6 0.1 pad_maximum_fusion
  56.6 3.1 %collective-permute-start.5 = (bf16[2,3,3,24,128]{4,3,2,1,0:T(8,128)(2,1)S(1)}, bf16[2,3,3,24,128]{4,3,2,1,0:T(8,128)(2,1)S(1)}, u32[]{:S(2)}, u32[]{:S(2)}) collective-permute-start(bf16[2,3,3,24,128]{4,3,2,1,0:T(8,128)(2,1)S(1)} %pad_maximum_fusion), channel_id=1, source_target_pairs={{0,32},{32,64},{64,96},{96,128},{128,160},{160,192},{192,224},{224... | collective-permute-start | bytes 331784 | tf_op jit(solution)/shard_map/ppermute | solution.py:497
  59.8 6.3 %all-to-all-done.1.refs_0_ = bf16[16,8,640]{2,1,0:T(8,128)(2,1)S(1)} async-done(((bf16[16,8,640]{2,1,0:T(8,128)(2,1)}), bf16[16,8,640]{2,1,0:T(8,128)(2,1)S(1)}, u32[]{:S(2)}, u32[]{:S(2)}) %all-to-all-start.1) | async-done | bytes 163872 | tf_op jit(solution)/shard_map/all_to_all | solution.py:594
  66.1 0.7 lat.1
  66.8 3.5 %all-to-all-start.2 = ((bf16[16,8,768]{2,1,0:T(8,128)(2,1)}), bf16[16,8,768]{2,1,0:T(8,128)(2,1)S(1)}, u32[]{:S(2)}, u32[]{:S(2)}) async-start(bf16[16,8,768]{2,1,0:T(8,128)(2,1)} %lat.1), calls=%async_computation.2 | async-start | bytes 393216 | tf_op jit(solution)/shard_map/all_to_all | solution.py:609
  70.4 0.9 owned.1
  71.2 8.1 %all-to-all-done.2.refs_1_ = bf16[16,8,768]{2,1,0:T(8,128)(2,1)S(1)} async-done(((bf16[16,8,768]{2,1,0:T(8,128)(2,1)}), bf16[16,8,768]{2,1,0:T(8,128)(2,1)S(1)}, u32[]{:S(2)}, u32[]{:S(2)}) %all-to-all-start.2) | async-done | bytes 196640 | tf_op jit(solution)/shard_map/all_to_all | solution.py:609
  79.3 8.2 %collective-permute-start.6 = (bf16[16,8,768]{2,1,0:T(8,128)(2,1)S(1)}, bf16[16,8,768]{2,1,0:T(8,128)(2,1)S(1)}, u32[]{:S(2)}, u32[]{:S(2)}) collective-permute-start(bf16[16,8,768]{2,1,0:T(8,128)(2,1)S(1)} %all-to-all-done.2.refs_1_), channel_id=1, source_target_pairs={{0,1},{1,0},{2,3},{3,2},{4,5},{5,4},{6,7},{7,6},{8,9},{9,8},{10,11... | collective-permute-start | bytes 589832 | tf_op jit(solution)/shard_map/ppermute | solution.py:485
  87.6 1.0 %collective-permute-done.6.refs_2_ = bf16[16,8,768]{2,1,0:T(8,128)(2,1)S(1)} collective-permute-done((bf16[16,8,768]{2,1,0:T(8,128)(2,1)S(1)}, bf16[16,8,768]{2,1,0:T(8,128)(2,1)S(1)}, u32[]{:S(2)}, u32[]{:S(2)}) %collective-permute-start.6) | collective-permute-done | bytes 196640 | tf_op jit(solution)/shard_map/ppermute | solution.py:485
  88.6 1.8 %unpack.1 = (f32[192,576]{1,0:T(8,128)}, f32[192,192]{1,0:T(8,128)}, f32[1,6,1,3312]{3,2,1,0:T(1,128)}, f32[1,192]{1,0:T(1,128)}, f32[1,192]{1,0:T(1,128)}, /*index=5*/f32[576]{0:T(1024)}, f32[1,192]{1,0:T(1,128)}) custom-call(s32[2]{0:T(128)S(1)} %pad_add_fusion.place_ref.refs_0_, bf16[16,8,768]{2,1,0:T(8,128)(2,1)S(1)} %all-to-all-done.2.refs_1_, ...), custom_call_target="tpu_custom_call" | custom-call | tf_op jit(solution)/shard_map/unpack/pallas_call | solution.py:464
  (28 shorter events, 0.1 us)
Async XLA Ops:
  0.6 0.9 %copy-start.1 = (bf16[2,6,24,192]{3,2,1,0:T(8,128)(2,1)S(1)}, bf16[2,6,24,192]{3,2,1,0:T(8,128)(2,1)}, u32[]{:S(2)}) copy-start(bf16[2,6,24,192]{3,2,1,0:T(8,128)(2,1)} %cot.3) | copy-start | bytes 331780
  1.6 14.0 %copy-start = (bf16[2,6,24,192]{3,2,1,0:T(8,128)(2,1)S(1)}, bf16[2,6,24,192]{3,2,1,0:T(8,128)(2,1)}, u32[]{:S(2)}) copy-start(bf16[2,6,24,192]{3,2,1,0:T(8,128)(2,1)} %own.3) | copy-start | bytes 331780
  1.6 14.2 %copy-start.3 = (bf16[192,192]{1,0:T(8,128)(2,1)S(1)}, bf16[192,192]{1,0:T(8,128)(2,1)}, u32[]{:S(2)}) copy-start(bf16[192,192]{1,0:T(8,128)(2,1)} %rest_4_.1) | copy-start | bytes 221188
  1.6 14.2 %copy-start.4 = (f32[1,1,6,3312]{3,1,2,0:T(1,128)S(1)}, f32[1,1,6,3312]{3,1,2,0:T(1,128)}, u32[]{:S(2)}) copy-start(f32[1,1,6,3312]{3,1,2,0:T(1,128)} %param.18) | copy-start | bytes 238468
  1.7 14.1 %copy-start.2 = (bf16[192,576]{1,0:T(8,128)(2,1)S(1)}, bf16[192,576]{1,0:T(8,128)(2,1)}, u32[]{:S(2)}) copy-start(bf16[192,576]{1,0:T(8,128)(2,1)} %rest_2_.1) | copy-start | bytes 663556
  1.7 23.8 %collective-permute-start = (bf16[2,3,3,18,128]{4,3,2,1,0:T(8,128)(2,1)S(1)}, bf16[2,3,3,18,128]{4,3,2,1,0:T(8,128)(2,1)S(1)}, u32[]{:S(2)}, u32[]{:S(2)}) collective-permute-start(bf16[2,3,3,18,128]{4,3,2,1,0:T(8,128)(2,1)S(1)} %get-tuple-element.51), channel_id=1, source_target_pairs={{0,480},{32,0},{64,32},{96,64},{128,96},{160,128},{192,160},{224,1... | collective-permute-start | bytes 248840 | tf_op jit(solution)/shard_map/ppermute | solution.py:497
  15.6 0.7 copy-start.7
  15.6 0.7 copy-start.8
  15.7 0.7 copy-start.5
  15.8 0.7 copy-start.6
  15.8 0.7 copy-start.9
  17.9 10.1 %collective-permute-start.1 = (bf16[2,3,3,6,128]{4,3,2,1,0:T(8,128)(2,1)S(1)}, bf16[2,3,3,6,128]{4,3,2,1,0:T(8,128)(2,1)S(1)}, u32[]{:S(2)}, u32[]{:S(2)}) collective-permute-start(bf16[2,3,3,6,128]{4,3,2,1,0:T(8,128)(2,1)S(1)} %get-tuple-element.54), channel_id=1, source_target_pairs={{0,511},{1,480},{2,481},{3,482},{4,483},{5,484},{6,485},{7,486},{8... | collective-permute-start | bytes 82952 | tf_op jit(solution)/shard_map/ppermute | solution.py:504
  21.2 6.8 %collective-permute-start.2 = (bf16[2,3,3,6,128]{4,3,2,1,0:T(8,128)(2,1)S(1)}, bf16[2,3,3,6,128]{4,3,2,1,0:T(8,128)(2,1)S(1)}, u32[]{:S(2)}, u32[]{:S(2)}) collective-permute-start(bf16[2,3,3,6,128]{4,3,2,1,0:T(8,128)(2,1)S(1)} %pad_maximum_fusion.1), channel_id=1, source_target_pairs={{0,31},{1,0},{2,1},{3,2},{4,3},{5,4},{6,5},{7,6},{8,7},{9,8},{10,9... | collective-permute-start | bytes 82952 | tf_op jit(solution)/shard_map/ppermute | solution.py:497
  31.1 5.0 %collective-permute-start.3 = (bf16[16,8,768]{2,1,0:T(8,128)(2,1)S(1)}, bf16[16,8,768]{2,1,0:T(8,128)(2,1)S(1)}, u32[]{:S(2)}, u32[]{:S(2)}) collective-permute-start(bf16[16,8,768]{2,1,0:T(8,128)(2,1)S(1)} %get-tuple-element.67), channel_id=1, source_target_pairs={{0,1},{1,0},{2,3},{3,2},{4,5},{5,4},{6,7},{7,6},{8,9},{9,8},{10,11... | collective-permute-start | bytes 589832 | tf_op jit(solution)/shard_map/ppermute | solution.py:485
  36.8 15.5 %all-to-all-start = ((bf16[16,8,768]{2,1,0:T(8,128)(2,1)}), bf16[16,8,768]{2,1,0:T(8,128)(2,1)S(1)}, u32[]{:S(2)}, u32[]{:S(2)}) async-start(bf16[16,8,768]{2,1,0:T(8,128)(2,1)} %pair.1), calls=%async_computation | async-start | bytes 393216 | tf_op jit(solution)/shard_map/all_to_all | solution.py:584
  42.4 5.3 %collective-permute-start.4 = (bf16[2,6,3,6,128]{4,3,2,1,0:T(8,128)(2,1)S(1)}, bf16[2,6,3,6,128]{4,3,2,1,0:T(8,128)(2,1)S(1)}, u32[]{:S(2)}, u32[]{:S(2)}) collective-permute-start(bf16[2,6,3,6,128]{4,3,2,1,0:T(8,128)(2,1)S(1)} %get-tuple-element.68), channel_id=1, source_target_pairs={{0,1},{1,2},{2,3},{3,4},{4,5},{5,6},{6,7},{7,8},{8,9},{9,10},{10,1... | collective-permute-start | bytes 165896 | tf_op jit(solution)/shard_map/ppermute | solution.py:497
  53.0 13.1 %all-to-all-start.1 = ((bf16[16,8,640]{2,1,0:T(8,128)(2,1)}), bf16[16,8,640]{2,1,0:T(8,128)(2,1)S(1)}, u32[]{:S(2)}, u32[]{:S(2)}) async-start(bf16[16,8,640]{2,1,0:T(8,128)(2,1)} %get-tuple-element.70), calls=%async_computation.1 | async-start | bytes 327680 | tf_op jit(solution)/shard_map/all_to_all | solution.py:594
  56.6 13.7 %collective-permute-start.5 = (bf16[2,3,3,24,128]{4,3,2,1,0:T(8,128)(2,1)S(1)}, bf16[2,3,3,24,128]{4,3,2,1,0:T(8,128)(2,1)S(1)}, u32[]{:S(2)}, u32[]{:S(2)}) collective-permute-start(bf16[2,3,3,24,128]{4,3,2,1,0:T(8,128)(2,1)S(1)} %pad_maximum_fusion), channel_id=1, source_target_pairs={{0,32},{32,64},{64,96},{96,128},{128,160},{160,192},{192,224},{224... | collective-permute-start | bytes 331784 | tf_op jit(solution)/shard_map/ppermute | solution.py:497
  66.8 12.5 %all-to-all-start.2 = ((bf16[16,8,768]{2,1,0:T(8,128)(2,1)}), bf16[16,8,768]{2,1,0:T(8,128)(2,1)S(1)}, u32[]{:S(2)}, u32[]{:S(2)}) async-start(bf16[16,8,768]{2,1,0:T(8,128)(2,1)} %lat.1), calls=%async_computation.2 | async-start | bytes 393216 | tf_op jit(solution)/shard_map/all_to_all | solution.py:609
  79.3 9.3 %collective-permute-start.6 = (bf16[16,8,768]{2,1,0:T(8,128)(2,1)S(1)}, bf16[16,8,768]{2,1,0:T(8,128)(2,1)S(1)}, u32[]{:S(2)}, u32[]{:S(2)}) collective-permute-start(bf16[16,8,768]{2,1,0:T(8,128)(2,1)S(1)} %all-to-all-done.2.refs_1_), channel_id=1, source_target_pairs={{0,1},{1,0},{2,3},{3,2},{4,5},{5,4},{6,7},{7,6},{8,9},{9,8},{10,11... | collective-permute-start | bytes 589832 | tf_op jit(solution)/shard_map/ppermute | solution.py:485
